TPU v7x, 32 devices: a whole 2x2x4 slice. The times are simulated.
32 devices in a mesh: seed: 8 (over y, x, core), hid: 4 (over z).
Axes of the slice: x: 2, y: 2, z: 4, core: 2. Of those that a mesh axis runs over, the one named last changes fastest.
Arguments:
- features: bfloat16 [262144, 100], P('seed'), may hold values from -6 to 6
- links_first: int32 [65536, 10], P('seed'), may hold values from -1 to 32767, as said below
- links_second: int32 [8192, 10], P('seed'), may hold values from -1 to 8191, as said below
- links_third: int32 [1024, 25], P('seed'), may hold values from -1 to 1023, as said below
- labels: int32 [1024], P('seed'), may hold values from 0 to 46
- valid: int32 [1024], P('seed'), may hold values from 0 to 1, as said below
- weight_first: float32 [200, 256], P(None, 'hid'), may hold values from -1.5 to 1.5
- moment_first: float32 [200, 256], P(None, 'hid')
- square_first: float32 [200, 256], P(None, 'hid'), as said below
- weight_stack: float32 [2, 512, 256], P(None, 'seed', 'hid'), may hold values from -4 to 4
- moment_stack: float32 [2, 512, 256], P(None, 'seed', 'hid')
- square_stack: float32 [2, 512, 256], P(None, 'seed', 'hid'), as said below
- weight_head: float32 [256, 47], P('hid'), may hold values from -6 to 6
- moment_head: float32 [256, 47], P('hid')
- square_head: float32 [256, 47], P('hid'), as said below
Outputs:
- loss_sum: float32 [], replicated
- count: float32 [], replicated
- new_moment_first: float32 [200, 256], P(None, 'hid')
- new_square_first: float32 [200, 256], P(None, 'hid')
- new_weight_first: float32 [200, 256], P(None, 'hid')
- new_moment_stack: float32 [2, 512, 256], P(None, 'seed', 'hid')
- new_square_stack: float32 [2, 512, 256], P(None, 'seed', 'hid')
- new_weight_stack: float32 [2, 512, 256], P(None, 'seed', 'hid')
- new_moment_head: float32 [256, 47], P('hid')
- new_square_head: float32 [256, 47], P('hid')
- new_weight_head: float32 [256, 47], P('hid')
Inputs may be any that keep to these rules, and one draw needn't show every extreme that they name: `links_first`: each row's nonempty slots come first, one or more; row i of a block names only rows 4 i to 4 i + 3 of the next level in the same block (its own sampled rows). `links_second`: each row's nonempty slots come first, one or more; row i of a block names only rows 8 i to 8 i + 7 of the next level in the same block (its own sampled rows). `links_third`: each row's nonempty slots come first, one or more; row i of a block names only rows 8 i to 8 i + 7 of the next level in the same block (its own sampled rows). The first seed is valid. `square_first`: positive. `square_stack`: positive. `square_head`: positive.
All inputs are finite; a program needn't handle non-finite values.
Results may differ from a plain program's by a relative error of at most 0.012.
The roundings to bfloat16 on the way count: a program that leaves them out, or rounds other values in their place, can miss the bound.
Values may be sent and summed in bfloat16 or wider, within the bound.
A program may use at most 128 MiB of HBM per device.

v0:
```python
import jax
import jax.numpy as jnp
from jax import lax
from jax.sharding import PartitionSpec as P

STEP = 5


epsilon_norm = 1e-06
epsilon_adam = 1e-08
learn_rate = 0.6
decay_rate = 0.01
beta_first = 0.5
beta_second = 0.5


def slot_counts(neighbors, ratio):
    present = neighbors >= 0
    offsets = neighbors - ratio * jnp.arange(neighbors.shape[0], dtype=jnp.int32)[:, None]
    hits = (offsets[:, :, None] == jnp.arange(ratio, dtype=jnp.int32)[None, None, :]) & present[
        :, :, None
    ]
    counts = jnp.sum(hits.astype(jnp.float32), axis=1)
    degree = jnp.maximum(jnp.sum(present.astype(jnp.float32), axis=1), 1.0)
    return (counts, degree)


def mean_rows(source_rows, neighbors):
    count_out = neighbors.shape[0]
    ratio = source_rows.shape[0] // count_out
    counts, degree = slot_counts(neighbors, ratio)
    windows = source_rows.reshape(count_out, ratio, source_rows.shape[1])
    totals = jnp.einsum(
        "or,orc->oc", counts.astype(source_rows.dtype), windows, preferred_element_type=jnp.float32
    )
    return totals / degree[:, None]


def mean_rows_back(grad_mean, neighbors, source_count):
    count_out = neighbors.shape[0]
    ratio = source_count // count_out
    counts, degree = slot_counts(neighbors, ratio)
    shares = (grad_mean / degree[:, None])[:, None, :] * counts[:, :, None]
    return shares.reshape(source_count, grad_mean.shape[1])


def normalize(preact):
    active = jax.nn.silu(preact)
    squares = jnp.sum(active * active, axis=1)
    totals = lax.psum(squares, "hid")
    scaling = lax.rsqrt(totals + epsilon_norm)
    return ((active * scaling[:, None]).astype(jnp.bfloat16), active, scaling)


def normalize_back(grad_out, preact, active, scaling):
    inner = jnp.sum(active * grad_out, axis=1)
    totals = lax.psum(inner, "hid")
    grad_active = (
        scaling[:, None] * grad_out - active * (scaling * scaling * scaling * totals)[:, None]
    )
    logistic = jax.nn.sigmoid(preact)
    return grad_active * logistic * (1.0 + preact * (1.0 - logistic))


def combine(source_rows, neighbors):
    count_out = neighbors.shape[0]
    gathered = lax.all_gather(source_rows, "hid", axis=1, tiled=True)
    itself = gathered[:count_out]
    merged = mean_rows(gathered, neighbors).astype(jnp.bfloat16)
    return jnp.concatenate([itself, merged], axis=1)


def spread_back(grad_self, grad_mean, neighbors, source_count):
    count_out = grad_self.shape[0]
    partial_rows = mean_rows_back(grad_mean, neighbors, source_count).at[:count_out].add(grad_self)
    return lax.psum_scatter(partial_rows, "hid", scatter_dimension=1, tiled=True)


def sage_forward(joined, weight_low):
    preact = jnp.dot(joined, weight_low, preferred_element_type=jnp.float32)
    output, active, scaling = normalize(preact)
    return (output, (joined, preact, active, scaling))


def sage_backward(grad_out, record, weight_low, neighbors, source_count):
    joined, preact, active, scaling = record
    grad_pre = normalize_back(grad_out, preact, active, scaling).astype(jnp.bfloat16)
    grad_weight = lax.dot_general(
        joined, grad_pre, (((0,), (0,)), ((), ())), preferred_element_type=jnp.float32
    )
    if neighbors is None:
        return (grad_weight, None)
    grad_joined = lax.dot_general(
        grad_pre, weight_low, (((1,), (1,)), ((), ())), preferred_element_type=jnp.float32
    )
    half_width = grad_joined.shape[1] // 2
    grad_rows = spread_back(
        grad_joined[:, :half_width], grad_joined[:, half_width:], neighbors, source_count
    )
    return (grad_weight, grad_rows)


def adamw(weight, moment, square, grad):
    new_moment = beta_first * moment + (1.0 - beta_first) * grad
    new_square = beta_second * square + (1.0 - beta_second) * grad * grad
    moment_hat = new_moment / (1.0 - beta_first**STEP)
    square_hat = new_square / (1.0 - beta_second**STEP)
    new_weight = weight - learn_rate * (
        moment_hat / (jnp.sqrt(square_hat) + epsilon_adam) + decay_rate * weight
    )
    return (new_moment, new_square, new_weight)


def per_device(
    features,
    links_first,
    links_second,
    links_third,
    labels,
    valid,
    weight_first,
    moment_first,
    square_first,
    weight_stack,
    moment_stack,
    square_stack,
    weight_head,
    moment_head,
    square_head,
):
    present = valid.astype(jnp.float32)
    stack_low = lax.all_gather(weight_stack.astype(jnp.bfloat16), "seed", axis=1, tiled=True)
    first_low = weight_first.astype(jnp.bfloat16)
    head_low = weight_head.astype(jnp.bfloat16)
    rows_two = links_first.shape[0]
    joined = jnp.concatenate(
        [features[:rows_two], mean_rows(features, links_first).astype(jnp.bfloat16)], axis=1
    )
    hidden_rows, record = sage_forward(joined, first_low)
    records = [record]
    for layer_pos, neighbors in ((0, links_second), (1, links_third)):
        joined = combine(hidden_rows, neighbors)
        hidden_rows, record = sage_forward(joined, stack_low[layer_pos])
        records.append(record)
    logits = jnp.dot(hidden_rows, head_low, preferred_element_type=jnp.float32)
    full_logits = lax.psum(logits, "hid")
    peak = jnp.max(full_logits, axis=1, keepdims=True)
    totals = peak[:, 0] + jnp.log(jnp.sum(jnp.exp(full_logits - peak), axis=1))
    onehot = (labels[:, None] == jnp.arange(full_logits.shape[1])[None, :]).astype(jnp.float32)
    target = jnp.sum(full_logits * onehot, axis=1)
    local_loss = jnp.sum((totals - target) * present)
    loss_sum, count = lax.psum((local_loss, jnp.sum(present)), "seed")
    weights_row = present / jnp.maximum(count, 1.0)
    grad_logits = ((jnp.exp(full_logits - totals[:, None]) - onehot) * weights_row[:, None]).astype(
        jnp.bfloat16
    )
    grad_head = lax.dot_general(
        hidden_rows, grad_logits, (((0,), (0,)), ((), ())), preferred_element_type=jnp.float32
    )
    grad_rows = lax.dot_general(
        grad_logits, head_low, (((1,), (1,)), ((), ())), preferred_element_type=jnp.float32
    )
    stack_grads = [None, None]
    for layer_pos, neighbors, source_count in (
        (1, links_third, links_second.shape[0]),
        (0, links_second, rows_two),
    ):
        grad_weight, grad_rows = sage_backward(
            grad_rows, records[layer_pos + 1], stack_low[layer_pos], neighbors, source_count
        )
        stack_grads[layer_pos] = grad_weight
    grad_first, unused_rows = sage_backward(grad_rows, records[0], first_low, None, 0)
    grad_stack = jnp.stack(stack_grads)
    grad_first, grad_head = lax.psum((grad_first, grad_head), "seed")
    grad_stack = lax.psum_scatter(grad_stack, "seed", scatter_dimension=1, tiled=True)
    moment_a, square_a, weight_a = adamw(weight_first, moment_first, square_first, grad_first)
    moment_b, square_b, weight_b = adamw(weight_stack, moment_stack, square_stack, grad_stack)
    moment_c, square_c, weight_c = adamw(weight_head, moment_head, square_head, grad_head)
    return (
        loss_sum,
        count,
        moment_a,
        square_a,
        weight_a,
        moment_b,
        square_b,
        weight_b,
        moment_c,
        square_c,
        weight_c,
    )


def solution(mesh):
    placed = (
        P("seed", None),
        P("seed", None),
        P("seed", None),
        P("seed", None),
        P("seed"),
        P("seed"),
        P(None, "hid"),
        P(None, "hid"),
        P(None, "hid"),
        P(None, "seed", "hid"),
        P(None, "seed", "hid"),
        P(None, "seed", "hid"),
        P("hid", None),
        P("hid", None),
        P("hid", None),
    )
    return jax.shard_map(
        per_device,
        mesh=mesh,
        in_specs=placed,
        out_specs=(
            P(),
            P(),
            P(None, "hid"),
            P(None, "hid"),
            P(None, "hid"),
            P(None, "seed", "hid"),
            P(None, "seed", "hid"),
            P(None, "seed", "hid"),
            P("hid", None),
            P("hid", None),
            P("hid", None),
        ),
        check_vma=False,
    )
```

profile of v0, /device:TPU:0, one launch (start us, length us, event | category | flops | bytes accessed | tf_op | source)
XLA Modules:
  0.0 548.4 jit_solution(13166206626791219309)
XLA Ops:
  7.2 2.8 slice.67
  10.0 10.6 %copy.91 = bf16[32768,100]{1,0:T(8,128)(2,1)} copy(bf16[32768,100]{0,1:T(8,128)(2,1)} %param.19) | data formatting | bytes 13107200 | tf_op args[0]
  20.8 0.7 convert_reduce_fusion
  21.5 2.4 copy.127
  23.9 48.0 %multiply_reduce_fusion = f32[8192,100]{1,0:T(8,128)} fusion(bf16[8192,4,100]{2,1,0:T(4,128)(2,1)} %bitcast.28, f32[8192,4]{1,0:T(8,128)} %copy.127), kind=kLoop, calls=%fused_computation | loop fusion | flops 9011200 | bytes 9961472
  71.9 3.8 copy.114
  75.8 0.3 divide_convert_fusion
  76.1 1.1 copy-done.5
  77.2 1.2 multiply_reduce_fusion.3
  78.5 20.8 %psum.77 = f32[8192]{0:T(1024)S(1)} all-reduce(f32[8192]{0:T(1024)S(1)} %get-tuple-element.102), channel_id=1, replica_groups=mesh['seed'=8,'hid'=4] {'hid'}, use_global_device_ids=true, to_apply=%region_3.4 | all-reduce | flops 8192 | bytes 65536 | tf_op jit(solution)/shard_map/psum | solution.py:50
  99.4 1.5 multiply_convert_fusion.1
  101.3 0.7 copy.129
  102.2 0.2 copy.128
  102.4 9.6 %all_gather.10 = bf16[2,512,64]{2,1,0:T(8,128)(2,1)S(1)} all-gather(bf16[2,64,64]{2,1,0:T(8,128)(2,1)S(1)} %convert_element_type.86), channel_id=1, replica_groups=mesh['seed'=8,'hid'=4] {'seed'}, dimensions={1}, use_global_device_ids=true | all-gather | bytes 147456 | tf_op jit(solution)/shard_map/all_gather | solution.py:132
  111.9 0.5 broadcast_maximum_fusion.2
  112.4 67.6 %all-gather.2.cloned.1.call-done = bf16[8192,256]{0,1:T(8,128)(2,1)} async-done(((bf16[8192,64]{0,1:T(8,128)(2,1)}), bf16[8192,256]{0,1:T(8,128)(2,1)}) %all-gather.2.cloned.1.call-update) | async-done | bytes 4194320 | tf_op jit(solution)/shard_map/all_gather | solution.py:67
  180.1 6.4 %copy.92 = bf16[8192,256]{1,0:T(8,128)(2,1)} copy(bf16[8192,256]{0,1:T(8,128)(2,1)} %all-gather.2.cloned.1.call-done) | data formatting | bytes 8388608 | tf_op jit(solution)/shard_map/all_gather | solution.py:67
  186.4 7.2 %multiply_reduce_fusion.1 = f32[1024,256]{1,0:T(8,128)S(1)} fusion(f32[1024,8]{1,0:T(8,128)S(1)} %copy.128, bf16[8192,256]{1,0:T(8,128)(2,1)} %copy.92), kind=kLoop, calls=%fused_computation.1 | loop fusion | flops 6029312 | bytes 5275648
  193.6 0.3 copy.118
  194.1 1.1 slice.78
  195.1 0.8 copy-done.7
  196.0 0.4 multiply_reduce_fusion.6
  196.4 9.0 %psum.78 = f32[1024]{0:T(1024)S(1)} all-reduce(f32[1024]{0:T(1024)S(1)} %get-tuple-element.104), channel_id=1, replica_groups=mesh['seed'=8,'hid'=4] {'hid'}, use_global_device_ids=true, to_apply=%region_7.8 | all-reduce | flops 1024 | bytes 8192 | tf_op jit(solution)/shard_map/psum | solution.py:50
  205.4 15.4 %all_gather.11 = bf16[1024,256]{0,1:T(8,128)(2,1)S(1)} all-gather(bf16[1024,64]{0,1:T(8,128)(2,1)S(1)} %multiply_convert_fusion.4), channel_id=1, replica_groups=mesh['seed'=8,'hid'=4] {'hid'}, dimensions={1}, use_global_device_ids=true | all-gather | bytes 655360 | tf_op jit(solution)/shard_map/all_gather | solution.py:67
  220.9 0.2 copy.93
  221.1 0.4 multiply_reduce_fusion.4
  221.6 0.2 multiply_reduce_fusion.8
  221.9 10.5 %psum.79 = f32[128]{0:T(128)S(1)} all-reduce(f32[128]{0:T(128)S(1)} %get-tuple-element.106), channel_id=1, replica_groups=mesh['seed'=8,'hid'=4] {'hid'}, use_global_device_ids=true, to_apply=%region_11.12 | all-reduce | flops 128 | bytes 1024 | tf_op jit(solution)/shard_map/psum | solution.py:50
  232.5 15.8 %psum.80 = f32[128,47]{0,1:T(8,128)S(1)} all-reduce(f32[128,47]{0,1:T(8,128)S(1)} %fusion.21), channel_id=1, replica_groups=mesh['seed'=8,'hid'=4] {'hid'}, use_global_device_ids=true, to_apply=%region_12.13 | all-reduce | flops 6016 | bytes 48128 | tf_op jit(solution)/shard_map/psum | solution.py:146
  248.4 0.6 convert_reduce_fusion.6
  249.0 12.4 %psum.82 = f32[]{:T(128)} all-reduce(f32[]{:T(128)} %get-tuple-element.81), channel_id=1, replica_groups=mesh['seed'=8,'hid'=4] {'seed'}, use_global_device_ids=true, to_apply=%region_19.20 | all-reduce | flops 1 | bytes 8 | tf_op jit(solution)/shard_map/psum | solution.py:152
  262.1 0.2 multiply_reduce_fusion.7
  262.3 10.2 %psum.83 = f32[128]{0:T(128)S(1)} all-reduce(f32[128]{0:T(128)S(1)} %get-tuple-element.108), channel_id=1, replica_groups=mesh['seed'=8,'hid'=4] {'hid'}, use_global_device_ids=true, to_apply=%region_21.22 | all-reduce | flops 128 | bytes 1024 | tf_op jit(solution)/shard_map/psum | solution.py:57
  272.6 0.5 copy-done.40
  273.5 0.3 copy.97
  274.1 1.0 copy-done.2
  275.3 0.3 mul.352
  275.8 23.8 %reduce-scatter.6.cloned.1.call-done = f32[1024,64]{0,1:T(8,128)} async-done(((f32[1024,256]{0,1:T(8,128)}), f32[1024,64]{0,1:T(8,128)}) %reduce-scatter.6.cloned.1.call-update) | async-done | bytes 262160 | tf_op jit(solution)/shard_map/reduce_scatter | solution.py:76
  299.6 1.0 multiply_reduce_fusion.5
  300.7 9.4 %psum.84 = f32[1024]{0:T(1024)S(1)} all-reduce(f32[1024]{0:T(1024)S(1)} %multiply_reduce_fusion.5), channel_id=1, replica_groups=mesh['seed'=8,'hid'=4] {'hid'}, use_global_device_ids=true, to_apply=%region_24.25 | all-reduce | flops 1024 | bytes 8192 | tf_op jit(solution)/shard_map/psum | solution.py:57
  310.1 1.5 convolution_bitcast_fusion.1
  311.6 0.2 copy.125
  311.8 1.0 reshape.146
  312.9 0.3 reduce-scatter.8.cloned.1.call-start
  313.2 0.5 fusion.9
  313.6 1.1 slice_divide_fusion
  314.8 1.6 copy.100
  316.3 3.8 broadcast_bitcast_fusion
  320.1 9.0 %copy.102 = f32[8192,256]{0,1:T(8,128)} copy(f32[8192,256]{1,0:T(8,128)} %broadcast_bitcast_fusion) | data formatting | bytes 16777216 | tf_op jit(solution)/shard_map/mul | solution.py:43
  329.1 7.9 %broadcast_multiply_fusion = f32[8192,256]{0,1:T(8,128)} fusion(f32[8192,256]{0,1:T(8,128)} %copy.102, f32[8192]{0:T(1024)S(1)} %mul.352), kind=kLoop, calls=%fused_computation.2 | loop fusion | flops 2097152 | bytes 16809984 | tf_op jit(solution)/shard_map/mul | solution.py:43
  336.9 2.3 fusion.4
  339.4 0.7 copy-done.22
  340.4 4.8 reduce-scatter.10.cloned.1.call-done
  345.2 0.9 reshape.147
  346.2 0.7 copy.110
  347.0 0.7 copy.109
  347.7 0.7 copy.108
  348.4 143.5 %reduce-scatter.8.cloned.1.call-done = f32[8192,64]{0,1:T(8,128)} async-done(((f32[8192,256]{0,1:T(8,128)}), f32[8192,64]{0,1:T(8,128)}) %reduce-scatter.8.cloned.1.call-update) | async-done | bytes 2097168 | tf_op jit(solution)/shard_map/reduce_scatter | solution.py:76
  491.9 2.2 multiply_reduce_fusion.2
  494.1 18.5 %psum.85 = f32[8192]{0:T(1024)S(1)} all-reduce(f32[8192]{0:T(1024)S(1)} %multiply_reduce_fusion.2), channel_id=1, replica_groups=mesh['seed'=8,'hid'=4] {'hid'}, use_global_device_ids=true, to_apply=%region_27.28 | all-reduce | flops 8192 | bytes 65536 | tf_op jit(solution)/shard_map/psum | solution.py:57
  512.7 4.4 fusion.1
  517.1 23.3 %all-reduce = (f32[]{:T(128)}, f32[200,64]{0,1:T(8,128)S(1)}, f32[64,47]{0,1:T(8,128)S(1)}) all-reduce(f32[]{:T(128)} %get-tuple-element.82, f32[200,64]{0,1:T(8,128)S(1)} %fusion.1, f32[64,47]{0,1:T(8,128)S(1)} %fusion.23), channel_id=1, replica_groups=mesh['seed'=8,'hid'=4] {'seed'}, use_global_device_ids=true, to_apply=%region_17.18 | all-reduce | flops 15809 | bytes 126472 | tf_op jit(solution)/shard_map/psum | solution.py:152
  540.5 0.6 multiply_subtract_fusion.2
  541.1 0.7 multiply_subtract_fusion.1
  (148 shorter events, 3.1 us)
Async XLA Ops:
  7.2 172.9 %all-gather.2.cloned.1.call-start = ((), (), s32[]{:S(2)}) async-start(), calls=%async_computation.3 | async-start | bytes 5242880 | tf_op jit(solution)/shard_map/all_gather | solution.py:67
  10.0 10.6 %copy-start.3 = (s32[8192,10]{0,1:T(8,128)S(1)}, s32[8192,10]{0,1:T(8,128)}, u32[]{:S(2)}) copy-start(s32[8192,10]{0,1:T(8,128)} %param.20) | copy-start | bytes 983044
  75.8 1.5 copy-start.5
  75.8 1.4 copy-start.16
  77.2 1.3 copy-start.4
  78.5 22.4 %copy-start = (f32[8192,64]{0,1:T(8,128)}, f32[8192,64]{0,1:T(8,128)S(1)}, u32[]{:S(2)}) copy-start(f32[8192,64]{0,1:T(8,128)S(1)} %get-tuple-element.103) | copy-start | bytes 6291460
  99.3 1.6 copy-start.14
  99.3 1.7 copy-start.10
  99.3 1.7 copy-start.26
  99.3 2.7 copy-start.9
  100.9 198.7 %reduce-scatter.6.cloned.1.call-start = ((), (), s32[]{:S(2)}) async-start(), calls=%async_computation.4 | async-start | bytes 1310720 | tf_op jit(solution)/shard_map/reduce_scatter | solution.py:76
  195.1 0.8 copy-start.7
  196.0 25.1 %copy-start.11 = (f32[128,8]{1,0:T(8,128)S(1)}, f32[128,8]{1,0:T(8,128)}, u32[]{:S(2)}) copy-start(f32[128,8]{1,0:T(8,128)} %copy.129) | copy-start | bytes 12292
  196.3 25.2 %copy-start.36 = (f32[128]{0:T(128)S(1)}, f32[128]{0:T(128)}, u32[]{:S(2)}) copy-start(f32[128]{0:T(128)} %broadcast_maximum_fusion.2) | copy-start | bytes 1540
  196.4 36.0 %copy-start.32 = (f32[64,47]{0,1:T(8,128)S(1)}, f32[64,47]{0,1:T(8,128)}, u32[]{:S(2)}) copy-start(f32[64,47]{0,1:T(8,128)} %param.31) | copy-start | bytes 36100
  205.3 43.0 %copy-start.45 = (s32[128]{0:T(128)S(1)}, s32[128]{0:T(128)}, u32[]{:S(2)}) copy-start(s32[128]{0:T(128)} %param.23) | copy-start | bytes 1540
  205.3 43.0 %copy-start.42 = (s32[128]{0:T(128)S(1)}, s32[128]{0:T(128)}, u32[]{:S(2)}) copy-start(s32[128]{0:T(128)} %param.24) | copy-start | bytes 1540
  220.9 52.4 %copy-start.24 = (bf16[128,256]{0,1:T(8,128)(2,1)}, bf16[128,256]{0,1:T(8,128)(2,1)S(1)}, u32[]{:S(2)}) copy-start(bf16[128,256]{0,1:T(8,128)(2,1)S(1)} %slice.80) | copy-start | bytes 196612
  221.6 50.9 %copy-start.20 = (bf16[128,256]{0,1:T(8,128)(2,1)}, bf16[128,256]{0,1:T(8,128)(2,1)S(1)}, u32[]{:S(2)}) copy-start(bf16[128,256]{0,1:T(8,128)(2,1)S(1)} %divide_convert_fusion.2) | copy-start | bytes 196612
  221.9 50.7 %copy-start.27 = (f32[128,64]{0,1:T(8,128)}, f32[128,64]{0,1:T(8,128)S(1)}, u32[]{:S(2)}) copy-start(f32[128,64]{0,1:T(8,128)S(1)} %get-tuple-element.107) | copy-start | bytes 98308
  232.4 40.2 %copy-start.37 = (f32[128]{0:T(128)}, f32[128]{0:T(128)S(1)}, u32[]{:S(2)}) copy-start(f32[128]{0:T(128)S(1)} %add_rsqrt_fusion.2) | copy-start | bytes 1540
  248.3 24.3 %copy-start.12 = (f32[128,47]{0,1:T(8,128)}, f32[128,47]{0,1:T(8,128)S(1)}, u32[]{:S(2)}) copy-start(f32[128,47]{0,1:T(8,128)S(1)} %psum.80) | copy-start | bytes 72196
  249.0 23.6 %copy-start.43 = (f32[128]{0:T(128)}, f32[128]{0:T(128)S(1)}, u32[]{:S(2)}) copy-start(f32[128]{0:T(128)S(1)} %get-tuple-element.95) | copy-start | bytes 1540
  262.1 10.5 %copy-start.47 = (f32[128]{0:T(128)}, f32[128]{0:T(128)S(1)}, u32[]{:S(2)}) copy-start(f32[128]{0:T(128)S(1)} %convert_divide_fusion) | copy-start | bytes 1540
  262.3 10.3 %copy-start.30 = (f32[128,64]{0,1:T(8,128)}, f32[128,64]{0,1:T(8,128)S(1)}, u32[]{:S(2)}) copy-start(f32[128,64]{0,1:T(8,128)S(1)} %get-tuple-element.109) | copy-start | bytes 98308
  272.5 0.5 copy-start.40
  274.0 1.6 copy-start.21
  274.0 1.6 copy-start.25
  274.0 1.6 copy-start.28
  274.0 1.6 copy-start.31
  274.0 1.6 copy-start.38
  274.0 1.6 copy-start.41
  274.0 36.0 %copy-start.8 = (bf16[1024,256]{0,1:T(8,128)(2,1)S(1)}, bf16[1024,256]{0,1:T(8,128)(2,1)}, u32[]{:S(2)}) copy-start(bf16[1024,256]{0,1:T(8,128)(2,1)} %copy-done.7) | copy-start | bytes 1572868
  274.1 1.0 copy-start.2
  275.1 70.1 %reduce-scatter.10.cloned.1.call-start = ((), (), s32[]{:S(2)}) async-start(), calls=%async_computation.6 | async-start | bytes 294912
  310.1 3.1 copy-start.6
  312.9 179.0 %reduce-scatter.8.cloned.1.call-start = ((), (), s32[]{:S(2)}) async-start(), calls=%async_computation.5 | async-start | bytes 10485760 | tf_op jit(solution)/shard_map/reduce_scatter | solution.py:76
  339.2 0.8 copy-start.22
  339.2 0.9 copy-start.23
  339.2 1.0 copy-start.13
  339.2 1.0 copy-start.29
  339.2 1.0 copy-start.39
  339.2 1.0 copy-start.44
  339.2 1.0 copy-start.46
  339.3 1.0 copy-start.48
  339.3 152.6 %copy-start.1 = (f32[8192,64]{0,1:T(8,128)S(1)}, f32[8192,64]{0,1:T(8,128)}, u32[]{:S(2)}) copy-start(f32[8192,64]{0,1:T(8,128)} %copy-done) | copy-start | bytes 6291460
  348.4 164.2 %copy-start.15 = (f32[8192]{0:T(1024)S(1)}, f32[8192]{0:T(1024)}, u32[]{:S(2)}) copy-start(f32[8192]{0:T(1024)} %copy-done.14) | copy-start | bytes 98308
  512.6 27.8 %copy-start.33 = (f32[64,47]{0,1:T(8,128)S(1)}, f32[64,47]{0,1:T(8,128)}, u32[]{:S(2)}) copy-start(f32[64,47]{0,1:T(8,128)} %param.31) | copy-start | bytes 36100
  512.6 27.8 %copy-start.34 = (f32[64,47]{0,1:T(8,128)S(1)}, f32[64,47]{0,1:T(8,128)}, u32[]{:S(2)}) copy-start(f32[64,47]{0,1:T(8,128)} %param.33) | copy-start | bytes 36100
  512.7 27.8 %copy-start.35 = (f32[64,47]{0,1:T(8,128)S(1)}, f32[64,47]{0,1:T(8,128)}, u32[]{:S(2)}) copy-start(f32[64,47]{0,1:T(8,128)} %param.32) | copy-start | bytes 36100
  512.7 28.4 %copy-start.17 = (f32[200,64]{0,1:T(8,128)S(1)}, f32[200,64]{0,1:T(8,128)}, u32[]{:S(2)}) copy-start(f32[200,64]{0,1:T(8,128)} %param.25) | copy-start | bytes 153604
  512.7 28.4 %copy-start.18 = (f32[200,64]{0,1:T(8,128)S(1)}, f32[200,64]{0,1:T(8,128)}, u32[]{:S(2)}) copy-start(f32[200,64]{0,1:T(8,128)} %param.27) | copy-start | bytes 153604
  512.7 28.4 %copy-start.19 = (f32[200,64]{0,1:T(8,128)S(1)}, f32[200,64]{0,1:T(8,128)}, u32[]{:S(2)}) copy-start(f32[200,64]{0,1:T(8,128)} %param.26) | copy-start | bytes 153604
Sparse Core Ops, SparseCore 0:
  101.0 78.9 all-gather.1
  275.2 24.3 reduce-scatter.5
  313.0 32.1 reduce-scatter.9
  347.4 144.4 reduce-scatter.7
where the time goes:
time: 550 us; the launch traced here: 548 us
  waiting for transfers between devices  240 us (44%)
  blocking collectives  155 us (28%)
  other arithmetic  76 us (14%)
  local copies, waits for them, and re-layouts  52.9 us (10%)
  between operations  15.4 us (3%)
  matrix products  9.09 us (2%)
    reduce_scatter x2, waiting for transfers between devices, spread_back(): lax.psum_scatter(partial_rows, 'hid', scatter_dimension=1, tiled=True)  167 us
    all_gather x1, waiting for transfers between devices, combine(): gathered = lax.all_gather(source_rows, 'hid', axis=1, tiled=True)  67.6 us
    unnamed x5, other arithmetic  55.6 us
    psum x3, blocking collectives, normalize(): totals = lax.psum(squares, 'hid')  40.3 us
    psum x3, blocking collectives, normalize_back(): totals = lax.psum(inner, 'hid')  38.1 us
    psum x2, blocking collectives, per_device(): loss_sum, count = lax.psum((local_loss, jnp.sum(present)), 'seed')  35.7 us
    unnamed x112, local copies, waits for them, and re-layouts  22.8 us
    psum x1, blocking collectives, per_device(): full_logits = lax.psum(logits, 'hid')  15.8 us
  transfers between devices with their start and end apart: 4, of which 4 were waited for; matrix products, arithmetic and copies ran while one was open for 6% of the time, Pallas kernels for 0%

commit v1 on v0

v1 whole, which is shorter than its diff:
```python
import functools

import jax
import jax.numpy as jnp
from jax import lax
from jax.experimental import pallas as pl
from jax.experimental.pallas import tpu as pltpu
from jax.sharding import PartitionSpec as P

STEP = 5
LANES = 128


epsilon_norm = 1e-06
epsilon_adam = 1e-08
learn_rate = 0.6
decay_rate = 0.01
beta_first = 0.5
beta_second = 0.5

f32, bf16, i32 = jnp.float32, jnp.bfloat16, jnp.int32
NT = (((1,), (1,)), ((), ()))
TN = (((0,), (0,)), ((), ()))


def dot(a, b):
    return jnp.dot(a, b, preferred_element_type=f32)


def dot_nt(a, b):
    return lax.dot_general(a, b, NT, preferred_element_type=f32)


def dot_tn(a, b):
    return lax.dot_general(a, b, TN, preferred_element_type=f32)


def iota(shape, axis):
    return lax.broadcasted_iota(i32, shape, axis)


def slot_counts(links, first_row, ratio):
    lanes = links.shape[1]
    base = (first_row + iota((1, lanes), 1)) * ratio
    offsets = links - base
    counts = [
        jnp.sum(jnp.where(offsets == r, 1.0, 0.0), axis=0, keepdims=True) for r in range(ratio)
    ]
    degree = jnp.maximum(
        jnp.sum(jnp.where(links >= 0, 1.0, 0.0), axis=0, keepdims=True), 1.0
    )
    return counts, degree


def stripes(counts):
    ratio, lanes = len(counts), counts[0].shape[1]
    which = iota((8, lanes), 0) % ratio
    out = jnp.zeros((8, lanes), f32)
    for r in range(ratio):
        out = jnp.where(which == r, counts[r], out)
    return out


def spread(mask, stripe):
    rows = mask.shape[0]
    values = mask.reshape(rows // 8, 8, LANES) * stripe[None]
    return values.reshape(rows, LANES).astype(bf16)


def window_mask(rows, ratio):
    return jnp.where(iota((rows, LANES), 0) // ratio == iota((rows, LANES), 1), 1.0, 0.0)


def activate(preact):
    logistic = 1.0 / (1.0 + jnp.exp(-preact))
    active = preact * logistic
    slope = logistic * (1.0 + preact * (1.0 - logistic))
    scaling = lax.rsqrt(jnp.sum(active * active, axis=0, keepdims=True) + epsilon_norm)
    return (active * scaling).astype(bf16), active, slope, scaling


def activate_back(grad_out, active, slope, scaling):
    inner = jnp.sum(active * grad_out, axis=0, keepdims=True)
    grad_active = scaling * grad_out - active * (scaling * scaling * scaling * inner)
    return (grad_active * slope).astype(bf16)


def placement(rows, classes, width):
    gap = LANES - width
    row, col = iota((rows, classes), 0), iota((rows, classes), 1)
    target = jnp.where(col < gap, width + col, LANES + width + col - gap)
    return jnp.where(row == target, 1.0, 0.0).astype(bf16)


def compute_kernel(
    sizes,
    features, links_first, links_second, links_third,
    labels, valid, count, first_ref, low_two, low_three, head_ref,
    grad_first, grad_two, grad_three, loss_ref,
    own_rows, child_rows, own_lead, links_a, links_b, links_a_lead, links_b_lead,
    mean_one, hidden_one, active_one, slope_one, scale_one, degree_rows, stripe_rows,
    joined_two, joined_three, spread_two, mask_four, mask_eight, pre_one, sems,
):
    n3, n2, n1, n0, parts, width, classes = sizes
    q2, q1, q0 = n2 // parts, n1 // parts, n0 // parts
    r3, r2, r1 = n3 // n2, n2 // n1, n1 // n0
    z = lax.axis_index("hid")
    two = q2 + q1 + LANES
    hid = 256

    def at(unit):
        return pl.ds(pl.multiple_of(z * unit, LANES), unit)

    copies = [
        (links_first.at[:, at(q2)], links_a.at[:, pl.ds(0, q2)]),
        (links_first.at[:, at(q1)], links_a.at[:, pl.ds(q2, q1)]),
        (links_first.at[:, pl.ds(0, LANES)], links_a_lead),
        (links_second.at[:, at(q1)], links_b),
        (links_second.at[:, pl.ds(0, LANES)], links_b_lead),
        (features.at[:, pl.ds(0, LANES)], own_lead),
        (features.at[:, at(q2)], own_rows.at[:, pl.ds(0, q2)]),
        (features.at[:, at(q1)], own_rows.at[:, pl.ds(q2, q1)]),
        (features.at[:, at(q2 * r3)], child_rows.at[:, pl.ds(0, q2 * r3)]),
        (features.at[:, at(q1 * r3)], child_rows.at[:, pl.ds(q2 * r3, q1 * r3)]),
        (
            features.at[:, pl.ds(pl.multiple_of(z * q0 * r3, LANES), LANES * r3)],
            child_rows.at[:, pl.ds((q2 + q1) * r3, LANES * r3)],
        ),
    ]
    started = [pltpu.make_async_copy(src, dst, sems.at[i]) for i, (src, dst) in enumerate(copies)]
    for copy in started:
        copy.start()
    mask_four[...] = window_mask(LANES * r3, r3)
    mask_eight[...] = window_mask(LANES * r2, r2)
    mean_one[...] = jnp.zeros_like(mean_one)
    for copy in started:
        copy.wait()

    counts_a, degree_a = slot_counts(links_a_lead[...], 0, r3)
    counts_b, degree_b = slot_counts(links_b_lead[...], 0, r2)
    counts_c, degree_c = slot_counts(links_third[...], 0, r1)
    lead = [*counts_a, degree_a, *counts_b, degree_b, *counts_c, degree_c]
    lead += [labels[...].astype(f32), valid[...].astype(f32)]
    packed = jnp.zeros((32, LANES), f32)
    for k, row in enumerate(lead):
        packed = jnp.where(iota((32, LANES), 0) == k, row, packed)
    source, target = iota((LANES, LANES), 0), iota((LANES, LANES), 1)
    mine = jnp.where((source == target + z * q0) & (target < q0), 1.0, 0.0).astype(bf16)
    packed = dot(packed.astype(bf16), mine)
    take = [packed[k : k + 1] for k in range(len(lead))]
    counts_a, degree_a = take[:r3], jnp.maximum(take[r3], 1.0)
    take = take[r3 + 1 :]
    counts_b, degree_b = take[:r2], jnp.maximum(take[r2], 1.0)
    take = take[r2 + 1 :]
    counts_c, degree_c = take[:r1], jnp.maximum(take[r1], 1.0)
    label, present = take[r1 + 1], take[r1 + 2]
    own_rows[:, pl.ds(q2 + q1, LANES)] = dot(own_lead[...], mine).astype(bf16)

    counts, degree = slot_counts(links_a[:, pl.ds(0, q2)], z * q2, r3)
    for t in range(q2 // LANES):
        stripe_rows[t] = stripes([c[:, t * LANES : (t + 1) * LANES] for c in counts])
    degree_rows[:, pl.ds(0, q2)] = degree
    counts, degree = slot_counts(links_a[:, pl.ds(q2, q1)], z * q1, r3)
    for t in range(q1 // LANES):
        stripe_rows[q2 // LANES + t] = stripes([c[:, t * LANES : (t + 1) * LANES] for c in counts])
    degree_rows[:, pl.ds(q2, q1)] = degree
    stripe_rows[two // LANES - 1] = stripes(counts_a)
    degree_rows[:, pl.ds(q2 + q1, LANES)] = degree_a

    def layer_one(tile, tiles):
        for t in range(tiles):
            lanes = pl.ds(pl.multiple_of((tile + t) * LANES, LANES), LANES)
            kids = pl.ds(pl.multiple_of((tile + t) * LANES * r3, LANES), LANES * r3)
            matrix = spread(mask_four[...], stripe_rows[tile + t])
            mean = dot(child_rows[:, kids], matrix) / degree_rows[:, lanes]
            mean_one[0:width, lanes] = mean.astype(bf16)
        lanes = pl.ds(pl.multiple_of(tile * LANES, LANES), LANES * tiles)
        preact = dot(first_ref[:, 0:width], own_rows[:, lanes])
        preact += dot(first_ref[:, LANES : 2 * LANES], mean_one[:, lanes])
        output, active, slope, scaling = activate(preact)
        hidden_one[:, lanes] = output
        active_one[:, lanes] = active
        slope_one[:, lanes] = slope
        scale_one[:, lanes] = scaling

    per = 4
    lax.fori_loop(0, q2 // LANES // per, lambda i, c: (layer_one(i * per, per), c)[1], 0)
    layer_one(q2 // LANES, q1 // LANES + 1)

    counts, degree_t = slot_counts(links_b[...], z * q1, r2)
    joined_two[0:hid, :] = hidden_one[:, pl.ds(q2, q1 + LANES)]
    for t in range(q1 // LANES):
        stripe = stripes([c[:, t * LANES : (t + 1) * LANES] for c in counts])
        rows = pl.ds(t * LANES * r2, LANES * r2)
        spread_two[rows, :] = spread(mask_eight[...], stripe)
        mean = dot(hidden_one[:, rows], spread_two[rows, :])
        lanes = slice(t * LANES, (t + 1) * LANES)
        joined_two[hid:, lanes] = (mean / degree_t[:, lanes]).astype(bf16)
    spread_lead = spread(mask_eight[0 : q0 * r2, :], stripes(counts_b))
    mean = dot(hidden_one[:, pl.ds(q2, q1)], spread_lead)
    joined_two[hid:, pl.ds(q1, LANES)] = (mean / degree_b).astype(bf16)
    preact = dot_tn(low_two[...], joined_two[...])
    output, active_two, slope_two, scale_two = activate(preact)

    joined_three[0:hid, :] = output[:, q1:]
    spread_three = spread(mask_eight[0 : q0 * r1, :], stripes(counts_c))
    mean = dot(output[:, 0:q1], spread_three)
    joined_three[hid:, :] = (mean / degree_c).astype(bf16)
    preact = dot_tn(low_three[...], joined_three[...])
    seeds, active_three, slope_three, scale_three = activate(preact)

    logits = dot(head_ref[...], seeds)
    row = iota(logits.shape, 0)
    logits = jnp.where(row < classes, logits, -1e30)
    peak = jnp.max(logits, axis=0, keepdims=True)
    shifted = jnp.exp(logits - peak)
    totals = jnp.sum(shifted, axis=0, keepdims=True)
    hot = jnp.where(row.astype(f32) == label, 1.0, 0.0)
    nll = peak + jnp.log(totals) - jnp.sum(jnp.where(hot > 0, logits, 0.0), axis=0, keepdims=True)
    loss = jnp.sum(jnp.where(present > 0, nll, 0.0), axis=1, keepdims=True)
    loss_ref[...] = jnp.broadcast_to(loss, loss_ref.shape)
    share = present / jnp.maximum(count[0, 0], 1.0)
    grad_logits = ((shifted / totals - hot) * share).astype(bf16)
    placed = dot(placement(2 * LANES, grad_logits.shape[0], width), grad_logits).astype(bf16)
    grad_first[...] = dot_nt(seeds, placed)
    grad_out = dot_tn(head_ref[...], grad_logits)

    grad_pre = activate_back(grad_out, active_three, slope_three, scale_three)
    grad_three[...] = dot_nt(joined_three[...], grad_pre)
    grad_joined = dot(low_three[...], grad_pre)
    grad_mean = (grad_joined[hid:] / degree_c).astype(bf16)
    grad_out = jnp.concatenate([dot_nt(grad_mean, spread_three), grad_joined[0:hid]], axis=1)

    grad_pre = activate_back(grad_out, active_two, slope_two, scale_two)
    grad_two[...] = dot_nt(joined_two[...], grad_pre)
    grad_joined = dot(low_two[...], grad_pre)
    grad_mean = (grad_joined[hid:, 0:q1] / degree_t).astype(bf16)
    lead_mean = (grad_joined[hid:, q1:] / degree_b).astype(bf16)

    pieces = q2 // LANES // per
    for i in range(pieces):
        tile = i * per * LANES
        lanes = pl.ds(tile, per * LANES)
        group = tile // (LANES * r2) * LANES
        grad_out = dot_nt(grad_mean[:, group : group + LANES], spread_two[lanes, :])
        pre_one[:, lanes] = activate_back(
            grad_out, active_one[:, lanes], slope_one[:, lanes], scale_one[:, lanes]
        )
    own = grad_joined[0:hid]
    lanes = pl.ds(q2, q1)
    pre_one[:, lanes] = activate_back(
        own[:, 0:q1] + dot_nt(lead_mean, spread_lead),
        active_one[:, lanes], slope_one[:, lanes], scale_one[:, lanes],
    )
    lanes = pl.ds(q2 + q1, LANES)
    pre_one[:, lanes] = activate_back(
        own[:, q1:], active_one[:, lanes], slope_one[:, lanes], scale_one[:, lanes]
    )
    grad_first[:, 0:width] = dot_nt(pre_one[...], own_rows[...])
    grad_first[:, LANES : LANES + width] = dot_nt(pre_one[...], mean_one[0:width, :])


def compute(sizes, *operands):
    n3, n2, n1, n0, parts, width, classes = sizes
    q2, q1 = n2 // parts, n1 // parts
    r3, r2 = n3 // n2, n2 // n1
    two = q2 + q1 + LANES
    slots = operands[1].shape[0]
    slots_b = operands[2].shape[0]
    hbm, vmem = pl.BlockSpec(memory_space=pl.ANY), pl.BlockSpec(memory_space=pltpu.VMEM)
    smem = pl.BlockSpec(memory_space=pltpu.SMEM)
    shape = jax.ShapeDtypeStruct
    return pl.pallas_call(
        functools.partial(compute_kernel, sizes),
        out_shape=(
            shape((256, 256), f32), shape((512, 256), f32), shape((512, 256), f32), shape((8, LANES), f32),
        ),
        in_specs=[hbm, hbm, hbm, vmem, vmem, vmem, smem, vmem, vmem, vmem, vmem],
        out_specs=(vmem,) * 4,
        scratch_shapes=[
            pltpu.VMEM((width, two), bf16),
            pltpu.VMEM((width, two * r3), bf16),
            pltpu.VMEM((width, LANES), bf16),
            pltpu.VMEM((slots, q2 + q1), i32),
            pltpu.VMEM((slots_b, q1), i32),
            pltpu.VMEM((slots, LANES), i32),
            pltpu.VMEM((slots_b, LANES), i32),
            pltpu.VMEM((LANES, two), bf16),
            pltpu.VMEM((256, two), bf16),
            pltpu.VMEM((256, two), f32),
            pltpu.VMEM((256, two), f32),
            pltpu.VMEM((1, two), f32),
            pltpu.VMEM((1, two), f32),
            pltpu.VMEM((two // LANES, 8, LANES), f32),
            pltpu.VMEM((512, q1 + LANES), bf16),
            pltpu.VMEM((512, LANES), bf16),
            pltpu.VMEM((q2, LANES), bf16),
            pltpu.VMEM((LANES * r3, LANES), f32),
            pltpu.VMEM((LANES * r2, LANES), f32),
            pltpu.VMEM((256, two), bf16),
            pltpu.SemaphoreType.DMA((11,)),
        ],
        compiler_params=pltpu.CompilerParams(vmem_limit_bytes=56 * 2**20),
    )(*operands)


def adamw(weight, moment, square, grad):
    new_moment = beta_first * moment + (1.0 - beta_first) * grad
    new_square = beta_second * square + (1.0 - beta_second) * grad * grad
    moment_hat = new_moment / (1.0 - beta_first**STEP)
    square_hat = new_square / (1.0 - beta_second**STEP)
    new_weight = weight - learn_rate * (
        moment_hat / (jnp.sqrt(square_hat) + epsilon_adam) + decay_rate * weight
    )
    return (new_moment, new_square, new_weight)


def per_device(
    features,
    links_first,
    links_second,
    links_third,
    labels,
    valid,
    weight_first,
    moment_first,
    square_first,
    weight_stack,
    moment_stack,
    square_stack,
    weight_head,
    moment_head,
    square_head,
):
    parts = lax.axis_size("hid")
    width, classes = features.shape[1], weight_head.shape[1]
    sizes = (
        features.shape[0], links_first.shape[0], links_second.shape[0], links_third.shape[0],
        parts, width, classes,
    )
    stack_low = lax.all_gather(weight_stack.astype(bf16), "seed", axis=1, tiled=True)
    stack_low = lax.all_gather(stack_low, "hid", axis=2, tiled=True)
    first_low = weight_first.T.astype(bf16)
    first_low = jnp.pad(first_low.reshape(-1, 2, width), ((0, 0), (0, 0), (0, LANES - width)))
    first_low = lax.all_gather(first_low.reshape(-1, 2 * LANES), "hid", axis=0, tiled=True)
    head_low = jnp.pad(weight_head.T.astype(bf16), ((0, 48 - classes), (0, 0)))
    head_low = lax.all_gather(head_low, "hid", axis=1, tiled=True)
    count = lax.psum(jnp.sum(valid.astype(f32)), "seed")
    grad_first, grad_two, grad_three, loss = compute(
        sizes,
        features.T, links_first.T, links_second.T, links_third.T,
        labels.reshape(1, -1), valid.reshape(1, -1), count.reshape(1, 1),
        first_low, stack_low[0], stack_low[1], head_low,
    )
    loss_sum = lax.psum(loss[0, 0], ("seed", "hid"))
    grad_stack = jnp.stack([grad_two, grad_three]).astype(bf16)
    grad_stack = lax.psum_scatter(grad_stack, "seed", scatter_dimension=1, tiled=True)
    grad_stack = lax.psum_scatter(grad_stack, "hid", scatter_dimension=2, tiled=True).astype(f32)
    grad_first = lax.psum_scatter(grad_first, "hid", scatter_dimension=0, tiled=True)
    grad_first = lax.psum(grad_first, "seed")
    gap = LANES - width
    grad_head = jnp.concatenate(
        [grad_first[:, width:LANES], grad_first[:, LANES + width : LANES + width + classes - gap]], axis=1
    )
    grad_first = jnp.concatenate(
        [grad_first[:, :width], grad_first[:, LANES : LANES + width]], axis=1
    ).T
    moment_a, square_a, weight_a = adamw(weight_first, moment_first, square_first, grad_first)
    moment_b, square_b, weight_b = adamw(weight_stack, moment_stack, square_stack, grad_stack)
    moment_c, square_c, weight_c = adamw(weight_head, moment_head, square_head, grad_head)
    return (
        loss_sum,
        count,
        moment_a,
        square_a,
        weight_a,
        moment_b,
        square_b,
        weight_b,
        moment_c,
        square_c,
        weight_c,
    )


def solution(mesh):
    placed = (
        P("seed", None),
        P("seed", None),
        P("seed", None),
        P("seed", None),
        P("seed"),
        P("seed"),
        P(None, "hid"),
        P(None, "hid"),
        P(None, "hid"),
        P(None, "seed", "hid"),
        P(None, "seed", "hid"),
        P(None, "seed", "hid"),
        P("hid", None),
        P("hid", None),
        P("hid", None),
    )
    return jax.shard_map(
        per_device,
        mesh=mesh,
        in_specs=placed,
        out_specs=(P(), P()) + placed[6:],
        check_vma=False,
    )
```

time: 550 us -> 236 us (0.43)
  waiting for transfers between devices: 240 us -> 83.2 us
  other arithmetic: 76 us -> 6.54 us
  blocking collectives: 155 us -> 106 us
  local copies, waits for them, and re-layouts: 52.9 us -> 13.5 us
  Pallas kernels: 0 us -> 12.6 us
  matrix products: 9.09 us -> 0 us
    reduce_scatter x2, waiting for transfers between devices: 167 us -> 50.9 us  [the longest x1 32 us: per_device(): lax.psum_scatter(grad_stack, 'seed', scatter_dimension=1, tiled=True)]
    psum x9 -> x2, blocking collectives: 130 us -> 51.1 us  [the longest x1 38.7 us: per_device(): loss_sum = lax.psum(loss[0, 0], ('seed', 'hid'))]
    all_gather x1 -> x0, waiting for transfers between devices: 67.6 us -> none  [combine(): gathered = lax.all_gather(source_rows, 'hid', axis=1, tiled=True)]
    unnamed x5 -> x0, other arithmetic: 55.6 us -> none
    all_gather x2 -> x4, blocking collectives: 25 us -> 54.4 us  [the longest x1 16.4 us: per_device(): stack_low = lax.all_gather(stack_low, 'hid', axis=2, tiled=True)]
    unnamed x5, waiting for transfers between devices: 4.86 us -> 19.3 us
    unnamed x112 -> x34, local copies, waits for them, and re-layouts: 22.8 us -> 8.82 us
    mul x6 -> x0, local copies, waits for them, and re-layouts: 13.5 us -> none  [mean_rows_back(): shares = (grad_mean / degree[:, None])[:, None, :] * counts[:, :, None]]
  transfers between devices with their start and end apart: 4 -> 4, of which waited for: 4 -> 4; matrix products, arithmetic and copies ran while one was open for 6% -> 4% of each run, Pallas kernels for 0% -> 0%
where the time goes in v1:
time: 236 us; the launch traced here: 235 us
  blocking collectives  106 us (45%)
  waiting for transfers between devices  83.2 us (35%)
  between operations  14 us (6%)
  local copies, waits for them, and re-layouts  13.5 us (6%)
  Pallas kernels  12.6 us (5%)
  other arithmetic  6.54 us (3%)
    psum x1, blocking collectives, per_device(): loss_sum = lax.psum(loss[0, 0], ('seed', 'hid'))  38.7 us
    reduce_scatter x1, waiting for transfers between devices, per_device(): lax.psum_scatter(grad_stack, 'seed', scatter_dimension=1, tiled=True)  32 us
    unnamed x5, waiting for transfers between devices  19.3 us
    reduce_scatter x1, waiting for transfers between devices, per_device(): lax.psum_scatter(grad_first, 'hid', scatter_dimension=0, tiled=True)  19 us
    all_gather x1, blocking collectives, per_device(): stack_low = lax.all_gather(stack_low, 'hid', axis=2, tiled=True)  16.4 us
    all_gather x1, blocking collectives, per_device(): lax.all_gather(first_low.reshape(-1, 2 * LANES), 'hid', axis=0, tiled=True)  14.2 us
    all_gather x1, blocking collectives, per_device(): head_low = lax.all_gather(head_low, 'hid', axis=1, tiled=True)  13.1 us
    psum x1, waiting for transfers between devices, per_device(): grad_first = lax.psum(grad_first, 'seed')  12.9 us
  transfers between devices with their start and end apart: 4, of which 4 were waited for; matrix products, arithmetic and copies ran while one was open for 4% of the time, Pallas kernels for 0%

profile of v1, /device:TPU:0, one launch (start us, length us, event | category | flops | bytes accessed | tf_op | source)
XLA Modules:
  0.0 235.4 jit_solution(5324242903545695385)
XLA Ops:
  7.2 0.0 reduce-scatter.6.cloned.1.call-start
  7.2 0.9 copy.79
  8.1 10.8 %all_gather.13 = bf16[2,512,64]{2,0,1:T(2,128)(2,1)S(1)} all-gather(bf16[2,64,64]{2,0,1:T(2,128)(2,1)S(1)} %copy.79), channel_id=1, replica_groups=mesh['seed'=8,'hid'=4] {'seed'}, dimensions={1}, use_global_device_ids=true | all-gather | bytes 147456 | tf_op jit(solution)/shard_map/all_gather | solution.py:341
  18.9 0.2 copy.58
  19.1 16.4 %all_gather.14 = bf16[2,512,256]{1,0,2:T(2,128)(2,1)S(1)} all-gather(bf16[2,512,64]{1,0,2:T(2,128)(2,1)S(1)} %copy.58), channel_id=1, replica_groups=mesh['seed'=8,'hid'=4] {'hid'}, dimensions={2}, use_global_device_ids=true | all-gather | bytes 655360 | tf_op jit(solution)/shard_map/all_gather | solution.py:342
  35.4 0.7 fusion.6
  36.2 0.0 copy-start.2
  36.2 0.0 copy-start.7
  36.2 1.1 copy.74
  37.3 0.0 copy-start.8
  37.3 1.3 convert_reduce_fusion
  38.6 1.1 copy.75
  39.7 12.4 %psum.21 = f32[]{:T(128)} all-reduce(f32[]{:T(128)} %convert_reduce_fusion), channel_id=1, replica_groups=mesh['seed'=8,'hid'=4] {'seed'}, use_global_device_ids=true, to_apply=%region_1.2 | all-reduce | flops 1 | bytes 8 | tf_op jit(solution)/shard_map/psum | solution.py:348
  52.1 0.8 convert_bitcast_fusion.2
  53.0 0.0 copy-start.4
  53.0 0.1 reshape.40
  53.1 14.2 %all_gather.12.first_ref = bf16[256,256]{1,0:T(8,128)(2,1)} all-gather(bf16[64,256]{1,0:T(8,128)(2,1)S(1)} %bitcast.44), channel_id=1, replica_groups=mesh['seed'=8,'hid'=4] {'hid'}, dimensions={0}, use_global_device_ids=true | all-gather | bytes 163840 | tf_op jit(solution)/shard_map/all_gather | solution.py:345
  67.3 0.7 convert_bitcast_fusion.3
  68.0 13.1 %all-gather = bf16[4,64,48]{1,2,0:T(8,128)(2,1)S(1)} all-gather(bf16[1,64,48]{1,2,0:T(8,128)(2,1)S(1)} %pad_bitcast_fusion), channel_id=1, replica_groups=mesh['seed'=8,'hid'=4] {'hid'}, dimensions={0}, use_global_device_ids=true | all-gather | bytes 30720 | tf_op jit(solution)/shard_map/all_gather | solution.py:347
  81.2 0.0 copy-start.1
  81.2 0.0 copy-start.5
  81.2 0.0 copy-start.6
  81.2 0.7 reshape.43
  81.9 12.6 %shard_map.230 = (f32[256,256]{1,0:T(8,128)}, f32[512,256]{1,0:T(8,128)}, f32[512,256]{1,0:T(8,128)}, f32[8,128]{1,0:T(8,128)}) custom-call(bf16[100,32768]{1,0:T(8,128)(2,1)} %bitcast.39, s32[10,8192]{1,0:T(8,128)} %bitcast.42, s32[10,1024]{1,0:T(8,128)} %bitcast.48, s32[25,128]{1,0:T(8,128)} %bitcast.49, s32[1,128]{1,0:T(1,128)} %bitcast.50, ...), custom_call_target="tpu_custom_call" | custom-call | tf_op jit(solution)/shard_map/pallas_call | solution.py:273
  94.5 0.0 reduce-scatter.6.cloned.1.call-update
  94.5 0.0 all-reduce.4.cloned.1.call-start
  94.5 1.3 convert_bitcast_fusion
  95.8 19.0 %reduce-scatter.6.cloned.1.call-done = f32[64,256]{1,0:T(8,128)} async-done(((f32[256,256]{1,0:T(8,128)}), f32[64,256]{1,0:T(8,128)}) %reduce-scatter.6.cloned.1.call-update) | async-done | bytes 65552 | tf_op jit(solution)/shard_map/reduce_scatter | solution.py:359
  114.8 0.0 all-reduce.4.cloned.1.call-update
  114.8 0.0 reduce-scatter.8.cloned.1.call-start
  114.8 0.8 pad_maximum_fusion
  115.7 0.0 reduce-scatter.8.cloned.1.call-update
  115.7 0.0 reduce-scatter.10.cloned.1.call-start
  115.8 1.2 slice.23
  117.0 38.7 %psum.22 = f32[]{:T(128)} all-reduce(f32[]{:T(128)} %bitcast.16), channel_id=1, replica_groups=mesh['seed'=8,'hid'=4] {'seed','hid'}, use_global_device_ids=true, to_apply=%region_2.3 | all-reduce | flops 1 | bytes 8 | tf_op jit(solution)/shard_map/psum | solution.py:355
  155.6 0.0 copy-done.2
  155.6 0.1 copy.68
  155.7 0.0 copy-done.7
  155.7 0.1 copy.62
  155.8 0.0 copy-done.8
  155.8 0.1 copy.65
  155.9 12.9 %all-reduce.4.cloned.1.call-done = f32[64,256]{1,0:T(8,128)} async-done(((f32[64,256]{1,0:T(8,128)}), f32[64,256]{1,0:T(8,128)}) %all-reduce.4.cloned.1.call-update) | async-done | bytes 65552 | tf_op jit(solution)/shard_map/psum | solution.py:360
  168.9 0.8 slice.32
  169.7 0.8 slice.33
  170.5 0.1 multiply_subtract_fusion.2
  170.6 0.7 copy.69
  171.3 0.7 copy.70
  172.0 0.7 copy.71
  172.7 0.8 fusion.7
  173.5 32.0 %reduce-scatter.8.cloned.1.call-done = bf16[2,64,256]{2,1,0:T(8,128)(2,1)} async-done(((bf16[2,512,256]{2,1,0:T(8,128)(2,1)}), bf16[2,64,256]{2,1,0:T(8,128)(2,1)}) %reduce-scatter.8.cloned.1.call-update) | async-done | bytes 65552 | tf_op jit(solution)/shard_map/reduce_scatter | solution.py:357
  205.5 1.0 copy.72
  206.4 0.7 reshape.44
  207.2 0.0 reduce-scatter.10.cloned.1.call-update
  207.2 0.0 copy-done
  207.2 0.0 copy-done.3
  207.2 0.0 copy-done.4
  207.2 0.8 multiply_subtract_fusion.1
  208.0 19.3 %reduce-scatter.10.cloned.1.call-done = bf16[64,128]{1,0:T(8,128)(2,1)} async-done(((bf16[256,128]{1,0:T(8,128)(2,1)}), bf16[64,128]{1,0:T(8,128)(2,1)}) %reduce-scatter.10.cloned.1.call-update) | async-done | bytes 16400
  227.3 0.8 reshape.45
  228.1 0.1 copy.73
  228.2 0.0 copy-done.1
  228.2 0.0 copy-done.5
  228.2 0.0 copy-done.6
  228.2 0.7 multiply_subtract_fusion
  (6 shorter events, 0.1 us)
Async XLA Ops:
  7.2 107.6 %reduce-scatter.6.cloned.1.call-start = ((), (), s32[]{:S(2)}) async-start(), calls=%async_computation.3 | async-start | bytes 327680 | tf_op jit(solution)/shard_map/reduce_scatter | solution.py:359
  36.2 119.5 %copy-start.2 = (f32[64,47]{0,1:T(8,128)S(1)}, f32[64,47]{0,1:T(8,128)}, u32[]{:S(2)}) copy-start(f32[64,47]{0,1:T(8,128)} %param.27) | copy-start | bytes 36100
  36.2 119.6 %copy-start.7 = (f32[64,47]{0,1:T(8,128)S(1)}, f32[64,47]{0,1:T(8,128)}, u32[]{:S(2)}) copy-start(f32[64,47]{0,1:T(8,128)} %param.28) | copy-start | bytes 36100
  37.3 118.5 %copy-start.8 = (f32[64,47]{0,1:T(8,128)S(1)}, f32[64,47]{0,1:T(8,128)}, u32[]{:S(2)}) copy-start(f32[64,47]{0,1:T(8,128)} %param.29) | copy-start | bytes 36100
  52.9 154.3 %copy-start = (f32[200,64]{0,1:T(8,128)S(1)}, f32[200,64]{0,1:T(8,128)}, u32[]{:S(2)}) copy-start(f32[200,64]{0,1:T(8,128)} %param.21) | copy-start | bytes 153604
  53.0 154.3 %copy-start.3 = (f32[200,64]{0,1:T(8,128)S(1)}, f32[200,64]{0,1:T(8,128)}, u32[]{:S(2)}) copy-start(f32[200,64]{0,1:T(8,128)} %param.23) | copy-start | bytes 153604
  53.0 154.3 %copy-start.4 = (f32[200,64]{0,1:T(8,128)S(1)}, f32[200,64]{0,1:T(8,128)}, u32[]{:S(2)}) copy-start(f32[200,64]{0,1:T(8,128)} %param.22) | copy-start | bytes 153604
  81.2 147.0 %copy-start.1 = (f32[2,64,64]{2,1,0:T(8,128)S(1)}, f32[2,64,64]{2,1,0:T(8,128)}, u32[]{:S(2)}) copy-start(f32[2,64,64]{2,1,0:T(8,128)} %param.24) | copy-start | bytes 98308
  81.2 147.0 %copy-start.5 = (f32[2,64,64]{2,1,0:T(8,128)S(1)}, f32[2,64,64]{2,1,0:T(8,128)}, u32[]{:S(2)}) copy-start(f32[2,64,64]{2,1,0:T(8,128)} %param.26) | copy-start | bytes 98308
  81.2 147.0 %copy-start.6 = (f32[2,64,64]{2,1,0:T(8,128)S(1)}, f32[2,64,64]{2,1,0:T(8,128)}, u32[]{:S(2)}) copy-start(f32[2,64,64]{2,1,0:T(8,128)} %param.25) | copy-start | bytes 98308
  94.5 74.4 %all-reduce.4.cloned.1.call-start = ((), (), s32[]{:S(2)}) async-start(), calls=%async_computation.4 | async-start | bytes 131072 | tf_op jit(solution)/shard_map/psum | solution.py:360
  114.8 90.7 %reduce-scatter.8.cloned.1.call-start = ((), (), s32[]{:S(2)}) async-start(), calls=%async_computation.5 | async-start | bytes 589824 | tf_op jit(solution)/shard_map/reduce_scatter | solution.py:357
  115.7 111.6 %reduce-scatter.10.cloned.1.call-start = ((), (), s32[]{:S(2)}) async-start(), calls=%async_computation.6 | async-start | bytes 81920
Sparse Core Ops, SparseCore 0:
  94.6 20.1 reduce-scatter.5
  118.1 50.7 all-reduce.3
  171.9 33.4 reduce-scatter.7
  208.2 19.0 reduce-scatter.9

commit v2 on v1

v2 whole, which is shorter than its diff:
```python
import functools

import jax
import jax.numpy as jnp
from jax import lax
from jax.experimental import pallas as pl
from jax.experimental.pallas import tpu as pltpu
from jax.sharding import PartitionSpec as P

STEP = 5
LANES = 128


epsilon_norm = 1e-06
epsilon_adam = 1e-08
learn_rate = 0.6
decay_rate = 0.01
beta_first = 0.5
beta_second = 0.5

f32, bf16, i32 = jnp.float32, jnp.bfloat16, jnp.int32
MESH = pl.DeviceIdType.MESH
NT = (((1,), (1,)), ((), ()))
TN = (((0,), (0,)), ((), ()))


def dot(a, b):
    return jnp.dot(a, b, preferred_element_type=f32)


def dot_nt(a, b):
    return lax.dot_general(a, b, NT, preferred_element_type=f32)


def dot_tn(a, b):
    return lax.dot_general(a, b, TN, preferred_element_type=f32)


def iota(shape, axis):
    return lax.broadcasted_iota(i32, shape, axis)


def slot_counts(links, first_row, ratio):
    lanes = links.shape[1]
    base = (first_row + iota((1, lanes), 1)) * ratio
    offsets = links - base
    counts = [
        jnp.sum(jnp.where(offsets == r, 1.0, 0.0), axis=0, keepdims=True) for r in range(ratio)
    ]
    degree = jnp.maximum(
        jnp.sum(jnp.where(links >= 0, 1.0, 0.0), axis=0, keepdims=True), 1.0
    )
    return counts, degree


def stripes(counts):
    ratio, lanes = len(counts), counts[0].shape[1]
    which = iota((8, lanes), 0) % ratio
    out = jnp.zeros((8, lanes), f32)
    for r in range(ratio):
        out = jnp.where(which == r, counts[r], out)
    return out


def spread(mask, stripe):
    rows = mask.shape[0]
    values = mask.reshape(rows // 8, 8, LANES) * stripe[None]
    return values.reshape(rows, LANES).astype(bf16)


def window_mask(rows, ratio):
    return jnp.where(iota((rows, LANES), 0) // ratio == iota((rows, LANES), 1), 1.0, 0.0)


def activate(preact):
    logistic = 1.0 / (1.0 + jnp.exp(-preact))
    active = preact * logistic
    slope = logistic * (1.0 + preact * (1.0 - logistic))
    scaling = lax.rsqrt(jnp.sum(active * active, axis=0, keepdims=True) + epsilon_norm)
    return (active * scaling).astype(bf16), active, slope, scaling


def activate_back(grad_out, active, slope, scaling):
    inner = jnp.sum(active * grad_out, axis=0, keepdims=True)
    grad_active = scaling * grad_out - active * (scaling * scaling * scaling * inner)
    return (grad_active * slope).astype(bf16)


def placement_rows(classes, columns, width):
    gap = LANES - width
    row, col = iota((classes, columns), 0), iota((classes, columns), 1)
    target = jnp.where(row < gap, width + row, LANES + width + row - gap)
    return jnp.where(col == target, 1.0, 0.0).astype(bf16)


def placement(rows, classes, width):
    gap = LANES - width
    row, col = iota((rows, classes), 0), iota((rows, classes), 1)
    target = jnp.where(col < gap, width + col, LANES + width + col - gap)
    return jnp.where(row == target, 1.0, 0.0).astype(bf16)


def shift_half(x):
    return pltpu.roll(x, LANES // 2, 1)


def step_kernel(
    sizes,
    features, links_first, links_second, links_third, labels, valid, weight_first, weight_stack, weight_head,
    first_out, stack_out, count_out,
    own_rows, child_rows, own_lead, links_a, links_b, links_a_lead, links_b_lead,
    mean_one, hidden_one, active_one, slope_one, scale_one, degree_rows, stripe_rows,
    joined_two, joined_three, spread_two, mask_four, mask_eight, pre_one,
    first_all, stack_all, valid_all, low_two, low_three,
    core_send, core_recv, stack_send, stack_recv, grad_one, first_send, first_recv, first_piece,
    local_sems, first_ssem, first_rsem, block_ssem, block_rsem, pair_ssem, pair_rsem, valid_ssem, valid_rsem,
    core_ssem, core_rsem, back_ssem, back_rsem, piece_ssem, piece_rsem, share_ssem, share_rsem,
):
    n3, n2, n1, n0, parts, seeds_axis, width, classes = sizes
    q2, q1, q0 = n2 // parts, n1 // parts, n0 // parts
    r3, r2, r1 = n3 // n2, n2 // n1, n1 // n0
    s, z = lax.axis_index("seed"), lax.axis_index("hid")
    core, chip = lax.rem(s, 2), s // 2
    chips = seeds_axis // 2
    sibling = s + 1 - 2 * core
    two = q2 + q1 + LANES
    hid = 256
    unit = hid // parts
    own_units = pl.ds(pl.multiple_of(z * unit, unit), unit)
    everyone = [(k, d) for d in range(parts) for k in range(seeds_axis) if (k, d) != (0, 0)]

    def place(k, d):
        return (lax.rem(s + k, seeds_axis), lax.rem(z + d, parts))

    barrier = pltpu.get_barrier_semaphore()
    for k, d in everyone:
        pl.semaphore_signal(barrier, inc=1, device_id=place(k, d), device_id_type=MESH)

    def at(size):
        return pl.ds(pl.multiple_of(z * size, LANES), size)

    copies = [
        (links_first.at[:, at(q2)], links_a.at[:, pl.ds(0, q2)]),
        (links_first.at[:, at(q1)], links_a.at[:, pl.ds(q2, q1)]),
        (links_first.at[:, pl.ds(0, LANES)], links_a_lead),
        (links_second.at[:, at(q1)], links_b),
        (links_second.at[:, pl.ds(0, LANES)], links_b_lead),
        (features.at[:, pl.ds(0, LANES)], own_lead),
        (features.at[:, at(q2)], own_rows.at[:, pl.ds(0, q2)]),
        (features.at[:, at(q1)], own_rows.at[:, pl.ds(q2, q1)]),
        (features.at[:, at(q2 * r3)], child_rows.at[:, pl.ds(0, q2 * r3)]),
        (features.at[:, at(q1 * r3)], child_rows.at[:, pl.ds(q2 * r3, q1 * r3)]),
        (
            features.at[:, pl.ds(pl.multiple_of(z * q0 * r3, LANES), LANES * r3)],
            child_rows.at[:, pl.ds((q2 + q1) * r3, LANES * r3)],
        ),
    ]
    started = [pltpu.make_async_copy(src, dst, local_sems.at[i]) for i, (src, dst) in enumerate(copies)]
    for copy in started:
        copy.start()

    row, col = iota((2 * width, hid), 0), iota((2 * width, hid), 1)
    columns = jnp.where(row < width, row, row - width + LANES)
    lift = jnp.where(columns == col, 1.0, 0.0).astype(bf16)
    seat = placement(hid, classes, width)
    shard = dot(weight_first[...].astype(bf16), lift)
    shard += dot_tn(weight_head[...].astype(bf16), placement_rows(classes, hid, width))
    first_all[own_units, :] = shard.astype(bf16)
    half = unit
    row, col = iota((half, LANES), 0), iota((half, LANES), 1)
    block = dot(weight_stack[0].astype(bf16), jnp.where(row == col, 1.0, 0.0).astype(bf16))
    block += dot(weight_stack[1].astype(bf16), jnp.where(row + half == col, 1.0, 0.0).astype(bf16))
    stack_all[core, z, chip] = block.astype(bf16)
    valid_all[s] = jnp.broadcast_to(valid[...].astype(f32), valid_all.shape[1:])

    pl.semaphore_wait(barrier, len(everyone))

    def send(src, dst, ssem, rsem, device):
        copy = pltpu.make_async_remote_copy(
            src_ref=src, dst_ref=dst, send_sem=ssem, recv_sem=rsem, device_id=device, device_id_type=MESH
        )
        copy.start()
        return copy

    first_moves = [
        send(first_all.at[own_units], first_all.at[own_units], first_ssem.at[d], first_rsem.at[d], place(0, d))
        for d in range(1, parts)
    ]
    others = [(k, d) for d in range(parts) for k in range(chips) if (k, d) != (0, 0)]
    mine_block = stack_all.at[core, z, chip]
    block_moves = [
        send(mine_block, mine_block, block_ssem.at[i], block_rsem.at[i], place(2 * k, d))
        for i, (k, d) in enumerate(others)
    ]
    valid_moves = [
        send(valid_all.at[s], valid_all.at[s], valid_ssem.at[k], valid_rsem.at[k], place(k, 0))
        for k in range(1, seeds_axis)
    ]

    mask_four[...] = window_mask(LANES * r3, r3)
    mask_eight[...] = window_mask(LANES * r2, r2)
    mean_one[...] = jnp.zeros_like(mean_one)
    for copy in started:
        copy.wait()

    counts_a, degree_a = slot_counts(links_a_lead[...], 0, r3)
    counts_b, degree_b = slot_counts(links_b_lead[...], 0, r2)
    counts_c, degree_c = slot_counts(links_third[...], 0, r1)
    lead = [*counts_a, degree_a, *counts_b, degree_b, *counts_c, degree_c]
    lead += [labels[...].astype(f32), valid[...].astype(f32)]
    packed = jnp.zeros((32, LANES), f32)
    for k, line in enumerate(lead):
        packed = jnp.where(iota((32, LANES), 0) == k, line, packed)
    source, target = iota((LANES, LANES), 0), iota((LANES, LANES), 1)
    mine = jnp.where((source == target + z * q0) & (target < q0), 1.0, 0.0).astype(bf16)
    packed = dot(packed.astype(bf16), mine)
    take = [packed[k : k + 1] for k in range(len(lead))]
    counts_a, degree_a = take[:r3], jnp.maximum(take[r3], 1.0)
    take = take[r3 + 1 :]
    counts_b, degree_b = take[:r2], jnp.maximum(take[r2], 1.0)
    take = take[r2 + 1 :]
    counts_c, degree_c = take[:r1], jnp.maximum(take[r1], 1.0)
    label, present = take[r1 + 1], take[r1 + 2]
    own_rows[:, pl.ds(q2 + q1, LANES)] = dot(own_lead[...], mine).astype(bf16)

    counts, degree = slot_counts(links_a[:, pl.ds(0, q2)], z * q2, r3)
    for t in range(q2 // LANES):
        stripe_rows[t] = stripes([c[:, t * LANES : (t + 1) * LANES] for c in counts])
    degree_rows[:, pl.ds(0, q2)] = degree
    counts, degree = slot_counts(links_a[:, pl.ds(q2, q1)], z * q1, r3)
    for t in range(q1 // LANES):
        stripe_rows[q2 // LANES + t] = stripes([c[:, t * LANES : (t + 1) * LANES] for c in counts])
    degree_rows[:, pl.ds(q2, q1)] = degree
    stripe_rows[two // LANES - 1] = stripes(counts_a)
    degree_rows[:, pl.ds(q2 + q1, LANES)] = degree_a

    def mean_tiles(tile, tiles):
        for t in range(tiles):
            lanes = pl.ds(pl.multiple_of((tile + t) * LANES, LANES), LANES)
            kids = pl.ds(pl.multiple_of((tile + t) * LANES * r3, LANES), LANES * r3)
            matrix = spread(mask_four[...], stripe_rows[tile + t])
            mean = dot(child_rows[:, kids], matrix) / degree_rows[:, lanes]
            mean_one[0:width, lanes] = mean.astype(bf16)

    def layer_one(tile, tiles):
        lanes = pl.ds(pl.multiple_of(tile * LANES, LANES), LANES * tiles)
        preact = dot(first_all[:, 0:width], own_rows[:, lanes])
        preact += dot(first_all[:, LANES : 2 * LANES], mean_one[:, lanes])
        output, active, slope, scaling = activate(preact)
        hidden_one[:, lanes] = output
        active_one[:, lanes] = active
        slope_one[:, lanes] = slope
        scale_one[:, lanes] = scaling

    per = 4
    tail = q1 // LANES + 1
    lax.fori_loop(0, q2 // LANES // per, lambda i, c: (mean_tiles(i * per, per), c)[1], 0)
    mean_tiles(q2 // LANES, tail)

    counts, degree_t = slot_counts(links_b[...], z * q1, r2)
    for t in range(q1 // LANES):
        stripe = stripes([c[:, t * LANES : (t + 1) * LANES] for c in counts])
        spread_two[pl.ds(t * LANES * r2, LANES * r2), :] = spread(mask_eight[...], stripe)
    spread_lead = spread(mask_eight[0 : q0 * r2, :], stripes(counts_b))
    spread_three = spread(mask_eight[0 : q0 * r1, :], stripes(counts_c))

    for copy in first_moves:
        copy.wait_recv()
    lax.fori_loop(0, q2 // LANES // per, lambda i, c: (layer_one(i * per, per), c)[1], 0)

    for copy in block_moves:
        copy.wait_recv()
    pair = stack_all.at[core]
    pair_move = send(pair, pair, pair_ssem, pair_rsem, (sibling, z))
    layer_one(q2 // LANES, tail)

    joined_two[0:hid, :] = hidden_one[:, pl.ds(q2, q1 + LANES)]
    for t in range(q1 // LANES):
        rows = pl.ds(t * LANES * r2, LANES * r2)
        mean = dot(hidden_one[:, rows], spread_two[rows, :])
        lanes = slice(t * LANES, (t + 1) * LANES)
        joined_two[hid:, lanes] = (mean / degree_t[:, lanes]).astype(bf16)
    mean = dot(hidden_one[:, pl.ds(q2, q1)], spread_lead)
    joined_two[hid:, pl.ds(q1, LANES)] = (mean / degree_b).astype(bf16)

    pair_move.wait_recv()
    low_half = iota((1, 1, LANES), 2) < half
    for b in range(2):
        for c in range(2):
            left = stack_all[c, 2 * b].astype(f32)
            right = stack_all[c, 2 * b + 1].astype(f32)
            lanes = slice(b * LANES, (b + 1) * LANES)
            swap = lambda v: shift_half(v.reshape(-1, LANES)).reshape(v.shape)
            low_two[:, c, :, lanes] = jnp.where(low_half, left, swap(right)).astype(bf16)
            low_three[:, c, :, lanes] = jnp.where(low_half, swap(left), right).astype(bf16)
    weight_two = low_two[...].reshape(2 * hid, hid)
    weight_three = low_three[...].reshape(2 * hid, hid)

    preact = dot_tn(weight_two, joined_two[...])
    output, active_two, slope_two, scale_two = activate(preact)

    joined_three[0:hid, :] = output[:, q1:]
    mean = dot(output[:, 0:q1], spread_three)
    joined_three[hid:, :] = (mean / degree_c).astype(bf16)
    preact = dot_tn(weight_three, joined_three[...])
    seeds, active_three, slope_three, scale_three = activate(preact)

    head = dot(first_all[...], seat).astype(bf16)
    for copy in valid_moves:
        copy.wait_recv()
    every_valid = jnp.sum(valid_all[...], axis=0)[0:1]
    count = jnp.sum(every_valid, axis=1, keepdims=True)
    count_out[...] = jnp.broadcast_to(count, count_out.shape)
    logits = dot_tn(head, seeds)
    line = iota(logits.shape, 0)
    peak = jnp.max(logits, axis=0, keepdims=True)
    shifted = jnp.exp(logits - peak)
    totals = jnp.sum(shifted, axis=0, keepdims=True)
    hot = jnp.where(line.astype(f32) == label, 1.0, 0.0)
    nll = peak + jnp.log(totals) - jnp.sum(hot * logits, axis=0, keepdims=True)
    loss = jnp.sum(jnp.where(present > 0, nll, 0.0), axis=1, keepdims=True)
    share = present / jnp.maximum(count, 1.0)
    grad_logits = ((shifted / totals - hot) * share).astype(bf16)
    placed = dot(seat, grad_logits).astype(bf16)
    grad_one[...] = dot_nt(seeds, placed)
    grad_out = dot(head, grad_logits)
    free = 2 * LANES - 3
    part_a = loss.astype(bf16).astype(f32)
    part_b = (loss - part_a).astype(bf16).astype(f32)
    part_c = loss - part_a - part_b
    row, col = iota((hid, LANES), 0), iota((hid, LANES), 1) + LANES
    notes = jnp.where(col == free, part_a, jnp.where(col == free + 1, part_b, part_c))
    notes = jnp.where((col >= free) & (lax.rem(row, unit) == 0), notes, 0.0)
    grad_one[:, LANES:] += notes

    grad_pre = activate_back(grad_out, active_three, slope_three, scale_three)
    grad_weight = dot_nt(joined_three[...], grad_pre).astype(bf16).reshape(chips, 2, -1, hid)
    for c in range(2):
        core_send[1, c] = grad_weight[:, c]
    core_moves = [
        send(core_send.at[1, 1 - core], core_recv.at[1], core_ssem.at[1], core_rsem.at[1], (sibling, z))
    ]
    grad_joined = dot(weight_three, grad_pre)
    grad_mean = (grad_joined[hid:] / degree_c).astype(bf16)
    grad_out = jnp.concatenate([dot_nt(grad_mean, spread_three), grad_joined[0:hid]], axis=1)

    grad_pre = activate_back(grad_out, active_two, slope_two, scale_two)
    grad_weight = dot_nt(joined_two[...], grad_pre).astype(bf16).reshape(chips, 2, -1, hid)
    for c in range(2):
        core_send[0, c] = grad_weight[:, c]
    core_moves += [
        send(core_send.at[0, 1 - core], core_recv.at[0], core_ssem.at[0], core_rsem.at[0], (sibling, z))
    ]
    grad_joined = dot(weight_two, grad_pre)
    grad_mean = (grad_joined[hid:, 0:q1] / degree_t).astype(bf16)
    lead_mean = (grad_joined[hid:, q1:] / degree_b).astype(bf16)

    def back_one(tile, grad_out):
        lanes = pl.ds(tile, grad_out.shape[1])
        pre_one[:, lanes] = activate_back(
            grad_out, active_one[:, lanes], slope_one[:, lanes], scale_one[:, lanes]
        )

    def back_piece(i):
        tile = i * per * LANES
        group = tile // (LANES * r2) * LANES
        back_one(tile, dot_nt(grad_mean[:, group : group + LANES], spread_two[pl.ds(tile, per * LANES), :]))

    own = grad_joined[0:hid]
    back_one(q2, own[:, 0:q1] + dot_nt(lead_mean, spread_lead))
    back_one(q2 + q1, own[:, q1:])
    pieces = q2 // LANES // per
    for i in range(pieces // 2):
        back_piece(i)

    for copy in core_moves:
        copy.wait_recv()
    sums = [core_send[l, core].astype(f32) + core_recv[l].astype(f32) for l in range(2)]
    low_half = iota((1, LANES), 1) < half
    for b in range(2):
        lanes = slice(b * LANES, (b + 1) * LANES)
        left, right = [v[:, :, lanes].reshape(-1, LANES) for v in sums]
        shape = stack_send.shape[1:]
        stack_send[2 * b] = jnp.where(low_half, left, shift_half(right)).astype(bf16).reshape(shape)
        stack_send[2 * b + 1] = jnp.where(low_half, shift_half(left), right).astype(bf16).reshape(shape)
    back_moves = [
        send(
            stack_send.at[lax.rem(z + d, parts), lax.rem(chip + k, chips)], stack_recv.at[i],
            back_ssem.at[i], back_rsem.at[i], place(2 * k, d),
        )
        for i, (k, d) in enumerate(others)
    ]

    for i in range(pieces // 2, pieces):
        back_piece(i)
    grad_one[:, 0:width] += dot_nt(pre_one[...], own_rows[...])
    grad_one[:, LANES : LANES + width] += dot_nt(pre_one[...], mean_one[0:width, :])
    first_send[...] = grad_one[...].astype(bf16)

    group = 2 * unit // 16

    def piece(owner, part):
        slot = lax.rem(owner, group)
        rows = pl.ds(pl.multiple_of(part * unit + slot // 2 * 16, 16), 16)
        return rows, pl.ds(pl.multiple_of(lax.rem(slot, 2) * LANES, LANES), LANES)

    piece_moves = []
    for i, (k, d) in enumerate(everyone):
        owner, part = place(k, d)
        rows, lanes = piece(owner, part)
        piece_moves.append(
            send(first_send.at[rows, lanes], first_recv.at[i], piece_ssem.at[i], piece_rsem.at[i], (owner, part))
        )

    for copy in back_moves:
        copy.wait_recv()
    total = stack_send[z, chip].astype(f32)
    for i in range(len(others)):
        total += stack_recv[i].astype(f32)
    stack_out[...] = total

    for copy in piece_moves:
        copy.wait_recv()
    rows, lanes = piece(s, z)
    total = first_send[rows, lanes].astype(f32)
    for i in range(len(everyone)):
        total += first_recv[i].astype(f32)
    rows, lanes = piece(s, 0)
    first_piece[rows, lanes] = total
    held = first_piece.at[rows, lanes]
    base = s // group * group
    share_moves = []
    for k in range(1, group):
        friend = base + lax.rem(s + k, group)
        share_moves.append(send(held, held, share_ssem.at[k], share_rsem.at[k], (friend, z)))
    for copy in share_moves:
        copy.wait_recv()
    first_out[...] = first_piece[...]

    moves = first_moves + block_moves + valid_moves + [pair_move] + core_moves
    for copy in moves + back_moves + piece_moves + share_moves:
        copy.wait_send()


def step(sizes, *operands):
    n3, n2, n1, n0, parts, seeds_axis, width, classes = sizes
    q2, q1 = n2 // parts, n1 // parts
    r3, r2 = n3 // n2, n2 // n1
    two = q2 + q1 + LANES
    hid = 256
    unit = hid // parts
    chips = seeds_axis // 2
    rows = 2 * hid // seeds_axis
    slots, slots_b = operands[1].shape[0], operands[2].shape[0]
    everyone, others = seeds_axis * parts - 1, chips * parts - 1
    group = 2 * unit // 16
    hbm, vmem = pl.BlockSpec(memory_space=pl.ANY), pl.BlockSpec(memory_space=pltpu.VMEM)
    shape = jax.ShapeDtypeStruct
    dma = pltpu.SemaphoreType.DMA
    return pl.pallas_call(
        functools.partial(step_kernel, sizes),
        out_shape=(shape((unit, hid), f32), shape((rows, LANES), f32), shape((8, LANES), f32)),
        in_specs=[hbm] * 3 + [vmem] * 6,
        out_specs=(vmem,) * 3,
        scratch_shapes=[
            pltpu.VMEM((width, two), bf16),
            pltpu.VMEM((width, two * r3), bf16),
            pltpu.VMEM((width, LANES), bf16),
            pltpu.VMEM((slots, q2 + q1), i32),
            pltpu.VMEM((slots_b, q1), i32),
            pltpu.VMEM((slots, LANES), i32),
            pltpu.VMEM((slots_b, LANES), i32),
            pltpu.VMEM((LANES, two), bf16),
            pltpu.VMEM((hid, two), bf16),
            pltpu.VMEM((hid, two), f32),
            pltpu.VMEM((hid, two), f32),
            pltpu.VMEM((1, two), f32),
            pltpu.VMEM((1, two), f32),
            pltpu.VMEM((two // LANES, 8, LANES), f32),
            pltpu.VMEM((2 * hid, q1 + LANES), bf16),
            pltpu.VMEM((2 * hid, LANES), bf16),
            pltpu.VMEM((q2, LANES), bf16),
            pltpu.VMEM((LANES * r3, LANES), f32),
            pltpu.VMEM((LANES * r2, LANES), f32),
            pltpu.VMEM((hid, two), bf16),
            pltpu.VMEM((hid, hid), bf16),
            pltpu.VMEM((2, parts, chips, rows, LANES), bf16),
            pltpu.VMEM((seeds_axis, 8, LANES), f32),
            pltpu.VMEM((chips, 2, rows, hid), bf16),
            pltpu.VMEM((chips, 2, rows, hid), bf16),
            pltpu.VMEM((2, 2, chips, rows, hid), bf16),
            pltpu.VMEM((2, chips, rows, hid), bf16),
            pltpu.VMEM((parts, chips, rows, LANES), bf16),
            pltpu.VMEM((others, rows, LANES), bf16),
            pltpu.VMEM((hid, hid), f32),
            pltpu.VMEM((hid, hid), bf16),
            pltpu.VMEM((everyone, 16, LANES), bf16),
            pltpu.VMEM((unit, hid), f32),
            dma((11,)),
            dma((parts,)), dma((parts,)),
            dma((others,)), dma((others,)),
            dma(()), dma(()),
            dma((seeds_axis,)), dma((seeds_axis,)),
            dma((2,)), dma((2,)),
            dma((others,)), dma((others,)),
            dma((everyone,)), dma((everyone,)),
            dma((group,)), dma((group,)),
        ],
        compiler_params=pltpu.CompilerParams(
            vmem_limit_bytes=56 * 2**20, collective_id=0, has_side_effects=True
        ),
    )(*operands)


def adamw(weight, moment, square, grad):
    new_moment = beta_first * moment + (1.0 - beta_first) * grad
    new_square = beta_second * square + (1.0 - beta_second) * grad * grad
    moment_hat = new_moment / (1.0 - beta_first**STEP)
    square_hat = new_square / (1.0 - beta_second**STEP)
    new_weight = weight - learn_rate * (
        moment_hat / (jnp.sqrt(square_hat) + epsilon_adam) + decay_rate * weight
    )
    return (new_moment, new_square, new_weight)


def update_kernel(
    width, classes,
    grad_first, grad_stack, count,
    w_a, m_a, s_a, w_b, m_b, s_b, w_c, m_c, s_c,
    loss_out, count_out, om_a, os_a, ow_a, om_b, os_b, ow_b, om_c, os_c, ow_c,
):
    def put(refs, where, values):
        for ref, value in zip(refs, values):
            ref[where] = value

    half = LANES // 2
    for l in range(2):
        grad = grad_stack[:, l * half : (l + 1) * half]
        put((om_b, os_b, ow_b), l, adamw(w_b[l], m_b[l], s_b[l], grad))
    for part in range(2):
        grad = grad_first[:, part * LANES : part * LANES + width]
        lanes = (slice(None), slice(part * width, (part + 1) * width))
        put((om_a, os_a, ow_a), lanes, adamw(w_a[lanes], m_a[lanes], s_a[lanes], grad))
    gap = LANES - width
    flipped = grad_first[...].T
    for start, stop, place in ((0, gap, width), (gap, classes, LANES + width)):
        rows = (slice(start, stop), slice(None))
        grad = flipped[place : place + stop - start]
        put((om_c, os_c, ow_c), rows, adamw(w_c[rows], m_c[rows], s_c[rows], grad))
    free = grad_first.shape[1] - 3
    loss_out[...] = jnp.sum(grad_first[0:1, free:], axis=1, keepdims=True)
    count_out[...] = count[0:1, 0:1]


def update(width, classes, *operands):
    vmem = pl.BlockSpec(memory_space=pltpu.VMEM)
    shape = jax.ShapeDtypeStruct
    outs = [shape((1, 1), f32)] * 2 + [shape(v.shape, f32) for v in operands[3:]]
    return pl.pallas_call(
        functools.partial(update_kernel, width, classes),
        out_shape=tuple(outs),
        in_specs=[vmem] * len(operands),
        out_specs=(vmem,) * len(outs),
    )(*operands)


def per_device(
    features,
    links_first,
    links_second,
    links_third,
    labels,
    valid,
    weight_first,
    moment_first,
    square_first,
    weight_stack,
    moment_stack,
    square_stack,
    weight_head,
    moment_head,
    square_head,
):
    width, classes = features.shape[1], weight_head.shape[1]
    sizes = (
        features.shape[0], links_first.shape[0], links_second.shape[0], links_third.shape[0],
        lax.axis_size("hid"), lax.axis_size("seed"), width, classes,
    )
    grad_first, grad_stack, count = step(
        sizes,
        features.T, links_first.T, links_second.T, links_third.T,
        labels.reshape(1, -1), valid.reshape(1, -1), weight_first.T, weight_stack, weight_head.T,
    )
    loss_sum, count, m_a, s_a, w_a, m_b, s_b, w_b, m_c, s_c, w_c = update(
        width, classes, grad_first, grad_stack, count,
        weight_first.T, moment_first.T, square_first.T,
        weight_stack, moment_stack, square_stack,
        weight_head.T, moment_head.T, square_head.T,
    )
    return (
        loss_sum.reshape(()), count.reshape(()),
        m_a.T, s_a.T, w_a.T,
        m_b, s_b, w_b,
        m_c.T, s_c.T, w_c.T,
    )


def solution(mesh):
    placed = (
        P("seed", None),
        P("seed", None),
        P("seed", None),
        P("seed", None),
        P("seed"),
        P("seed"),
        P(None, "hid"),
        P(None, "hid"),
        P(None, "hid"),
        P(None, "seed", "hid"),
        P(None, "seed", "hid"),
        P(None, "seed", "hid"),
        P("hid", None),
        P("hid", None),
        P("hid", None),
    )
    return jax.shard_map(
        per_device,
        mesh=mesh,
        in_specs=placed,
        out_specs=(P(), P()) + placed[6:],
        check_vma=False,
    )
```

time: 236 us -> 41.6 us (0.18)
  blocking collectives: 106 us -> 0 us
  waiting for transfers between devices: 83.2 us -> 0 us
  Pallas kernels: 12.6 us -> 40.8 us
  local copies, waits for them, and re-layouts: 13.5 us -> 0 us
  between operations: 14 us -> 0.65 us
  other arithmetic: 6.54 us -> 0 us
    all_gather x4 -> x0, blocking collectives: 54.4 us -> none  [the longest x1 16.4 us: per_device(): stack_low = lax.all_gather(stack_low, 'hid', axis=2, tiled=True)]
    psum x2 -> x0, blocking collectives: 51.1 us -> none  [the longest x1 38.7 us: per_device(): loss_sum = lax.psum(loss[0, 0], ('seed', 'hid'))]
    reduce_scatter x2 -> x0, waiting for transfers between devices: 50.9 us -> none  [the longest x1 32 us: per_device(): lax.psum_scatter(grad_stack, 'seed', scatter_dimension=1, tiled=True)]
    pallas_call x1 -> x2, Pallas kernels: 12.6 us -> 40.8 us  [the longest x1 38.7 us: step(): pl.pallas_call(functools.partial(step_kernel, sizes), out_shape=(shape((u...]
    unnamed x5 -> x0, waiting for transfers between devices: 19.3 us -> none
    psum x1 -> x0, waiting for transfers between devices: 12.9 us -> none  [per_device(): grad_first = lax.psum(grad_first, 'seed')]
    unnamed x34 -> x0, local copies, waits for them, and re-layouts: 8.82 us -> none
    slice x5 -> x0, local copies, waits for them, and re-layouts: 4.37 us -> none  [the longest x1 1.2 us: per_device(): loss_sum = lax.psum(loss[0, 0], ('seed', 'hid'))]
  transfers between devices with their start and end apart: 4 -> 0, of which waited for: 4 -> 0; matrix products, arithmetic and copies ran while one was open for 4% -> 0% of each run, Pallas kernels for 0% -> 0%
where the time goes in v2:
time: 41.6 us; the launch traced here: 41.4 us
  Pallas kernels  40.8 us (98%)
  between operations  0.65 us (2%)
    pallas_call x1, Pallas kernels, step(): pl.pallas_call(functools.partial(step_kernel, sizes), out_shape=(shape((u...  38.7 us
    pallas_call x1, Pallas kernels, update(): pl.pallas_call(functools.partial(update_kernel, width, classes), out_shap...  2.02 us

profile of v2, /device:TPU:0, one launch (start us, length us, event | category | flops | bytes accessed | tf_op | source)
XLA Modules:
  0.0 41.4 jit_solution(14141293938619430572)
XLA Ops:
  0.6 38.7 %shard_map.230 = (f32[64,256]{1,0:T(8,128)}, f32[64,128]{1,0:T(8,128)}, f32[8,128]{1,0:T(8,128)}) custom-call(bf16[100,32768]{1,0:T(8,128)(2,1)} %bitcast.20, s32[10,8192]{1,0:T(8,128)} %bitcast.21, s32[10,1024]{1,0:T(8,128)} %bitcast.26, s32[25,128]{1,0:T(8,128)} %bitcast.31, s32[1,128]{1,0:T(1,128)} %bitcast.32, s32[1,128]{1,0:T(1,128)} %bitcast.33, ...), custom_call_target="tpu_custom_call" | custom-call | tf_op jit(solution)/shard_map/pallas_call | solution.py:460
  39.4 2.0 %shard_map.231 = (f32[1,1]{1,0:T(1,128)}, f32[1,1]{1,0:T(1,128)}, f32[64,200]{1,0:T(8,128)}, f32[64,200]{1,0:T(8,128)}, f32[64,200]{1,0:T(8,128)}, /*index=5*/f3...) custom-call(f32[64,256]{1,0:T(8,128)} %get-tuple-element.25.grad_fir, ...), custom_call_target="tpu_custom_call" | custom-call | tf_op jit(solution)/shard_map/pallas_call | solution.py:559

commit v3 on v2

--- a/solution.py
+++ b/solution.py
@@ -111,10 +111,11 @@
     own_rows, child_rows, own_lead, links_a, links_b, links_a_lead, links_b_lead,
     mean_one, hidden_one, active_one, slope_one, scale_one, degree_rows, stripe_rows,
     joined_two, joined_three, spread_two, mask_four, mask_eight, pre_one,
-    first_all, stack_all, valid_all, low_two, low_three,
-    core_send, core_recv, stack_send, stack_recv, grad_one, first_send, first_recv, first_piece,
-    local_sems, first_ssem, first_rsem, block_ssem, block_rsem, pair_ssem, pair_rsem, valid_ssem, valid_rsem,
-    core_ssem, core_rsem, back_ssem, back_rsem, piece_ssem, piece_rsem, share_ssem, share_rsem,
+    first_all, stack_all, valid_all, low_stack,
+    core_send, core_recv, plane_send, plane_recv, turn_send, turn_recv,
+    grad_one, first_send, first_recv, first_piece, first_own, stack_own, head_own,
+    local_sems, first_sems, block_sems, chips_sems, pair_sems, valid_sems,
+    core_sems, plane_sems, turn_sems, piece_sems, share_sems,
 ):
     n3, n2, n1, n0, parts, seeds_axis, width, classes = sizes
     q2, q1, q0 = n2 // parts, n1 // parts, n0 // parts
@@ -128,18 +129,22 @@
     unit = hid // parts
     own_units = pl.ds(pl.multiple_of(z * unit, unit), unit)
     everyone = [(k, d) for d in range(parts) for k in range(seeds_axis) if (k, d) != (0, 0)]
+    near = [(k, d) for k, d in everyone if k == 0 or d == 0]
 
     def place(k, d):
         return (lax.rem(s + k, seeds_axis), lax.rem(z + d, parts))
 
     barrier = pltpu.get_barrier_semaphore()
-    for k, d in everyone:
+    for k, d in near:
         pl.semaphore_signal(barrier, inc=1, device_id=place(k, d), device_id_type=MESH)
 
     def at(size):
         return pl.ds(pl.multiple_of(z * size, LANES), size)
 
     copies = [
+        (weight_stack, stack_own),
+        (weight_first, first_own),
+        (weight_head, head_own),
         (links_first.at[:, at(q2)], links_a.at[:, pl.ds(0, q2)]),
         (links_first.at[:, at(q1)], links_a.at[:, pl.ds(q2, q1)]),
         (links_first.at[:, pl.ds(0, LANES)], links_a_lead),
@@ -159,48 +164,70 @@
     for copy in started:
         copy.start()
 
+    for copy in started[:3]:
+        copy.wait()
+    half = unit
+    depth = stack_own.shape[1]
+    short = depth // 2
+    row, col = iota((half, LANES), 0), iota((half, LANES), 1)
+    to_left = jnp.where(row == col, 1.0, 0.0).astype(bf16)
+    to_right = jnp.where(row + half == col, 1.0, 0.0).astype(bf16)
+    for l in range(2):
+        block = dot(stack_own[l, 0:short].astype(bf16), to_left)
+        block += dot(stack_own[l, short:].astype(bf16), to_right)
+        stack_all[l, core, z, chip] = block.astype(bf16)
     row, col = iota((2 * width, hid), 0), iota((2 * width, hid), 1)
     columns = jnp.where(row < width, row, row - width + LANES)
     lift = jnp.where(columns == col, 1.0, 0.0).astype(bf16)
     seat = placement(hid, classes, width)
-    shard = dot(weight_first[...].astype(bf16), lift)
-    shard += dot_tn(weight_head[...].astype(bf16), placement_rows(classes, hid, width))
+    shard = dot(first_own[...].astype(bf16), lift)
+    shard += dot_tn(head_own[...].astype(bf16), placement_rows(classes, hid, width))
     first_all[own_units, :] = shard.astype(bf16)
-    half = unit
-    row, col = iota((half, LANES), 0), iota((half, LANES), 1)
-    block = dot(weight_stack[0].astype(bf16), jnp.where(row == col, 1.0, 0.0).astype(bf16))
-    block += dot(weight_stack[1].astype(bf16), jnp.where(row + half == col, 1.0, 0.0).astype(bf16))
-    stack_all[core, z, chip] = block.astype(bf16)
     valid_all[s] = jnp.broadcast_to(valid[...].astype(f32), valid_all.shape[1:])
 
-    pl.semaphore_wait(barrier, len(everyone))
-
-    def send(src, dst, ssem, rsem, device):
+    pl.semaphore_wait(barrier, len(near))
+
+    moves = []
+
+    def send(src, dst, sems, where, device):
         copy = pltpu.make_async_remote_copy(
-            src_ref=src, dst_ref=dst, send_sem=ssem, recv_sem=rsem, device_id=device, device_id_type=MESH
+            src_ref=src, dst_ref=dst, send_sem=sems.at[(0, *where)], recv_sem=sems.at[(1, *where)],
+            device_id=device, device_id_type=MESH,
         )
         copy.start()
+        moves.append(copy)
         return copy
 
+    def arrive(copies):
+        for copy in copies:
+            copy.wait_recv()
+
+    def send_blocks(l):
+        mine = stack_all.at[l, core, z, chip]
+        return [send(mine, mine, block_sems, (l, d), place(0, d)) for d in range(1, parts)]
+
+    def send_chips(l):
+        mine = stack_all.at[l, core, :, chip]
+        return [send(mine, mine, chips_sems, (l, k), place(2 * k, 0)) for k in range(1, chips)]
+
+    def send_pair(l):
+        mine = stack_all.at[l, core]
+        return [send(mine, mine, pair_sems, (l,), (sibling, z))]
+
+    block_moves = [send_blocks(0)]
     first_moves = [
-        send(first_all.at[own_units], first_all.at[own_units], first_ssem.at[d], first_rsem.at[d], place(0, d))
+        send(first_all.at[own_units], first_all.at[own_units], first_sems, (d,), place(0, d))
         for d in range(1, parts)
     ]
-    others = [(k, d) for d in range(parts) for k in range(chips) if (k, d) != (0, 0)]
-    mine_block = stack_all.at[core, z, chip]
-    block_moves = [
-        send(mine_block, mine_block, block_ssem.at[i], block_rsem.at[i], place(2 * k, d))
-        for i, (k, d) in enumerate(others)
-    ]
+    block_moves += [send_blocks(1)]
     valid_moves = [
-        send(valid_all.at[s], valid_all.at[s], valid_ssem.at[k], valid_rsem.at[k], place(k, 0))
-        for k in range(1, seeds_axis)
+        send(valid_all.at[s], valid_all.at[s], valid_sems, (k,), place(k, 0)) for k in range(1, seeds_axis)
     ]
 
     mask_four[...] = window_mask(LANES * r3, r3)
     mask_eight[...] = window_mask(LANES * r2, r2)
     mean_one[...] = jnp.zeros_like(mean_one)
-    for copy in started:
+    for copy in started[3:]:
         copy.wait()
 
     counts_a, degree_a = slot_counts(links_a_lead[...], 0, r3)
@@ -264,15 +291,15 @@
     spread_lead = spread(mask_eight[0 : q0 * r2, :], stripes(counts_b))
     spread_three = spread(mask_eight[0 : q0 * r1, :], stripes(counts_c))
 
-    for copy in first_moves:
-        copy.wait_recv()
+    arrive(block_moves[0])
+    chips_moves = [send_chips(0)]
+    arrive(first_moves)
+    arrive(block_moves[1])
+    chips_moves += [send_chips(1)]
     lax.fori_loop(0, q2 // LANES // per, lambda i, c: (layer_one(i * per, per), c)[1], 0)
-
-    for copy in block_moves:
-        copy.wait_recv()
-    pair = stack_all.at[core]
-    pair_move = send(pair, pair, pair_ssem, pair_rsem, (sibling, z))
     layer_one(q2 // LANES, tail)
+    arrive(chips_moves[0])
+    pair_moves = [send_pair(0)]
 
     joined_two[0:hid, :] = hidden_one[:, pl.ds(q2, q1 + LANES)]
     for t in range(q1 // LANES):
@@ -283,31 +310,39 @@
     mean = dot(hidden_one[:, pl.ds(q2, q1)], spread_lead)
     joined_two[hid:, pl.ds(q1, LANES)] = (mean / degree_b).astype(bf16)
 
-    pair_move.wait_recv()
-    low_half = iota((1, 1, LANES), 2) < half
-    for b in range(2):
-        for c in range(2):
-            left = stack_all[c, 2 * b].astype(f32)
-            right = stack_all[c, 2 * b + 1].astype(f32)
-            lanes = slice(b * LANES, (b + 1) * LANES)
-            swap = lambda v: shift_half(v.reshape(-1, LANES)).reshape(v.shape)
-            low_two[:, c, :, lanes] = jnp.where(low_half, left, swap(right)).astype(bf16)
-            low_three[:, c, :, lanes] = jnp.where(low_half, swap(left), right).astype(bf16)
-    weight_two = low_two[...].reshape(2 * hid, hid)
-    weight_three = low_three[...].reshape(2 * hid, hid)
-
+    low_half = iota((1, LANES), 1) < half
+
+    def interleave(left, right):
+        return jnp.where(low_half, left, shift_half(right)), jnp.where(low_half, shift_half(left), right)
+
+    def gathered(l):
+        for b in range(parts // 2):
+            for c in range(2):
+                left = stack_all[l, c, 2 * b].astype(f32).reshape(-1, LANES)
+                right = stack_all[l, c, 2 * b + 1].astype(f32).reshape(-1, LANES)
+                for h, value in enumerate(interleave(left, right)):
+                    lanes = slice(b * LANES, (b + 1) * LANES)
+                    low_stack[l, :, c, h, :, lanes] = value.astype(bf16).reshape(chips, short, LANES)
+        return low_stack[l].reshape(2 * hid, hid)
+
+    arrive(pair_moves[0])
+    weight_two = gathered(0)
     preact = dot_tn(weight_two, joined_two[...])
     output, active_two, slope_two, scale_two = activate(preact)
+
+    arrive(chips_moves[1])
+    pair_moves += [send_pair(1)]
 
     joined_three[0:hid, :] = output[:, q1:]
     mean = dot(output[:, 0:q1], spread_three)
     joined_three[hid:, :] = (mean / degree_c).astype(bf16)
+    arrive(pair_moves[1])
+    weight_three = gathered(1)
     preact = dot_tn(weight_three, joined_three[...])
     seeds, active_three, slope_three, scale_three = activate(preact)
 
     head = dot(first_all[...], seat).astype(bf16)
-    for copy in valid_moves:
-        copy.wait_recv()
+    arrive(valid_moves)
     every_valid = jnp.sum(valid_all[...], axis=0)[0:1]
     count = jnp.sum(every_valid, axis=1, keepdims=True)
     count_out[...] = jnp.broadcast_to(count, count_out.shape)
@@ -333,27 +368,53 @@
     notes = jnp.where((col >= free) & (lax.rem(row, unit) == 0), notes, 0.0)
     grad_one[:, LANES:] += notes
 
+    def keep_grad(l, value):
+        value = value.astype(bf16).reshape(chips, 2, depth, hid)
+        for c in range(2):
+            core_send[l, c] = value[:, c]
+
+    def send_core(l):
+        return [send(core_send.at[l, 1 - core], core_recv.at[l], core_sems, (l,), (sibling, z))]
+
+    def send_plane(l):
+        plane_send[l] = (core_send[l, core].astype(f32) + core_recv[l].astype(f32)).astype(bf16)
+        return [
+            send(plane_send.at[l, lax.rem(chip + k, chips)], plane_recv.at[l, k], plane_sems, (l, k), place(2 * k, 0))
+            for k in range(1, chips)
+        ]
+
+    def send_turn(l):
+        total = plane_send[l, chip].astype(f32)
+        for k in range(1, chips):
+            total += plane_recv[l, k].astype(f32)
+        for b in range(parts // 2):
+            lanes = slice(b * LANES, (b + 1) * LANES)
+            for h, value in enumerate(interleave(total[0:short, lanes], total[short:, lanes])):
+                turn_send[l, 2 * b + h] = value.astype(bf16)
+        return [
+            send(turn_send.at[l, lax.rem(z + d, parts)], turn_recv.at[l, d], turn_sems, (l, d), place(0, d))
+            for d in range(1, parts)
+        ]
+
+    def finish_stack(l):
+        total = turn_send[l, z].astype(f32)
+        for d in range(1, parts):
+            total += turn_recv[l, d].astype(f32)
+        stack_out[l] = total
+
     grad_pre = activate_back(grad_out, active_three, slope_three, scale_three)
-    grad_weight = dot_nt(joined_three[...], grad_pre).astype(bf16).reshape(chips, 2, -1, hid)
-    for c in range(2):
-        core_send[1, c] = grad_weight[:, c]
-    core_moves = [
-        send(core_send.at[1, 1 - core], core_recv.at[1], core_ssem.at[1], core_rsem.at[1], (sibling, z))
-    ]
+    keep_grad(1, dot_nt(joined_three[...], grad_pre))
     grad_joined = dot(weight_three, grad_pre)
     grad_mean = (grad_joined[hid:] / degree_c).astype(bf16)
     grad_out = jnp.concatenate([dot_nt(grad_mean, spread_three), grad_joined[0:hid]], axis=1)
+    core_moves = [None, send_core(1)]
 
     grad_pre = activate_back(grad_out, active_two, slope_two, scale_two)
-    grad_weight = dot_nt(joined_two[...], grad_pre).astype(bf16).reshape(chips, 2, -1, hid)
-    for c in range(2):
-        core_send[0, c] = grad_weight[:, c]
-    core_moves += [
-        send(core_send.at[0, 1 - core], core_recv.at[0], core_ssem.at[0], core_rsem.at[0], (sibling, z))
-    ]
+    keep_grad(0, dot_nt(joined_two[...], grad_pre))
     grad_joined = dot(weight_two, grad_pre)
     grad_mean = (grad_joined[hid:, 0:q1] / degree_t).astype(bf16)
     lead_mean = (grad_joined[hid:, q1:] / degree_b).astype(bf16)
+    core_moves[0] = send_core(0)
 
     def back_one(tile, grad_out):
         lanes = pl.ds(tile, grad_out.shape[1])
@@ -369,29 +430,7 @@
     own = grad_joined[0:hid]
     back_one(q2, own[:, 0:q1] + dot_nt(lead_mean, spread_lead))
     back_one(q2 + q1, own[:, q1:])
-    pieces = q2 // LANES // per
-    for i in range(pieces // 2):
-        back_piece(i)
-
-    for copy in core_moves:
-        copy.wait_recv()
-    sums = [core_send[l, core].astype(f32) + core_recv[l].astype(f32) for l in range(2)]
-    low_half = iota((1, LANES), 1) < half
-    for b in range(2):
-        lanes = slice(b * LANES, (b + 1) * LANES)
-        left, right = [v[:, :, lanes].reshape(-1, LANES) for v in sums]
-        shape = stack_send.shape[1:]
-        stack_send[2 * b] = jnp.where(low_half, left, shift_half(right)).astype(bf16).reshape(shape)
-        stack_send[2 * b + 1] = jnp.where(low_half, shift_half(left), right).astype(bf16).reshape(shape)
-    back_moves = [
-        send(
-            stack_send.at[lax.rem(z + d, parts), lax.rem(chip + k, chips)], stack_recv.at[i],
-            back_ssem.at[i], back_rsem.at[i], place(2 * k, d),
-        )
-        for i, (k, d) in enumerate(others)
-    ]
-
-    for i in range(pieces // 2, pieces):
+    for i in range(q2 // LANES // per):
         back_piece(i)
     grad_one[:, 0:width] += dot_nt(pre_one[...], own_rows[...])
     grad_one[:, LANES : LANES + width] += dot_nt(pre_one[...], mean_one[0:width, :])
@@ -409,18 +448,18 @@
         owner, part = place(k, d)
         rows, lanes = piece(owner, part)
         piece_moves.append(
-            send(first_send.at[rows, lanes], first_recv.at[i], piece_ssem.at[i], piece_rsem.at[i], (owner, part))
+            send(first_send.at[rows, lanes], first_recv.at[i], piece_sems, (i,), (owner, part))
         )
 
-    for copy in back_moves:
-        copy.wait_recv()
-    total = stack_send[z, chip].astype(f32)
-    for i in range(len(others)):
-        total += stack_recv[i].astype(f32)
-    stack_out[...] = total
-
-    for copy in piece_moves:
-        copy.wait_recv()
+    plane_moves, turn_moves = [None, None], [None, None]
+    for l in (1, 0):
+        arrive(core_moves[l])
+        plane_moves[l] = send_plane(l)
+    for l in (1, 0):
+        arrive(plane_moves[l])
+        turn_moves[l] = send_turn(l)
+
+    arrive(piece_moves)
     rows, lanes = piece(s, z)
     total = first_send[rows, lanes].astype(f32)
     for i in range(len(everyone)):
@@ -432,13 +471,14 @@
     share_moves = []
     for k in range(1, group):
         friend = base + lax.rem(s + k, group)
-        share_moves.append(send(held, held, share_ssem.at[k], share_rsem.at[k], (friend, z)))
-    for copy in share_moves:
-        copy.wait_recv()
+        share_moves.append(send(held, held, share_sems, (k,), (friend, z)))
+    for l in (1, 0):
+        arrive(turn_moves[l])
+        finish_stack(l)
+    arrive(share_moves)
     first_out[...] = first_piece[...]
 
-    moves = first_moves + block_moves + valid_moves + [pair_move] + core_moves
-    for copy in moves + back_moves + piece_moves + share_moves:
+    for copy in moves:
         copy.wait_send()
 
 
@@ -452,15 +492,16 @@
     chips = seeds_axis // 2
     rows = 2 * hid // seeds_axis
     slots, slots_b = operands[1].shape[0], operands[2].shape[0]
-    everyone, others = seeds_axis * parts - 1, chips * parts - 1
+    everyone = seeds_axis * parts - 1
+    short = rows // 2
     group = 2 * unit // 16
     hbm, vmem = pl.BlockSpec(memory_space=pl.ANY), pl.BlockSpec(memory_space=pltpu.VMEM)
     shape = jax.ShapeDtypeStruct
     dma = pltpu.SemaphoreType.DMA
     return pl.pallas_call(
         functools.partial(step_kernel, sizes),
-        out_shape=(shape((unit, hid), f32), shape((rows, LANES), f32), shape((8, LANES), f32)),
-        in_specs=[hbm] * 3 + [vmem] * 6,
+        out_shape=(shape((unit, hid), f32), shape((2, short, LANES), f32), shape((8, LANES), f32)),
+        in_specs=[hbm] * 3 + [vmem] * 3 + [hbm] * 3,
         out_specs=(vmem,) * 3,
         scratch_shapes=[
             pltpu.VMEM((width, two), bf16),
@@ -484,27 +525,31 @@
             pltpu.VMEM((LANES * r2, LANES), f32),
             pltpu.VMEM((hid, two), bf16),
             pltpu.VMEM((hid, hid), bf16),
-            pltpu.VMEM((2, parts, chips, rows, LANES), bf16),
+            pltpu.VMEM((2, 2, parts, chips, short, LANES), bf16),
             pltpu.VMEM((seeds_axis, 8, LANES), f32),
-            pltpu.VMEM((chips, 2, rows, hid), bf16),
-            pltpu.VMEM((chips, 2, rows, hid), bf16),
+            pltpu.VMEM((2, chips, 2, 2, short, hid), bf16),
             pltpu.VMEM((2, 2, chips, rows, hid), bf16),
             pltpu.VMEM((2, chips, rows, hid), bf16),
-            pltpu.VMEM((parts, chips, rows, LANES), bf16),
-            pltpu.VMEM((others, rows, LANES), bf16),
+            pltpu.VMEM((2, chips, rows, hid), bf16),
+            pltpu.VMEM((2, chips, rows, hid), bf16),
+            pltpu.VMEM((2, parts, short, LANES), bf16),
+            pltpu.VMEM((2, parts, short, LANES), bf16),
             pltpu.VMEM((hid, hid), f32),
             pltpu.VMEM((hid, hid), bf16),
             pltpu.VMEM((everyone, 16, LANES), bf16),
             pltpu.VMEM((unit, hid), f32),
-            dma((11,)),
-            dma((parts,)), dma((parts,)),
-            dma((others,)), dma((others,)),
-            dma(()), dma(()),
-            dma((seeds_axis,)), dma((seeds_axis,)),
-            dma((2,)), dma((2,)),
-            dma((others,)), dma((others,)),
-            dma((everyone,)), dma((everyone,)),
-            dma((group,)), dma((group,)),
+            *[pltpu.VMEM(v.shape, f32) for v in operands[6:]],
+            dma((14,)),
+            dma((2, parts)),
+            dma((2, 2, parts)),
+            dma((2, 2, chips)),
+            dma((2, 2)),
+            dma((2, seeds_axis)),
+            dma((2, 2)),
+            dma((2, 2, chips)),
+            dma((2, 2, parts)),
+            dma((2, everyone)),
+            dma((2, group)),
         ],
         compiler_params=pltpu.CompilerParams(
             vmem_limit_bytes=56 * 2**20, collective_id=0, has_side_effects=True
@@ -534,9 +579,12 @@
             ref[where] = value
 
     half = LANES // 2
+    short = grad_stack.shape[1]
     for l in range(2):
-        grad = grad_stack[:, l * half : (l + 1) * half]
-        put((om_b, os_b, ow_b), l, adamw(w_b[l], m_b[l], s_b[l], grad))
+        for h in range(2):
+            grad = grad_stack[l, :, h * half : (h + 1) * half]
+            rows = (l, slice(h * short, (h + 1) * short))
+            put((om_b, os_b, ow_b), rows, adamw(w_b[rows], m_b[rows], s_b[rows], grad))
     for part in range(2):
         grad = grad_first[:, part * LANES : part * LANES + width]
         lanes = (slice(None), slice(part * width, (part + 1) * width))

time: 41.6 us -> 36.1 us (0.87)
  Pallas kernels: 40.8 us -> 35.2 us
    pallas_call x1, Pallas kernels: 38.7 us -> 33.2 us  [step(): pl.pallas_call(functools.partial(step_kernel, sizes), out_shape=(shape((u...]
where the time goes in v3:
time: 36.1 us; the launch traced here: 35.9 us
  Pallas kernels  35.2 us (98%)
  between operations  0.65 us (2%)
    pallas_call x1, Pallas kernels, step(): pl.pallas_call(functools.partial(step_kernel, sizes), out_shape=(shape((u...  33.2 us
    pallas_call x1, Pallas kernels, update(): pl.pallas_call(functools.partial(update_kernel, width, classes), out_shap...  2.04 us

profile of v3, /device:TPU:0, one launch (start us, length us, event | category | flops | bytes accessed | tf_op | source)
XLA Modules:
  0.0 35.9 jit_solution(2365597415873986579)
XLA Ops:
  0.6 33.2 %shard_map.230 = (f32[64,256]{1,0:T(8,128)}, f32[2,32,128]{2,1,0:T(8,128)}, f32[8,128]{1,0:T(8,128)}) custom-call(bf16[100,32768]{1,0:T(8,128)(2,1)} %bitcast.20, s32[10,8192]{1,0:T(8,128)} %bitcast.21, s32[10,1024]{1,0:T(8,128)} %bitcast.26, s32[25,128]{1,0:T(8,128)} %bitcast.31, s32[1,128]{1,0:T(1,128)} %bitcast.32, s32[1,128]{1,0:T(1,128)} %bitcast.33, ...), custom_call_target="tpu_custom_call" | custom-call | tf_op jit(solution)/shard_map/pallas_call | solution.py:501
  33.8 2.0 %shard_map.231 = (f32[1,1]{1,0:T(1,128)}, f32[1,1]{1,0:T(1,128)}, f32[64,200]{1,0:T(8,128)}, f32[64,200]{1,0:T(8,128)}, f32[64,200]{1,0:T(8,128)}, /*index=5*/f3...) custom-call(f32[64,256]{1,0:T(8,128)} %get-tuple-element.25.grad_fir, ...), custom_call_target="tpu_custom_call" | custom-call | tf_op jit(solution)/shard_map/pallas_call | solution.py:607

commit v4 on v3

--- a/solution.py
+++ b/solution.py
@@ -107,13 +107,14 @@
 def step_kernel(
     sizes,
     features, links_first, links_second, links_third, labels, valid, weight_first, weight_stack, weight_head,
-    first_out, stack_out, count_out,
+    first_out, stack_out,
     own_rows, child_rows, own_lead, links_a, links_b, links_a_lead, links_b_lead,
     mean_one, hidden_one, active_one, slope_one, scale_one, degree_rows, stripe_rows,
     joined_two, joined_three, spread_two, mask_four, mask_eight, pre_one,
     first_all, stack_all, valid_all, low_stack,
     core_send, core_recv, plane_send, plane_recv, turn_send, turn_recv,
     grad_one, first_send, first_recv, first_piece, first_own, stack_own, head_own,
+    links_c, labels_own, valid_own,
     local_sems, first_sems, block_sems, chips_sems, pair_sems, valid_sems,
     core_sems, plane_sems, turn_sems, piece_sems, share_sems,
 ):
@@ -145,6 +146,9 @@
         (weight_stack, stack_own),
         (weight_first, first_own),
         (weight_head, head_own),
+        (valid, valid_own),
+        (labels, labels_own),
+        (links_third, links_c),
         (links_first.at[:, at(q2)], links_a.at[:, pl.ds(0, q2)]),
         (links_first.at[:, at(q1)], links_a.at[:, pl.ds(q2, q1)]),
         (links_first.at[:, pl.ds(0, LANES)], links_a_lead),
@@ -164,7 +168,7 @@
     for copy in started:
         copy.start()
 
-    for copy in started[:3]:
+    for copy in started[:4]:
         copy.wait()
     half = unit
     depth = stack_own.shape[1]
@@ -183,7 +187,7 @@
     shard = dot(first_own[...].astype(bf16), lift)
     shard += dot_tn(head_own[...].astype(bf16), placement_rows(classes, hid, width))
     first_all[own_units, :] = shard.astype(bf16)
-    valid_all[s] = jnp.broadcast_to(valid[...].astype(f32), valid_all.shape[1:])
+    valid_all[s] = jnp.broadcast_to(valid_own[...].astype(f32), valid_all.shape[1:])
 
     pl.semaphore_wait(barrier, len(near))
 
@@ -214,12 +218,11 @@
         mine = stack_all.at[l, core]
         return [send(mine, mine, pair_sems, (l,), (sibling, z))]
 
-    block_moves = [send_blocks(0)]
+    block_moves = [send_blocks(0), send_blocks(1)]
     first_moves = [
         send(first_all.at[own_units], first_all.at[own_units], first_sems, (d,), place(0, d))
         for d in range(1, parts)
     ]
-    block_moves += [send_blocks(1)]
     valid_moves = [
         send(valid_all.at[s], valid_all.at[s], valid_sems, (k,), place(k, 0)) for k in range(1, seeds_axis)
     ]
@@ -227,14 +230,14 @@
     mask_four[...] = window_mask(LANES * r3, r3)
     mask_eight[...] = window_mask(LANES * r2, r2)
     mean_one[...] = jnp.zeros_like(mean_one)
-    for copy in started[3:]:
+    for copy in started[4:]:
         copy.wait()
 
     counts_a, degree_a = slot_counts(links_a_lead[...], 0, r3)
     counts_b, degree_b = slot_counts(links_b_lead[...], 0, r2)
-    counts_c, degree_c = slot_counts(links_third[...], 0, r1)
+    counts_c, degree_c = slot_counts(links_c[...], 0, r1)
     lead = [*counts_a, degree_a, *counts_b, degree_b, *counts_c, degree_c]
-    lead += [labels[...].astype(f32), valid[...].astype(f32)]
+    lead += [labels_own[...].astype(f32), valid_own[...].astype(f32)]
     packed = jnp.zeros((32, LANES), f32)
     for k, line in enumerate(lead):
         packed = jnp.where(iota((32, LANES), 0) == k, line, packed)
@@ -291,11 +294,11 @@
     spread_lead = spread(mask_eight[0 : q0 * r2, :], stripes(counts_b))
     spread_three = spread(mask_eight[0 : q0 * r1, :], stripes(counts_c))
 
-    arrive(block_moves[0])
-    chips_moves = [send_chips(0)]
+    chips_moves = []
+    for l in range(2):
+        arrive(block_moves[l])
+        chips_moves.append(send_chips(l))
     arrive(first_moves)
-    arrive(block_moves[1])
-    chips_moves += [send_chips(1)]
     lax.fori_loop(0, q2 // LANES // per, lambda i, c: (layer_one(i * per, per), c)[1], 0)
     layer_one(q2 // LANES, tail)
     arrive(chips_moves[0])
@@ -345,7 +348,6 @@
     arrive(valid_moves)
     every_valid = jnp.sum(valid_all[...], axis=0)[0:1]
     count = jnp.sum(every_valid, axis=1, keepdims=True)
-    count_out[...] = jnp.broadcast_to(count, count_out.shape)
     logits = dot_tn(head, seeds)
     line = iota(logits.shape, 0)
     peak = jnp.max(logits, axis=0, keepdims=True)
@@ -430,7 +432,13 @@
     own = grad_joined[0:hid]
     back_one(q2, own[:, 0:q1] + dot_nt(lead_mean, spread_lead))
     back_one(q2 + q1, own[:, q1:])
-    for i in range(q2 // LANES // per):
+    plane_moves, turn_moves = [None, None], [None, None]
+    pieces = q2 // LANES // per
+    for i in range(pieces // 2):
+        back_piece(i)
+    arrive(core_moves[1])
+    plane_moves[1] = send_plane(1)
+    for i in range(pieces // 2, pieces):
         back_piece(i)
     grad_one[:, 0:width] += dot_nt(pre_one[...], own_rows[...])
     grad_one[:, LANES : LANES + width] += dot_nt(pre_one[...], mean_one[0:width, :])
@@ -444,17 +452,15 @@
         return rows, pl.ds(pl.multiple_of(lax.rem(slot, 2) * LANES, LANES), LANES)
 
     piece_moves = []
-    for i, (k, d) in enumerate(everyone):
+    for i, (k, d) in reversed(list(enumerate(everyone))):
         owner, part = place(k, d)
         rows, lanes = piece(owner, part)
         piece_moves.append(
             send(first_send.at[rows, lanes], first_recv.at[i], piece_sems, (i,), (owner, part))
         )
 
-    plane_moves, turn_moves = [None, None], [None, None]
-    for l in (1, 0):
-        arrive(core_moves[l])
-        plane_moves[l] = send_plane(l)
+    arrive(core_moves[0])
+    plane_moves[0] = send_plane(0)
     for l in (1, 0):
         arrive(plane_moves[l])
         turn_moves[l] = send_turn(l)
@@ -476,7 +482,9 @@
         arrive(turn_moves[l])
         finish_stack(l)
     arrive(share_moves)
-    first_out[...] = first_piece[...]
+    spare = (iota((unit, LANES), 0) == 0) & (iota((unit, LANES), 1) == LANES - 4)
+    first_out[:, 0 : hid - LANES] = first_piece[:, 0 : hid - LANES]
+    first_out[:, hid - LANES :] = jnp.where(spare, count, first_piece[:, hid - LANES :])
 
     for copy in moves:
         copy.wait_send()
@@ -500,9 +508,9 @@
     dma = pltpu.SemaphoreType.DMA
     return pl.pallas_call(
         functools.partial(step_kernel, sizes),
-        out_shape=(shape((unit, hid), f32), shape((2, short, LANES), f32), shape((8, LANES), f32)),
-        in_specs=[hbm] * 3 + [vmem] * 3 + [hbm] * 3,
-        out_specs=(vmem,) * 3,
+        out_shape=(shape((unit, hid), f32), shape((2, short, LANES), f32)),
+        in_specs=[hbm] * 9,
+        out_specs=(vmem,) * 2,
         scratch_shapes=[
             pltpu.VMEM((width, two), bf16),
             pltpu.VMEM((width, two * r3), bf16),
@@ -539,7 +547,8 @@
             pltpu.VMEM((everyone, 16, LANES), bf16),
             pltpu.VMEM((unit, hid), f32),
             *[pltpu.VMEM(v.shape, f32) for v in operands[6:]],
-            dma((14,)),
+            *[pltpu.VMEM(v.shape, i32) for v in operands[3:6]],
+            dma((17,)),
             dma((2, parts)),
             dma((2, 2, parts)),
             dma((2, 2, chips)),
@@ -570,7 +579,7 @@
 
 def update_kernel(
     width, classes,
-    grad_first, grad_stack, count,
+    grad_first, grad_stack,
     w_a, m_a, s_a, w_b, m_b, s_b, w_c, m_c, s_c,
     loss_out, count_out, om_a, os_a, ow_a, om_b, os_b, ow_b, om_c, os_c, ow_c,
 ):
@@ -597,13 +606,13 @@
         put((om_c, os_c, ow_c), rows, adamw(w_c[rows], m_c[rows], s_c[rows], grad))
     free = grad_first.shape[1] - 3
     loss_out[...] = jnp.sum(grad_first[0:1, free:], axis=1, keepdims=True)
-    count_out[...] = count[0:1, 0:1]
+    count_out[...] = grad_first[0:1, free - 1 : free]
 
 
 def update(width, classes, *operands):
     vmem = pl.BlockSpec(memory_space=pltpu.VMEM)
     shape = jax.ShapeDtypeStruct
-    outs = [shape((1, 1), f32)] * 2 + [shape(v.shape, f32) for v in operands[3:]]
+    outs = [shape((1, 1), f32)] * 2 + [shape(v.shape, f32) for v in operands[2:]]
     return pl.pallas_call(
         functools.partial(update_kernel, width, classes),
         out_shape=tuple(outs),
@@ -634,13 +643,13 @@
         features.shape[0], links_first.shape[0], links_second.shape[0], links_third.shape[0],
         lax.axis_size("hid"), lax.axis_size("seed"), width, classes,
     )
-    grad_first, grad_stack, count = step(
+    grad_first, grad_stack = step(
         sizes,
         features.T, links_first.T, links_second.T, links_third.T,
         labels.reshape(1, -1), valid.reshape(1, -1), weight_first.T, weight_stack, weight_head.T,
     )
     loss_sum, count, m_a, s_a, w_a, m_b, s_b, w_b, m_c, s_c, w_c = update(
-        width, classes, grad_first, grad_stack, count,
+        width, classes, grad_first, grad_stack,
         weight_first.T, moment_first.T, square_first.T,
         weight_stack, moment_stack, square_stack,
         weight_head.T, moment_head.T, square_head.T,

time: 36.1 us -> 34.7 us (0.961)
  Pallas kernels: 35.2 us -> 33.9 us
    pallas_call x1, Pallas kernels: 33.2 us -> 31.9 us  [step(): pl.pallas_call(functools.partial(step_kernel, sizes), out_shape=(shape((u...]
where the time goes in v4:
time: 34.7 us; the launch traced here: 34.5 us
  Pallas kernels  33.9 us (98%)
  between operations  0.65 us (2%)
    pallas_call x1, Pallas kernels, step(): pl.pallas_call(functools.partial(step_kernel, sizes), out_shape=(shape((u...  31.9 us
    pallas_call x1, Pallas kernels, update(): pl.pallas_call(functools.partial(update_kernel, width, classes), out_shap...  2 us

profile of v4, /device:TPU:0, one launch (start us, length us, event | category | flops | bytes accessed | tf_op | source)
XLA Modules:
  0.0 34.5 jit_solution(7783110603053294804)
XLA Ops:
  0.6 31.9 %shard_map.230 = (f32[64,256]{1,0:T(8,128)}, f32[2,32,128]{2,1,0:T(8,128)}) custom-call(bf16[100,32768]{1,0:T(8,128)(2,1)} %bitcast.20, s32[10,8192]{1,0:T(8,128)} %bitcast.21, s32[10,1024]{1,0:T(8,128)} %bitcast.26, s32[25,128]{1,0:T(8,128)} %bitcast.31, s32[1,128]{1,0:T(1,128)} %bitcast.32, s32[1,128]{1,0:T(1,128)} %bitcast.33, f32[64,200]{1,0:T(8,128)} %bitcast.22, ...), custom_call_target="tpu_custom_call" | custom-call | tf_op jit(solution)/shard_map/pallas_call | solution.py:509
  32.5 2.0 %shard_map.231 = (f32[1,1]{1,0:T(1,128)}, f32[1,1]{1,0:T(1,128)}, f32[64,200]{1,0:T(8,128)}, f32[64,200]{1,0:T(8,128)}, f32[64,200]{1,0:T(8,128)}, /*index=5*/f3...) custom-call(f32[64,256]{1,0:T(8,128)} %get-tuple-element.24.grad_fir, ...), custom_call_target="tpu_custom_call" | custom-call | tf_op jit(solution)/shard_map/pallas_call | solution.py:616

commit v5 on v4

--- a/solution.py
+++ b/solution.py
@@ -73,9 +73,9 @@
 
 
 def activate(preact):
-    logistic = 1.0 / (1.0 + jnp.exp(-preact))
+    logistic = 0.5 * jnp.tanh(0.5 * preact) + 0.5
     active = preact * logistic
-    slope = logistic * (1.0 + preact * (1.0 - logistic))
+    slope = logistic + (active - active * logistic)
     scaling = lax.rsqrt(jnp.sum(active * active, axis=0, keepdims=True) + epsilon_norm)
     return (active * scaling).astype(bf16), active, slope, scaling
 
@@ -107,16 +107,16 @@
 def step_kernel(
     sizes,
     features, links_first, links_second, links_third, labels, valid, weight_first, weight_stack, weight_head,
-    first_out, stack_out,
+    first_out, stack_out, count_out,
     own_rows, child_rows, own_lead, links_a, links_b, links_a_lead, links_b_lead,
-    mean_one, hidden_one, active_one, slope_one, scale_one, degree_rows, stripe_rows,
-    joined_two, joined_three, spread_two, mask_four, mask_eight, pre_one,
+    joined_one, hidden_one, active_one, slope_one, scale_one, degree_rows, stripe_rows,
+    joined_two, joined_three, spread_two, mask_four, mask_eight,
     first_all, stack_all, valid_all, low_stack,
-    core_send, core_recv, plane_send, plane_recv, turn_send, turn_recv,
-    grad_one, first_send, first_recv, first_piece, first_own, stack_own, head_own,
+    core_send, core_recv, plane_send, plane_recv, turn_send,
+    grad_one, first_send, half_recv, half_send, part_recv, share, count_own, first_own, stack_own, head_own,
     links_c, labels_own, valid_own,
-    local_sems, first_sems, block_sems, chips_sems, pair_sems, valid_sems,
-    core_sems, plane_sems, turn_sems, piece_sems, share_sems,
+    local_sems, first_sems, block_sems, own_sems, chips_sems, pair_sems, valid_sems,
+    core_sems, plane_sems, turn_sems, half_sems, part_sems, share_sems, out_sems,
 ):
     n3, n2, n1, n0, parts, seeds_axis, width, classes = sizes
     q2, q1, q0 = n2 // parts, n1 // parts, n0 // parts
@@ -129,8 +129,7 @@
     hid = 256
     unit = hid // parts
     own_units = pl.ds(pl.multiple_of(z * unit, unit), unit)
-    everyone = [(k, d) for d in range(parts) for k in range(seeds_axis) if (k, d) != (0, 0)]
-    near = [(k, d) for k, d in everyone if k == 0 or d == 0]
+    near = [(0, d) for d in range(1, parts)] + [(k, 0) for k in range(1, seeds_axis)]
 
     def place(k, d):
         return (lax.rem(s + k, seeds_axis), lax.rem(z + d, parts))
@@ -168,18 +167,55 @@
     for copy in started:
         copy.start()
 
-    for copy in started[:4]:
-        copy.wait()
-    half = unit
+    started[0].wait()
     depth = stack_own.shape[1]
     short = depth // 2
-    row, col = iota((half, LANES), 0), iota((half, LANES), 1)
+    row, col = iota((unit, LANES), 0), iota((unit, LANES), 1)
     to_left = jnp.where(row == col, 1.0, 0.0).astype(bf16)
-    to_right = jnp.where(row + half == col, 1.0, 0.0).astype(bf16)
+    to_right = jnp.where(row + unit == col, 1.0, 0.0).astype(bf16)
     for l in range(2):
         block = dot(stack_own[l, 0:short].astype(bf16), to_left)
         block += dot(stack_own[l, short:].astype(bf16), to_right)
-        stack_all[l, core, z, chip] = block.astype(bf16)
+        stack_all[l, core, 0, chip] = block.astype(bf16)
+    pl.semaphore_wait(barrier, len(near))
+
+    moves = []
+
+    def send(src, dst, sems, where, device):
+        copy = pltpu.make_async_remote_copy(
+            src_ref=src, dst_ref=dst, send_sem=sems.at[(0, *where)], recv_sem=sems.at[(1, *where)],
+            device_id=device, device_id_type=MESH,
+        )
+        copy.start()
+        moves.append(copy)
+        return copy
+
+    def arrive(copies):
+        for copy in copies:
+            copy.wait_recv()
+
+    def send_blocks(l):
+        mine = stack_all.at[l, core, 0, chip]
+        return [
+            send(mine, stack_all.at[l, core, d, chip], block_sems, (l, d), place(0, d)) for d in range(1, parts)
+        ]
+
+    def send_own(l):
+        mine = stack_all.at[l, core, 0, chip]
+        return [send(mine, mine, own_sems, (l, k), place(2 * k, 0)) for k in range(1, chips)]
+
+    def send_chips(l):
+        mine = stack_all.at[l, core, 1:parts, chip]
+        return [send(mine, mine, chips_sems, (l, k), place(2 * k, 0)) for k in range(1, chips)]
+
+    def send_pair(l):
+        mine = stack_all.at[l, core]
+        return [send(mine, mine, pair_sems, (l,), (sibling, z))]
+
+    block_moves = [send_blocks(0), send_blocks(1)]
+    own_moves = [send_own(0), send_own(1)]
+    for copy in started[1:4]:
+        copy.wait()
     row, col = iota((2 * width, hid), 0), iota((2 * width, hid), 1)
     columns = jnp.where(row < width, row, row - width + LANES)
     lift = jnp.where(columns == col, 1.0, 0.0).astype(bf16)
@@ -189,36 +225,6 @@
     first_all[own_units, :] = shard.astype(bf16)
     valid_all[s] = jnp.broadcast_to(valid_own[...].astype(f32), valid_all.shape[1:])
 
-    pl.semaphore_wait(barrier, len(near))
-
-    moves = []
-
-    def send(src, dst, sems, where, device):
-        copy = pltpu.make_async_remote_copy(
-            src_ref=src, dst_ref=dst, send_sem=sems.at[(0, *where)], recv_sem=sems.at[(1, *where)],
-            device_id=device, device_id_type=MESH,
-        )
-        copy.start()
-        moves.append(copy)
-        return copy
-
-    def arrive(copies):
-        for copy in copies:
-            copy.wait_recv()
-
-    def send_blocks(l):
-        mine = stack_all.at[l, core, z, chip]
-        return [send(mine, mine, block_sems, (l, d), place(0, d)) for d in range(1, parts)]
-
-    def send_chips(l):
-        mine = stack_all.at[l, core, :, chip]
-        return [send(mine, mine, chips_sems, (l, k), place(2 * k, 0)) for k in range(1, chips)]
-
-    def send_pair(l):
-        mine = stack_all.at[l, core]
-        return [send(mine, mine, pair_sems, (l,), (sibling, z))]
-
-    block_moves = [send_blocks(0), send_blocks(1)]
     first_moves = [
         send(first_all.at[own_units], first_all.at[own_units], first_sems, (d,), place(0, d))
         for d in range(1, parts)
@@ -229,7 +235,8 @@
 
     mask_four[...] = window_mask(LANES * r3, r3)
     mask_eight[...] = window_mask(LANES * r2, r2)
-    mean_one[...] = jnp.zeros_like(mean_one)
+    for part in range(2):
+        joined_one[pl.ds((part + 1) * LANES - 32, 32), :] = jnp.zeros((32, two), bf16)
     for copy in started[4:]:
         copy.wait()
 
@@ -270,12 +277,12 @@
             kids = pl.ds(pl.multiple_of((tile + t) * LANES * r3, LANES), LANES * r3)
             matrix = spread(mask_four[...], stripe_rows[tile + t])
             mean = dot(child_rows[:, kids], matrix) / degree_rows[:, lanes]
-            mean_one[0:width, lanes] = mean.astype(bf16)
+            joined_one[LANES : LANES + width, lanes] = mean.astype(bf16)
+            joined_one[0:width, lanes] = own_rows[:, lanes]
 
     def layer_one(tile, tiles):
         lanes = pl.ds(pl.multiple_of(tile * LANES, LANES), LANES * tiles)
-        preact = dot(first_all[:, 0:width], own_rows[:, lanes])
-        preact += dot(first_all[:, LANES : 2 * LANES], mean_one[:, lanes])
+        preact = dot(first_all[...], joined_one[:, lanes])
         output, active, slope, scaling = activate(preact)
         hidden_one[:, lanes] = output
         active_one[:, lanes] = active
@@ -299,10 +306,14 @@
         arrive(block_moves[l])
         chips_moves.append(send_chips(l))
     arrive(first_moves)
-    lax.fori_loop(0, q2 // LANES // per, lambda i, c: (layer_one(i * per, per), c)[1], 0)
+    turns = q2 // LANES // per
+    pair_moves = []
+    for l in range(2):
+        lax.fori_loop(l * turns // 2, (l + 1) * turns // 2, lambda i, c: (layer_one(i * per, per), c)[1], 0)
+        arrive(own_moves[l] + chips_moves[l])
+        pair_moves.append(send_pair(l))
+    arrive(valid_moves)
     layer_one(q2 // LANES, tail)
-    arrive(chips_moves[0])
-    pair_moves = [send_pair(0)]
 
     joined_two[0:hid, :] = hidden_one[:, pl.ds(q2, q1 + LANES)]
     for t in range(q1 // LANES):
@@ -313,7 +324,7 @@
     mean = dot(hidden_one[:, pl.ds(q2, q1)], spread_lead)
     joined_two[hid:, pl.ds(q1, LANES)] = (mean / degree_b).astype(bf16)
 
-    low_half = iota((1, LANES), 1) < half
+    low_half = iota((1, LANES), 1) < unit
 
     def interleave(left, right):
         return jnp.where(low_half, left, shift_half(right)), jnp.where(low_half, shift_half(left), right)
@@ -321,8 +332,8 @@
     def gathered(l):
         for b in range(parts // 2):
             for c in range(2):
-                left = stack_all[l, c, 2 * b].astype(f32).reshape(-1, LANES)
-                right = stack_all[l, c, 2 * b + 1].astype(f32).reshape(-1, LANES)
+                left = stack_all[l, c, lax.rem(z - 2 * b + parts, parts)].astype(f32).reshape(-1, LANES)
+                right = stack_all[l, c, lax.rem(z - 2 * b - 1 + parts, parts)].astype(f32).reshape(-1, LANES)
                 for h, value in enumerate(interleave(left, right)):
                     lanes = slice(b * LANES, (b + 1) * LANES)
                     low_stack[l, :, c, h, :, lanes] = value.astype(bf16).reshape(chips, short, LANES)
@@ -332,9 +343,6 @@
     weight_two = gathered(0)
     preact = dot_tn(weight_two, joined_two[...])
     output, active_two, slope_two, scale_two = activate(preact)
-
-    arrive(chips_moves[1])
-    pair_moves += [send_pair(1)]
 
     joined_three[0:hid, :] = output[:, q1:]
     mean = dot(output[:, 0:q1], spread_three)
@@ -345,7 +353,6 @@
     seeds, active_three, slope_three, scale_three = activate(preact)
 
     head = dot(first_all[...], seat).astype(bf16)
-    arrive(valid_moves)
     every_valid = jnp.sum(valid_all[...], axis=0)[0:1]
     count = jnp.sum(every_valid, axis=1, keepdims=True)
     logits = dot_tn(head, seeds)
@@ -356,8 +363,11 @@
     hot = jnp.where(line.astype(f32) == label, 1.0, 0.0)
     nll = peak + jnp.log(totals) - jnp.sum(hot * logits, axis=0, keepdims=True)
     loss = jnp.sum(jnp.where(present > 0, nll, 0.0), axis=1, keepdims=True)
-    share = present / jnp.maximum(count, 1.0)
-    grad_logits = ((shifted / totals - hot) * share).astype(bf16)
+    count_own[...] = jnp.broadcast_to(count, count_own.shape)
+    out_moves = [pltpu.make_async_copy(count_own, count_out, out_sems.at[0])]
+    out_moves[0].start()
+    weight = present / jnp.maximum(count, 1.0)
+    grad_logits = ((shifted / totals - hot) * weight).astype(bf16)
     placed = dot(seat, grad_logits).astype(bf16)
     grad_one[...] = dot_nt(seeds, placed)
     grad_out = dot(head, grad_logits)
@@ -367,7 +377,7 @@
     part_c = loss - part_a - part_b
     row, col = iota((hid, LANES), 0), iota((hid, LANES), 1) + LANES
     notes = jnp.where(col == free, part_a, jnp.where(col == free + 1, part_b, part_c))
-    notes = jnp.where((col >= free) & (lax.rem(row, unit) == 0), notes, 0.0)
+    notes = jnp.where((col >= free) & (lax.rem(row, unit) == 2 * z + core), notes, 0.0)
     grad_one[:, LANES:] += notes
 
     def keep_grad(l, value):
@@ -393,23 +403,19 @@
             lanes = slice(b * LANES, (b + 1) * LANES)
             for h, value in enumerate(interleave(total[0:short, lanes], total[short:, lanes])):
                 turn_send[l, 2 * b + h] = value.astype(bf16)
+        out_moves.append(pltpu.make_async_copy(turn_send.at[l, z], stack_out.at[l, 0], out_sems.at[1 + l]))
+        out_moves[-1].start()
         return [
-            send(turn_send.at[l, lax.rem(z + d, parts)], turn_recv.at[l, d], turn_sems, (l, d), place(0, d))
+            send(turn_send.at[l, lax.rem(z + d, parts)], stack_out.at[l, d], turn_sems, (l, d), place(0, d))
             for d in range(1, parts)
         ]
 
-    def finish_stack(l):
-        total = turn_send[l, z].astype(f32)
-        for d in range(1, parts):
-            total += turn_recv[l, d].astype(f32)
-        stack_out[l] = total
-
     grad_pre = activate_back(grad_out, active_three, slope_three, scale_three)
     keep_grad(1, dot_nt(joined_three[...], grad_pre))
+    core_moves = [None, send_core(1)]
     grad_joined = dot(weight_three, grad_pre)
     grad_mean = (grad_joined[hid:] / degree_c).astype(bf16)
     grad_out = jnp.concatenate([dot_nt(grad_mean, spread_three), grad_joined[0:hid]], axis=1)
-    core_moves = [None, send_core(1)]
 
     grad_pre = activate_back(grad_out, active_two, slope_two, scale_two)
     keep_grad(0, dot_nt(joined_two[...], grad_pre))
@@ -420,72 +426,56 @@
 
     def back_one(tile, grad_out):
         lanes = pl.ds(tile, grad_out.shape[1])
-        pre_one[:, lanes] = activate_back(
-            grad_out, active_one[:, lanes], slope_one[:, lanes], scale_one[:, lanes]
-        )
-
-    def back_piece(i):
+        grad_pre = activate_back(grad_out, active_one[:, lanes], slope_one[:, lanes], scale_one[:, lanes])
+        return dot_nt(grad_pre, joined_one[:, lanes])
+
+    own = grad_joined[0:hid]
+    total = back_one(q2 + q1, own[:, q1:])
+    total += back_one(q2, own[:, 0:q1] + dot_nt(lead_mean, spread_lead))
+    plane_moves, turn_moves = [None, None], [None, None]
+    for i in range(turns):
+        if i == turns // 2:
+            arrive(core_moves[1])
+            plane_moves[1] = send_plane(1)
         tile = i * per * LANES
         group = tile // (LANES * r2) * LANES
-        back_one(tile, dot_nt(grad_mean[:, group : group + LANES], spread_two[pl.ds(tile, per * LANES), :]))
-
-    own = grad_joined[0:hid]
-    back_one(q2, own[:, 0:q1] + dot_nt(lead_mean, spread_lead))
-    back_one(q2 + q1, own[:, q1:])
-    plane_moves, turn_moves = [None, None], [None, None]
-    pieces = q2 // LANES // per
-    for i in range(pieces // 2):
-        back_piece(i)
-    arrive(core_moves[1])
-    plane_moves[1] = send_plane(1)
-    for i in range(pieces // 2, pieces):
-        back_piece(i)
-    grad_one[:, 0:width] += dot_nt(pre_one[...], own_rows[...])
-    grad_one[:, LANES : LANES + width] += dot_nt(pre_one[...], mean_one[0:width, :])
-    first_send[...] = grad_one[...].astype(bf16)
-
-    group = 2 * unit // 16
-
-    def piece(owner, part):
-        slot = lax.rem(owner, group)
-        rows = pl.ds(pl.multiple_of(part * unit + slot // 2 * 16, 16), 16)
-        return rows, pl.ds(pl.multiple_of(lax.rem(slot, 2) * LANES, LANES), LANES)
-
-    piece_moves = []
-    for i, (k, d) in reversed(list(enumerate(everyone))):
-        owner, part = place(k, d)
-        rows, lanes = piece(owner, part)
-        piece_moves.append(
-            send(first_send.at[rows, lanes], first_recv.at[i], piece_sems, (i,), (owner, part))
-        )
-
+        total += back_one(tile, dot_nt(grad_mean[:, group : group + LANES], spread_two[pl.ds(tile, per * LANES), :]))
+    first_send[...] = (grad_one[...] + total).astype(bf16)
+
+    def half(c):
+        return pl.ds(pl.multiple_of(c * LANES, LANES), LANES)
+
+    def part(d):
+        return pl.ds(pl.multiple_of(lax.rem(z + d, parts) * unit, unit), unit)
+
+    half_moves = [send(first_send.at[:, half(1 - core)], half_recv, half_sems, (0,), (sibling, z))]
     arrive(core_moves[0])
     plane_moves[0] = send_plane(0)
-    for l in (1, 0):
-        arrive(plane_moves[l])
-        turn_moves[l] = send_turn(l)
-
-    arrive(piece_moves)
-    rows, lanes = piece(s, z)
-    total = first_send[rows, lanes].astype(f32)
-    for i in range(len(everyone)):
-        total += first_recv[i].astype(f32)
-    rows, lanes = piece(s, 0)
-    first_piece[rows, lanes] = total
-    held = first_piece.at[rows, lanes]
-    base = s // group * group
-    share_moves = []
-    for k in range(1, group):
-        friend = base + lax.rem(s + k, group)
-        share_moves.append(send(held, held, share_sems, (k,), (friend, z)))
-    for l in (1, 0):
-        arrive(turn_moves[l])
-        finish_stack(l)
+
+    arrive(half_moves)
+    half_send[...] = (first_send[:, half(core)].astype(f32) + half_recv[...].astype(f32)).astype(bf16)
+    part_moves = [
+        send(half_send.at[part(d)], part_recv.at[d], part_sems, (d,), place(0, d)) for d in range(1, parts)
+    ]
+    arrive(plane_moves[1])
+    turn_moves[1] = send_turn(1)
+    arrive(part_moves)
+    total = half_send[part(0), :].astype(f32)
+    for d in range(1, parts):
+        total += part_recv[d].astype(f32)
+    share[...] = total.astype(bf16)
+    held = first_out.at[chip, :, half(core)]
+    out_moves.append(pltpu.make_async_copy(share, held, out_sems.at[3]))
+    out_moves[-1].start()
+    share_moves = [send(share, held, share_sems, (k,), place(k, 0)) for k in range(1, seeds_axis)]
+    arrive(plane_moves[0])
+    turn_moves[0] = send_turn(0)
+
+    for copies in turn_moves:
+        arrive(copies)
     arrive(share_moves)
-    spare = (iota((unit, LANES), 0) == 0) & (iota((unit, LANES), 1) == LANES - 4)
-    first_out[:, 0 : hid - LANES] = first_piece[:, 0 : hid - LANES]
-    first_out[:, hid - LANES :] = jnp.where(spare, count, first_piece[:, hid - LANES :])
-
+    for copy in out_moves:
+        copy.wait()
     for copy in moves:
         copy.wait_send()
 
@@ -500,17 +490,15 @@
     chips = seeds_axis // 2
     rows = 2 * hid // seeds_axis
     slots, slots_b = operands[1].shape[0], operands[2].shape[0]
-    everyone = seeds_axis * parts - 1
     short = rows // 2
-    group = 2 * unit // 16
-    hbm, vmem = pl.BlockSpec(memory_space=pl.ANY), pl.BlockSpec(memory_space=pltpu.VMEM)
+    hbm = pl.BlockSpec(memory_space=pl.ANY)
     shape = jax.ShapeDtypeStruct
     dma = pltpu.SemaphoreType.DMA
     return pl.pallas_call(
         functools.partial(step_kernel, sizes),
-        out_shape=(shape((unit, hid), f32), shape((2, short, LANES), f32)),
+        out_shape=(shape((chips, unit, hid), bf16), shape((2, parts, short, LANES), bf16), shape((8, LANES), f32)),
         in_specs=[hbm] * 9,
-        out_specs=(vmem,) * 2,
+        out_specs=(hbm,) * 3,
         scratch_shapes=[
             pltpu.VMEM((width, two), bf16),
             pltpu.VMEM((width, two * r3), bf16),
@@ -519,7 +507,7 @@
             pltpu.VMEM((slots_b, q1), i32),
             pltpu.VMEM((slots, LANES), i32),
             pltpu.VMEM((slots_b, LANES), i32),
-            pltpu.VMEM((LANES, two), bf16),
+            pltpu.VMEM((2 * LANES, two), bf16),
             pltpu.VMEM((hid, two), bf16),
             pltpu.VMEM((hid, two), f32),
             pltpu.VMEM((hid, two), f32),
@@ -531,7 +519,6 @@
             pltpu.VMEM((q2, LANES), bf16),
             pltpu.VMEM((LANES * r3, LANES), f32),
             pltpu.VMEM((LANES * r2, LANES), f32),
-            pltpu.VMEM((hid, two), bf16),
             pltpu.VMEM((hid, hid), bf16),
             pltpu.VMEM((2, 2, parts, chips, short, LANES), bf16),
             pltpu.VMEM((seeds_axis, 8, LANES), f32),
@@ -541,24 +528,29 @@
             pltpu.VMEM((2, chips, rows, hid), bf16),
             pltpu.VMEM((2, chips, rows, hid), bf16),
             pltpu.VMEM((2, parts, short, LANES), bf16),
-            pltpu.VMEM((2, parts, short, LANES), bf16),
             pltpu.VMEM((hid, hid), f32),
             pltpu.VMEM((hid, hid), bf16),
-            pltpu.VMEM((everyone, 16, LANES), bf16),
-            pltpu.VMEM((unit, hid), f32),
+            pltpu.VMEM((hid, LANES), bf16),
+            pltpu.VMEM((hid, LANES), bf16),
+            pltpu.VMEM((parts, unit, LANES), bf16),
+            pltpu.VMEM((unit, LANES), bf16),
+            pltpu.VMEM((8, LANES), f32),
             *[pltpu.VMEM(v.shape, f32) for v in operands[6:]],
             *[pltpu.VMEM(v.shape, i32) for v in operands[3:6]],
             dma((17,)),
             dma((2, parts)),
             dma((2, 2, parts)),
             dma((2, 2, chips)),
+            dma((2, 2, chips)),
             dma((2, 2)),
             dma((2, seeds_axis)),
             dma((2, 2)),
             dma((2, 2, chips)),
             dma((2, 2, parts)),
-            dma((2, everyone)),
-            dma((2, group)),
+            dma((2, 1)),
+            dma((2, parts)),
+            dma((2, seeds_axis)),
+            dma((4,)),
         ],
         compiler_params=pltpu.CompilerParams(
             vmem_limit_bytes=56 * 2**20, collective_id=0, has_side_effects=True
@@ -579,7 +571,7 @@
 
 def update_kernel(
     width, classes,
-    grad_first, grad_stack,
+    first_parts, stack_parts, count,
     w_a, m_a, s_a, w_b, m_b, s_b, w_c, m_c, s_c,
     loss_out, count_out, om_a, os_a, ow_a, om_b, os_b, ow_b, om_c, os_c, ow_c,
 ):
@@ -588,6 +580,8 @@
             ref[where] = value
 
     half = LANES // 2
+    grad_first = jnp.sum(first_parts[...].astype(f32), axis=0)
+    grad_stack = jnp.sum(stack_parts[...].astype(f32), axis=1)
     short = grad_stack.shape[1]
     for l in range(2):
         for h in range(2):
@@ -599,20 +593,20 @@
         lanes = (slice(None), slice(part * width, (part + 1) * width))
         put((om_a, os_a, ow_a), lanes, adamw(w_a[lanes], m_a[lanes], s_a[lanes], grad))
     gap = LANES - width
-    flipped = grad_first[...].T
+    flipped = grad_first.T
     for start, stop, place in ((0, gap, width), (gap, classes, LANES + width)):
         rows = (slice(start, stop), slice(None))
         grad = flipped[place : place + stop - start]
         put((om_c, os_c, ow_c), rows, adamw(w_c[rows], m_c[rows], s_c[rows], grad))
-    free = grad_first.shape[1] - 3
-    loss_out[...] = jnp.sum(grad_first[0:1, free:], axis=1, keepdims=True)
-    count_out[...] = grad_first[0:1, free - 1 : free]
+    losses = jnp.where(iota((8, LANES), 1) >= LANES - 3, grad_first[0:8, LANES:], 0.0)
+    loss_out[...] = jnp.sum(losses, keepdims=True)
+    count_out[...] = count[0:1, 0:1]
 
 
 def update(width, classes, *operands):
     vmem = pl.BlockSpec(memory_space=pltpu.VMEM)
     shape = jax.ShapeDtypeStruct
-    outs = [shape((1, 1), f32)] * 2 + [shape(v.shape, f32) for v in operands[2:]]
+    outs = [shape((1, 1), f32)] * 2 + [shape(v.shape, f32) for v in operands[3:]]
     return pl.pallas_call(
         functools.partial(update_kernel, width, classes),
         out_shape=tuple(outs),
@@ -643,13 +637,13 @@
         features.shape[0], links_first.shape[0], links_second.shape[0], links_third.shape[0],
         lax.axis_size("hid"), lax.axis_size("seed"), width, classes,
     )
-    grad_first, grad_stack = step(
+    grad_first, grad_stack, count = step(
         sizes,
         features.T, links_first.T, links_second.T, links_third.T,
         labels.reshape(1, -1), valid.reshape(1, -1), weight_first.T, weight_stack, weight_head.T,
     )
     loss_sum, count, m_a, s_a, w_a, m_b, s_b, w_b, m_c, s_c, w_c = update(
-        width, classes, grad_first, grad_stack,
+        width, classes, grad_first, grad_stack, count,
         weight_first.T, moment_first.T, square_first.T,
         weight_stack, moment_stack, square_stack,
         weight_head.T, moment_head.T, square_head.T,

time: 34.7 us -> 32.1 us (0.925)
  Pallas kernels: 33.9 us -> 31.3 us
    pallas_call x1, Pallas kernels: 31.9 us -> 29.2 us  [step(): pl.pallas_call(functools.partial(step_kernel, sizes), out_shape=(shape((c...]
where the time goes in v5:
time: 32.1 us; the launch traced here: 31.9 us
  Pallas kernels  31.3 us (98%)
  between operations  0.65 us (2%)
    pallas_call x1, Pallas kernels, step(): pl.pallas_call(functools.partial(step_kernel, sizes), out_shape=(shape((c...  29.2 us
    pallas_call x1, Pallas kernels, update(): pl.pallas_call(functools.partial(update_kernel, width, classes), out_shap...  2.05 us

profile of v5, /device:TPU:0, one launch (start us, length us, event | category | flops | bytes accessed | tf_op | source)
XLA Modules:
  0.0 31.9 jit_solution(8091020501616403506)
XLA Ops:
  0.6 29.2 %shard_map.230 = (bf16[4,64,256]{2,1,0:T(8,128)(2,1)}, bf16[2,4,32,128]{3,2,1,0:T(8,128)(2,1)}, f32[8,128]{1,0:T(8,128)}) custom-call(bf16[100,32768]{1,0:T(8,128)(2,1)} %bitcast.20, s32[10,8192]{1,0:T(8,128)} %bitcast.21, s32[10,1024]{1,0:T(8,128)} %bitcast.26, s32[25,128]{1,0:T(8,128)} %bitcast.31, s32[1,128]{1,0:T(1,128)} %bitcast.32, s32[1,128]{1,0:T(1,128)} %bitcast.33, ...), custom_call_target="tpu_custom_call" | custom-call | tf_op jit(solution)/shard_map/pallas_call | solution.py:497
  29.9 2.0 %shard_map.231 = (f32[1,1]{1,0:T(1,128)}, f32[1,1]{1,0:T(1,128)}, f32[64,200]{1,0:T(8,128)}, f32[64,200]{1,0:T(8,128)}, f32[64,200]{1,0:T(8,128)}, /*index=5*/f3...) custom-call(bf16[4,64,256]{2,1,0:T(8,128)(2,1)} %get-tuple-element.2, ...), custom_call_target="tpu_custom_call" | custom-call | tf_op jit(solution)/shard_map/pallas_call | solution.py:610

commit v6 on v5

--- a/solution.py
+++ b/solution.py
@@ -115,7 +115,7 @@
     core_send, core_recv, plane_send, plane_recv, turn_send,
     grad_one, first_send, half_recv, half_send, part_recv, share, count_own, first_own, stack_own, head_own,
     links_c, labels_own, valid_own,
-    local_sems, first_sems, block_sems, own_sems, chips_sems, pair_sems, valid_sems,
+    local_sems, first_sems, block_sems, chips_sems, pair_sems, valid_sems,
     core_sems, plane_sems, turn_sems, half_sems, part_sems, share_sems, out_sems,
 ):
     n3, n2, n1, n0, parts, seeds_axis, width, classes = sizes
@@ -176,7 +176,7 @@
     for l in range(2):
         block = dot(stack_own[l, 0:short].astype(bf16), to_left)
         block += dot(stack_own[l, short:].astype(bf16), to_right)
-        stack_all[l, core, 0, chip] = block.astype(bf16)
+        stack_all[core, 0, chip, l] = block.astype(bf16)
     pl.semaphore_wait(barrier, len(near))
 
     moves = []
@@ -194,26 +194,22 @@
         for copy in copies:
             copy.wait_recv()
 
-    def send_blocks(l):
-        mine = stack_all.at[l, core, 0, chip]
-        return [
-            send(mine, stack_all.at[l, core, d, chip], block_sems, (l, d), place(0, d)) for d in range(1, parts)
-        ]
-
-    def send_own(l):
-        mine = stack_all.at[l, core, 0, chip]
-        return [send(mine, mine, own_sems, (l, k), place(2 * k, 0)) for k in range(1, chips)]
-
-    def send_chips(l):
-        mine = stack_all.at[l, core, 1:parts, chip]
-        return [send(mine, mine, chips_sems, (l, k), place(2 * k, 0)) for k in range(1, chips)]
-
-    def send_pair(l):
-        mine = stack_all.at[l, core]
-        return [send(mine, mine, pair_sems, (l,), (sibling, z))]
-
-    block_moves = [send_blocks(0), send_blocks(1)]
-    own_moves = [send_own(0), send_own(1)]
+    flip = 1 - 2 * z // parts
+    distances = [0] + [i + flip * (parts - 2 * i) for i in range(1, parts)]
+
+    def send_chips(d):
+        block = stack_all.at[core, d, chip]
+        return [send(block, block, chips_sems, (d, k), place(2 * k, 0)) for k in range(1, chips)]
+
+    def send_pair(d):
+        block = stack_all.at[core, d]
+        return send(block, block, pair_sems, (d,), (sibling, z))
+
+    block_moves = [
+        send(stack_all.at[core, 0, chip], stack_all.at[core, d, chip], block_sems, (d,), place(0, d))
+        for d in distances[1:]
+    ]
+    chips_moves = [send_chips(0)]
     for copy in started[1:4]:
         copy.wait()
     row, col = iota((2 * width, hid), 0), iota((2 * width, hid), 1)
@@ -301,19 +297,30 @@
     spread_lead = spread(mask_eight[0 : q0 * r2, :], stripes(counts_b))
     spread_three = spread(mask_eight[0 : q0 * r1, :], stripes(counts_c))
 
-    chips_moves = []
-    for l in range(2):
-        arrive(block_moves[l])
-        chips_moves.append(send_chips(l))
+    for d, copy in zip(distances[1:], block_moves):
+        arrive([copy])
+        chips_moves.append(send_chips(d))
+    arrive(chips_moves[0])
+    pair_moves = [send_pair(0)]
     arrive(first_moves)
     turns = q2 // LANES // per
-    pair_moves = []
-    for l in range(2):
-        lax.fori_loop(l * turns // 2, (l + 1) * turns // 2, lambda i, c: (layer_one(i * per, per), c)[1], 0)
-        arrive(own_moves[l] + chips_moves[l])
-        pair_moves.append(send_pair(l))
+    at_turn = lambda i, c: (layer_one(i * per, per), c)[1]
+    lax.fori_loop(0, turns // 2, at_turn, 0)
+    for i in range(1, parts // 2):
+        arrive(chips_moves[i])
+        pair_moves.append(send_pair(distances[i]))
+    lax.fori_loop(turns // 2, turns, at_turn, 0)
+    for i in range(parts // 2, parts):
+        arrive(chips_moves[i])
+        pair_moves.append(send_pair(distances[i]))
     arrive(valid_moves)
     layer_one(q2 // LANES, tail)
+    head = dot(first_all[...], seat).astype(bf16)
+    every_valid = jnp.sum(valid_all[...], axis=0)[0:1]
+    count = jnp.sum(every_valid, axis=1, keepdims=True)
+    count_own[...] = jnp.broadcast_to(count, count_own.shape)
+    out_moves = [pltpu.make_async_copy(count_own, count_out, out_sems.at[0])]
+    out_moves[0].start()
 
     joined_two[0:hid, :] = hidden_one[:, pl.ds(q2, q1 + LANES)]
     for t in range(q1 // LANES):
@@ -332,14 +339,14 @@
     def gathered(l):
         for b in range(parts // 2):
             for c in range(2):
-                left = stack_all[l, c, lax.rem(z - 2 * b + parts, parts)].astype(f32).reshape(-1, LANES)
-                right = stack_all[l, c, lax.rem(z - 2 * b - 1 + parts, parts)].astype(f32).reshape(-1, LANES)
+                left = stack_all[c, lax.rem(z - 2 * b + parts, parts), :, l].astype(f32).reshape(-1, LANES)
+                right = stack_all[c, lax.rem(z - 2 * b - 1 + parts, parts), :, l].astype(f32).reshape(-1, LANES)
                 for h, value in enumerate(interleave(left, right)):
                     lanes = slice(b * LANES, (b + 1) * LANES)
                     low_stack[l, :, c, h, :, lanes] = value.astype(bf16).reshape(chips, short, LANES)
         return low_stack[l].reshape(2 * hid, hid)
 
-    arrive(pair_moves[0])
+    arrive(pair_moves)
     weight_two = gathered(0)
     preact = dot_tn(weight_two, joined_two[...])
     output, active_two, slope_two, scale_two = activate(preact)
@@ -347,38 +354,19 @@
     joined_three[0:hid, :] = output[:, q1:]
     mean = dot(output[:, 0:q1], spread_three)
     joined_three[hid:, :] = (mean / degree_c).astype(bf16)
-    arrive(pair_moves[1])
     weight_three = gathered(1)
     preact = dot_tn(weight_three, joined_three[...])
     seeds, active_three, slope_three, scale_three = activate(preact)
 
-    head = dot(first_all[...], seat).astype(bf16)
-    every_valid = jnp.sum(valid_all[...], axis=0)[0:1]
-    count = jnp.sum(every_valid, axis=1, keepdims=True)
     logits = dot_tn(head, seeds)
     line = iota(logits.shape, 0)
     peak = jnp.max(logits, axis=0, keepdims=True)
     shifted = jnp.exp(logits - peak)
     totals = jnp.sum(shifted, axis=0, keepdims=True)
     hot = jnp.where(line.astype(f32) == label, 1.0, 0.0)
-    nll = peak + jnp.log(totals) - jnp.sum(hot * logits, axis=0, keepdims=True)
-    loss = jnp.sum(jnp.where(present > 0, nll, 0.0), axis=1, keepdims=True)
-    count_own[...] = jnp.broadcast_to(count, count_own.shape)
-    out_moves = [pltpu.make_async_copy(count_own, count_out, out_sems.at[0])]
-    out_moves[0].start()
     weight = present / jnp.maximum(count, 1.0)
     grad_logits = ((shifted / totals - hot) * weight).astype(bf16)
-    placed = dot(seat, grad_logits).astype(bf16)
-    grad_one[...] = dot_nt(seeds, placed)
     grad_out = dot(head, grad_logits)
-    free = 2 * LANES - 3
-    part_a = loss.astype(bf16).astype(f32)
-    part_b = (loss - part_a).astype(bf16).astype(f32)
-    part_c = loss - part_a - part_b
-    row, col = iota((hid, LANES), 0), iota((hid, LANES), 1) + LANES
-    notes = jnp.where(col == free, part_a, jnp.where(col == free + 1, part_b, part_c))
-    notes = jnp.where((col >= free) & (lax.rem(row, unit) == 2 * z + core), notes, 0.0)
-    grad_one[:, LANES:] += notes
 
     def keep_grad(l, value):
         value = value.astype(bf16).reshape(chips, 2, depth, hid)
@@ -412,34 +400,52 @@
 
     grad_pre = activate_back(grad_out, active_three, slope_three, scale_three)
     keep_grad(1, dot_nt(joined_three[...], grad_pre))
-    core_moves = [None, send_core(1)]
     grad_joined = dot(weight_three, grad_pre)
     grad_mean = (grad_joined[hid:] / degree_c).astype(bf16)
     grad_out = jnp.concatenate([dot_nt(grad_mean, spread_three), grad_joined[0:hid]], axis=1)
 
     grad_pre = activate_back(grad_out, active_two, slope_two, scale_two)
+    core_one = send_core(1)
     keep_grad(0, dot_nt(joined_two[...], grad_pre))
     grad_joined = dot(weight_two, grad_pre)
     grad_mean = (grad_joined[hid:, 0:q1] / degree_t).astype(bf16)
     lead_mean = (grad_joined[hid:, q1:] / degree_b).astype(bf16)
-    core_moves[0] = send_core(0)
-
-    def back_one(tile, grad_out):
+    core_moves = [send_core(0), core_one]
+
+    nll = peak + jnp.log(totals) - jnp.sum(hot * logits, axis=0, keepdims=True)
+    loss = jnp.sum(jnp.where(present > 0, nll, 0.0), axis=1, keepdims=True)
+    placed = dot(seat, grad_logits).astype(bf16)
+    grad_one[...] = dot_nt(seeds, placed)
+    free = 2 * LANES - 3
+    part_a = loss.astype(bf16).astype(f32)
+    part_b = (loss - part_a).astype(bf16).astype(f32)
+    part_c = loss - part_a - part_b
+    row, col = iota((hid, LANES), 0), iota((hid, LANES), 1) + LANES
+    notes = jnp.where(col == free, part_a, jnp.where(col == free + 1, part_b, part_c))
+    notes = jnp.where((col >= free) & (lax.rem(row, unit) == 2 * z + core), notes, 0.0)
+    grad_one[:, LANES:] += notes
+
+    own = grad_joined[0:hid]
+    plane_moves, turn_moves = [None, None], [None, None]
+    step_lanes = 2 * LANES
+
+    def named(tile):
+        group = tile // (LANES * r2) * LANES
+        return dot_nt(grad_mean[:, group : group + LANES], spread_two[pl.ds(tile, step_lanes), :])
+
+    pieces = [(q2 + q1, lambda tile: own[:, q1:]), (q2, lambda tile: own[:, 0:q1] + dot_nt(lead_mean, spread_lead))]
+    pieces += [(tile, named) for tile in range(0, q2, step_lanes)]
+    grad_out = pieces[0][1](pieces[0][0])
+    total, waiting = None, None
+    for i, (tile, _) in enumerate(pieces):
+        ahead = pieces[i + 1][1](pieces[i + 1][0]) if i + 1 < len(pieces) else None
         lanes = pl.ds(tile, grad_out.shape[1])
         grad_pre = activate_back(grad_out, active_one[:, lanes], slope_one[:, lanes], scale_one[:, lanes])
-        return dot_nt(grad_pre, joined_one[:, lanes])
-
-    own = grad_joined[0:hid]
-    total = back_one(q2 + q1, own[:, q1:])
-    total += back_one(q2, own[:, 0:q1] + dot_nt(lead_mean, spread_lead))
-    plane_moves, turn_moves = [None, None], [None, None]
-    for i in range(turns):
-        if i == turns // 2:
-            arrive(core_moves[1])
-            plane_moves[1] = send_plane(1)
-        tile = i * per * LANES
-        group = tile // (LANES * r2) * LANES
-        total += back_one(tile, dot_nt(grad_mean[:, group : group + LANES], spread_two[pl.ds(tile, per * LANES), :]))
+        if waiting is not None:
+            total = waiting() if total is None else total + waiting()
+        waiting = functools.partial(lambda g, v: dot_nt(g, joined_one[:, v]), grad_pre, lanes)
+        grad_out = ahead
+    total += waiting()
     first_send[...] = (grad_one[...] + total).astype(bf16)
 
     def half(c):
@@ -449,8 +455,9 @@
         return pl.ds(pl.multiple_of(lax.rem(z + d, parts) * unit, unit), unit)
 
     half_moves = [send(first_send.at[:, half(1 - core)], half_recv, half_sems, (0,), (sibling, z))]
-    arrive(core_moves[0])
-    plane_moves[0] = send_plane(0)
+    for l in (1, 0):
+        arrive(core_moves[l])
+        plane_moves[l] = send_plane(l)
 
     arrive(half_moves)
     half_send[...] = (first_send[:, half(core)].astype(f32) + half_recv[...].astype(f32)).astype(bf16)
@@ -520,7 +527,7 @@
             pltpu.VMEM((LANES * r3, LANES), f32),
             pltpu.VMEM((LANES * r2, LANES), f32),
             pltpu.VMEM((hid, hid), bf16),
-            pltpu.VMEM((2, 2, parts, chips, short, LANES), bf16),
+            pltpu.VMEM((2, parts, chips, 2, short, LANES), bf16),
             pltpu.VMEM((seeds_axis, 8, LANES), f32),
             pltpu.VMEM((2, chips, 2, 2, short, hid), bf16),
             pltpu.VMEM((2, 2, chips, rows, hid), bf16),
@@ -539,10 +546,9 @@
             *[pltpu.VMEM(v.shape, i32) for v in operands[3:6]],
             dma((17,)),
             dma((2, parts)),
-            dma((2, 2, parts)),
-            dma((2, 2, chips)),
-            dma((2, 2, chips)),
-            dma((2, 2)),
+            dma((2, parts)),
+            dma((2, parts, chips)),
+            dma((2, parts)),
             dma((2, seeds_axis)),
             dma((2, 2)),
             dma((2, 2, chips)),

time: 32.1 us -> 31 us (0.966)
  Pallas kernels: 31.3 us -> 30.2 us
    pallas_call x1, Pallas kernels: 29.2 us -> 28.2 us  [step(): pl.pallas_call(functools.partial(step_kernel, sizes), out_shape=(shape((c...]
where the time goes in v6:
time: 31 us; the launch traced here: 30.9 us
  Pallas kernels  30.2 us (97%)
  between operations  0.65 us (2%)
    pallas_call x1, Pallas kernels, step(): pl.pallas_call(functools.partial(step_kernel, sizes), out_shape=(shape((c...  28.2 us
    pallas_call x1, Pallas kernels, update(): pl.pallas_call(functools.partial(update_kernel, width, classes), out_shap...  2.05 us

profile of v6, /device:TPU:0, one launch (start us, length us, event | category | flops | bytes accessed | tf_op | source)
XLA Modules:
  0.0 30.9 jit_solution(5841234729304318730)
XLA Ops:
  0.6 28.2 %shard_map.230 = (bf16[4,64,256]{2,1,0:T(8,128)(2,1)}, bf16[2,4,32,128]{3,2,1,0:T(8,128)(2,1)}, f32[8,128]{1,0:T(8,128)}) custom-call(bf16[100,32768]{1,0:T(8,128)(2,1)} %bitcast.20, s32[10,8192]{1,0:T(8,128)} %bitcast.21, s32[10,1024]{1,0:T(8,128)} %bitcast.26, s32[25,128]{1,0:T(8,128)} %bitcast.31, s32[1,128]{1,0:T(1,128)} %bitcast.32, s32[1,128]{1,0:T(1,128)} %bitcast.33, ...), custom_call_target="tpu_custom_call" | custom-call | tf_op jit(solution)/shard_map/pallas_call | solution.py:504
  28.8 2.0 %shard_map.231 = (f32[1,1]{1,0:T(1,128)}, f32[1,1]{1,0:T(1,128)}, f32[64,200]{1,0:T(8,128)}, f32[64,200]{1,0:T(8,128)}, f32[64,200]{1,0:T(8,128)}, /*index=5*/f3...) custom-call(bf16[4,64,256]{2,1,0:T(8,128)(2,1)} %get-tuple-element.2, ...), custom_call_target="tpu_custom_call" | custom-call | tf_op jit(solution)/shard_map/pallas_call | solution.py:616

commit v7 on v6

--- a/solution.py
+++ b/solution.py
@@ -47,9 +47,7 @@
     counts = [
         jnp.sum(jnp.where(offsets == r, 1.0, 0.0), axis=0, keepdims=True) for r in range(ratio)
     ]
-    degree = jnp.maximum(
-        jnp.sum(jnp.where(links >= 0, 1.0, 0.0), axis=0, keepdims=True), 1.0
-    )
+    degree = jnp.sum(jnp.where(links >= 0, 1.0, 0.0), axis=0, keepdims=True)
     return counts, degree
 
 
@@ -72,10 +70,14 @@
     return jnp.where(iota((rows, LANES), 0) // ratio == iota((rows, LANES), 1), 1.0, 0.0)
 
 
-def activate(preact):
+def sigmoid_parts(preact):
     logistic = 0.5 * jnp.tanh(0.5 * preact) + 0.5
     active = preact * logistic
-    slope = logistic + (active - active * logistic)
+    return active, logistic + (active - active * logistic)
+
+
+def activate(preact):
+    active, slope = sigmoid_parts(preact)
     scaling = lax.rsqrt(jnp.sum(active * active, axis=0, keepdims=True) + epsilon_norm)
     return (active * scaling).astype(bf16), active, slope, scaling
 
@@ -109,13 +111,13 @@
     features, links_first, links_second, links_third, labels, valid, weight_first, weight_stack, weight_head,
     first_out, stack_out, count_out,
     own_rows, child_rows, own_lead, links_a, links_b, links_a_lead, links_b_lead,
-    joined_one, hidden_one, active_one, slope_one, scale_one, degree_rows, stripe_rows,
+    joined_one, hidden_one, active_one, slope_one, scale_one, square_rows, degree_rows, stripe_rows,
     joined_two, joined_three, spread_two, mask_four, mask_eight,
     first_all, stack_all, valid_all, low_stack,
     core_send, core_recv, plane_send, plane_recv, turn_send,
     grad_one, first_send, half_recv, half_send, part_recv, share, count_own, first_own, stack_own, head_own,
     links_c, labels_own, valid_own,
-    local_sems, first_sems, block_sems, chips_sems, pair_sems, valid_sems,
+    local_sems, first_sems, block_sems, chips_sems, wide_sems, pair_sems, valid_sems,
     core_sems, plane_sems, turn_sems, half_sems, part_sems, share_sems, out_sems,
 ):
     n3, n2, n1, n0, parts, seeds_axis, width, classes = sizes
@@ -164,7 +166,7 @@
         ),
     ]
     started = [pltpu.make_async_copy(src, dst, local_sems.at[i]) for i, (src, dst) in enumerate(copies)]
-    for copy in started:
+    for copy in started[:4]:
         copy.start()
 
     started[0].wait()
@@ -177,6 +179,8 @@
         block = dot(stack_own[l, 0:short].astype(bf16), to_left)
         block += dot(stack_own[l, short:].astype(bf16), to_right)
         stack_all[core, 0, chip, l] = block.astype(bf16)
+    for copy in started[4:]:
+        copy.start()
     pl.semaphore_wait(barrier, len(near))
 
     moves = []
@@ -200,6 +204,10 @@
     def send_chips(d):
         block = stack_all.at[core, d, chip]
         return [send(block, block, chips_sems, (d, k), place(2 * k, 0)) for k in range(1, chips)]
+
+    def send_plane_wide(d):
+        block = stack_all.at[core, d, chip]
+        return [send(block, block, wide_sems, (k,), place(k, 0)) for k in range(1, seeds_axis)]
 
     def send_pair(d):
         block = stack_all.at[core, d]
@@ -222,9 +230,8 @@
     valid_all[s] = jnp.broadcast_to(valid_own[...].astype(f32), valid_all.shape[1:])
 
     first_moves = [
-        send(first_all.at[own_units], first_all.at[own_units], first_sems, (d,), place(0, d))
-        for d in range(1, parts)
-    ]
+        send(first_all.at[own_units], first_all.at[own_units], first_sems, (d,), place(0, d)) for d in reversed(distances[1:])
+    ][::-1]
     valid_moves = [
         send(valid_all.at[s], valid_all.at[s], valid_sems, (k,), place(k, 0)) for k in range(1, seeds_axis)
     ]
@@ -248,22 +255,22 @@
     mine = jnp.where((source == target + z * q0) & (target < q0), 1.0, 0.0).astype(bf16)
     packed = dot(packed.astype(bf16), mine)
     take = [packed[k : k + 1] for k in range(len(lead))]
-    counts_a, degree_a = take[:r3], jnp.maximum(take[r3], 1.0)
+    counts_a, degree_a = take[:r3], 1.0 / jnp.maximum(take[r3], 1.0)
     take = take[r3 + 1 :]
-    counts_b, degree_b = take[:r2], jnp.maximum(take[r2], 1.0)
+    counts_b, degree_b = take[:r2], 1.0 / jnp.maximum(take[r2], 1.0)
     take = take[r2 + 1 :]
-    counts_c, degree_c = take[:r1], jnp.maximum(take[r1], 1.0)
+    counts_c, degree_c = take[:r1], 1.0 / jnp.maximum(take[r1], 1.0)
     label, present = take[r1 + 1], take[r1 + 2]
     own_rows[:, pl.ds(q2 + q1, LANES)] = dot(own_lead[...], mine).astype(bf16)
 
     counts, degree = slot_counts(links_a[:, pl.ds(0, q2)], z * q2, r3)
     for t in range(q2 // LANES):
         stripe_rows[t] = stripes([c[:, t * LANES : (t + 1) * LANES] for c in counts])
-    degree_rows[:, pl.ds(0, q2)] = degree
+    degree_rows[:, pl.ds(0, q2)] = 1.0 / jnp.maximum(degree, 1.0)
     counts, degree = slot_counts(links_a[:, pl.ds(q2, q1)], z * q1, r3)
     for t in range(q1 // LANES):
         stripe_rows[q2 // LANES + t] = stripes([c[:, t * LANES : (t + 1) * LANES] for c in counts])
-    degree_rows[:, pl.ds(q2, q1)] = degree
+    degree_rows[:, pl.ds(q2, q1)] = 1.0 / jnp.maximum(degree, 1.0)
     stripe_rows[two // LANES - 1] = stripes(counts_a)
     degree_rows[:, pl.ds(q2 + q1, LANES)] = degree_a
 
@@ -272,49 +279,53 @@
             lanes = pl.ds(pl.multiple_of((tile + t) * LANES, LANES), LANES)
             kids = pl.ds(pl.multiple_of((tile + t) * LANES * r3, LANES), LANES * r3)
             matrix = spread(mask_four[...], stripe_rows[tile + t])
-            mean = dot(child_rows[:, kids], matrix) / degree_rows[:, lanes]
+            mean = dot(child_rows[:, kids], matrix) * degree_rows[:, lanes]
             joined_one[LANES : LANES + width, lanes] = mean.astype(bf16)
             joined_one[0:width, lanes] = own_rows[:, lanes]
 
-    def layer_one(tile, tiles):
-        lanes = pl.ds(pl.multiple_of(tile * LANES, LANES), LANES * tiles)
-        preact = dot(first_all[...], joined_one[:, lanes])
-        output, active, slope, scaling = activate(preact)
-        hidden_one[:, lanes] = output
-        active_one[:, lanes] = active
-        slope_one[:, lanes] = slope
-        scale_one[:, lanes] = scaling
+    def layer_one(i):
+        units = pl.ds(pl.multiple_of(lax.rem(z - distances[i] + parts, parts) * unit, unit), unit)
+
+        def tile_units(tile, tiles):
+            lanes = pl.ds(pl.multiple_of(tile * LANES, LANES), LANES * tiles)
+            active, slope = sigmoid_parts(dot(first_all[units, :], joined_one[:, lanes]))
+            active_one[units, lanes] = active
+            slope_one[units, lanes] = slope
+            square_rows[i : i + 1, lanes] = jnp.sum(active * active, axis=0, keepdims=True)
+
+        tile_units(0, two // LANES)
 
     per = 4
+    wide = 16
     tail = q1 // LANES + 1
     lax.fori_loop(0, q2 // LANES // per, lambda i, c: (mean_tiles(i * per, per), c)[1], 0)
     mean_tiles(q2 // LANES, tail)
 
     counts, degree_t = slot_counts(links_b[...], z * q1, r2)
+    share_t = 1.0 / jnp.maximum(degree_t, 1.0)
     for t in range(q1 // LANES):
         stripe = stripes([c[:, t * LANES : (t + 1) * LANES] for c in counts])
         spread_two[pl.ds(t * LANES * r2, LANES * r2), :] = spread(mask_eight[...], stripe)
     spread_lead = spread(mask_eight[0 : q0 * r2, :], stripes(counts_b))
     spread_three = spread(mask_eight[0 : q0 * r1, :], stripes(counts_c))
 
+    layer_one(0)
     for d, copy in zip(distances[1:], block_moves):
         arrive([copy])
-        chips_moves.append(send_chips(d))
+        chips_moves.append((send_plane_wide if copy is block_moves[-1] else send_chips)(d))
+    pair_moves = []
     arrive(chips_moves[0])
-    pair_moves = [send_pair(0)]
-    arrive(first_moves)
-    turns = q2 // LANES // per
-    at_turn = lambda i, c: (layer_one(i * per, per), c)[1]
-    lax.fori_loop(0, turns // 2, at_turn, 0)
-    for i in range(1, parts // 2):
+    pair_moves.append(send_pair(distances[0]))
+    for i in range(1, parts):
+        arrive(first_moves[i - 1 : i])
+        layer_one(i)
+    for i in range(1, parts - 1):
         arrive(chips_moves[i])
         pair_moves.append(send_pair(distances[i]))
-    lax.fori_loop(turns // 2, turns, at_turn, 0)
-    for i in range(parts // 2, parts):
-        arrive(chips_moves[i])
-        pair_moves.append(send_pair(distances[i]))
+    squares = jnp.sum(square_rows[0:parts, :], axis=0, keepdims=True)
+    scale_one[...] = lax.rsqrt(squares + epsilon_norm)
+    hidden_one[...] = (active_one[...] * scale_one[...]).astype(bf16)
     arrive(valid_moves)
-    layer_one(q2 // LANES, tail)
     head = dot(first_all[...], seat).astype(bf16)
     every_valid = jnp.sum(valid_all[...], axis=0)[0:1]
     count = jnp.sum(every_valid, axis=1, keepdims=True)
@@ -327,9 +338,9 @@
         rows = pl.ds(t * LANES * r2, LANES * r2)
         mean = dot(hidden_one[:, rows], spread_two[rows, :])
         lanes = slice(t * LANES, (t + 1) * LANES)
-        joined_two[hid:, lanes] = (mean / degree_t[:, lanes]).astype(bf16)
+        joined_two[hid:, lanes] = (mean * share_t[:, lanes]).astype(bf16)
     mean = dot(hidden_one[:, pl.ds(q2, q1)], spread_lead)
-    joined_two[hid:, pl.ds(q1, LANES)] = (mean / degree_b).astype(bf16)
+    joined_two[hid:, pl.ds(q1, LANES)] = (mean * degree_b).astype(bf16)
 
     low_half = iota((1, LANES), 1) < unit
 
@@ -339,21 +350,21 @@
     def gathered(l):
         for b in range(parts // 2):
             for c in range(2):
-                left = stack_all[c, lax.rem(z - 2 * b + parts, parts), :, l].astype(f32).reshape(-1, LANES)
-                right = stack_all[c, lax.rem(z - 2 * b - 1 + parts, parts), :, l].astype(f32).reshape(-1, LANES)
+                left = stack_all[c, lax.rem(z - 2 * b + parts, parts), :, l].reshape(-1, LANES)
+                right = stack_all[c, lax.rem(z - 2 * b - 1 + parts, parts), :, l].reshape(-1, LANES)
                 for h, value in enumerate(interleave(left, right)):
                     lanes = slice(b * LANES, (b + 1) * LANES)
                     low_stack[l, :, c, h, :, lanes] = value.astype(bf16).reshape(chips, short, LANES)
         return low_stack[l].reshape(2 * hid, hid)
 
-    arrive(pair_moves)
+    arrive(pair_moves + chips_moves[-1])
     weight_two = gathered(0)
     preact = dot_tn(weight_two, joined_two[...])
     output, active_two, slope_two, scale_two = activate(preact)
 
     joined_three[0:hid, :] = output[:, q1:]
     mean = dot(output[:, 0:q1], spread_three)
-    joined_three[hid:, :] = (mean / degree_c).astype(bf16)
+    joined_three[hid:, :] = (mean * degree_c).astype(bf16)
     weight_three = gathered(1)
     preact = dot_tn(weight_three, joined_three[...])
     seeds, active_three, slope_three, scale_three = activate(preact)
@@ -401,15 +412,15 @@
     grad_pre = activate_back(grad_out, active_three, slope_three, scale_three)
     keep_grad(1, dot_nt(joined_three[...], grad_pre))
     grad_joined = dot(weight_three, grad_pre)
-    grad_mean = (grad_joined[hid:] / degree_c).astype(bf16)
+    grad_mean = (grad_joined[hid:] * degree_c).astype(bf16)
     grad_out = jnp.concatenate([dot_nt(grad_mean, spread_three), grad_joined[0:hid]], axis=1)
 
     grad_pre = activate_back(grad_out, active_two, slope_two, scale_two)
     core_one = send_core(1)
     keep_grad(0, dot_nt(joined_two[...], grad_pre))
     grad_joined = dot(weight_two, grad_pre)
-    grad_mean = (grad_joined[hid:, 0:q1] / degree_t).astype(bf16)
-    lead_mean = (grad_joined[hid:, q1:] / degree_b).astype(bf16)
+    grad_mean = (grad_joined[hid:, 0:q1] * share_t).astype(bf16)
+    lead_mean = (grad_joined[hid:, q1:] * degree_b).astype(bf16)
     core_moves = [send_core(0), core_one]
 
     nll = peak + jnp.log(totals) - jnp.sum(hot * logits, axis=0, keepdims=True)
@@ -462,7 +473,7 @@
     arrive(half_moves)
     half_send[...] = (first_send[:, half(core)].astype(f32) + half_recv[...].astype(f32)).astype(bf16)
     part_moves = [
-        send(half_send.at[part(d)], part_recv.at[d], part_sems, (d,), place(0, d)) for d in range(1, parts)
+        send(half_send.at[part(d)], part_recv.at[d], part_sems, (d,), place(0, d)) for d in distances[1:]
     ]
     arrive(plane_moves[1])
     turn_moves[1] = send_turn(1)
@@ -519,6 +530,7 @@
             pltpu.VMEM((hid, two), f32),
             pltpu.VMEM((hid, two), f32),
             pltpu.VMEM((1, two), f32),
+            pltpu.VMEM((8, two), f32),
             pltpu.VMEM((1, two), f32),
             pltpu.VMEM((two // LANES, 8, LANES), f32),
             pltpu.VMEM((2 * hid, q1 + LANES), bf16),
@@ -548,6 +560,7 @@
             dma((2, parts)),
             dma((2, parts)),
             dma((2, parts, chips)),
+            dma((2, seeds_axis)),
             dma((2, parts)),
             dma((2, seeds_axis)),
             dma((2, 2)),

time: 31 us -> 30.6 us (0.987)
  Pallas kernels: 30.2 us -> 29.7 us
    pallas_call x1, Pallas kernels: 28.2 us -> 27.7 us  [step(): pl.pallas_call(functools.partial(step_kernel, sizes), out_shape=(shape((c...]
where the time goes in v7:
time: 30.6 us; the launch traced here: 30.4 us
  Pallas kernels  29.7 us (97%)
  between operations  0.65 us (2%)
    pallas_call x1, Pallas kernels, step(): pl.pallas_call(functools.partial(step_kernel, sizes), out_shape=(shape((c...  27.7 us
    pallas_call x1, Pallas kernels, update(): pl.pallas_call(functools.partial(update_kernel, width, classes), out_shap...  2.05 us

profile of v7, /device:TPU:0, one launch (start us, length us, event | category | flops | bytes accessed | tf_op | source)
XLA Modules:
  0.0 30.4 jit_solution(3188317164962548932)
XLA Ops:
  0.6 27.7 %shard_map.230 = (bf16[4,64,256]{2,1,0:T(8,128)(2,1)}, bf16[2,4,32,128]{3,2,1,0:T(8,128)(2,1)}, f32[8,128]{1,0:T(8,128)}) custom-call(bf16[100,32768]{1,0:T(8,128)(2,1)} %bitcast.20, s32[10,8192]{1,0:T(8,128)} %bitcast.21, s32[10,1024]{1,0:T(8,128)} %bitcast.26, s32[25,128]{1,0:T(8,128)} %bitcast.31, s32[1,128]{1,0:T(1,128)} %bitcast.32, s32[1,128]{1,0:T(1,128)} %bitcast.33, ...), custom_call_target="tpu_custom_call" | custom-call | tf_op jit(solution)/shard_map/pallas_call | solution.py:515
  28.3 2.0 %shard_map.231 = (f32[1,1]{1,0:T(1,128)}, f32[1,1]{1,0:T(1,128)}, f32[64,200]{1,0:T(8,128)}, f32[64,200]{1,0:T(8,128)}, f32[64,200]{1,0:T(8,128)}, /*index=5*/f3...) custom-call(bf16[4,64,256]{2,1,0:T(8,128)(2,1)} %get-tuple-element.2, ...), custom_call_target="tpu_custom_call" | custom-call | tf_op jit(solution)/shard_map/pallas_call | solution.py:629

commit v8 on v7

--- a/solution.py
+++ b/solution.py
@@ -117,7 +117,7 @@
     core_send, core_recv, plane_send, plane_recv, turn_send,
     grad_one, first_send, half_recv, half_send, part_recv, share, count_own, first_own, stack_own, head_own,
     links_c, labels_own, valid_own,
-    local_sems, first_sems, block_sems, chips_sems, wide_sems, pair_sems, valid_sems,
+    local_sems, first_sems, cross_sems, block_sems, chips_sems, wide_sems, pair_sems, valid_sems,
     core_sems, plane_sems, turn_sems, half_sems, part_sems, share_sems, out_sems,
 ):
     n3, n2, n1, n0, parts, seeds_axis, width, classes = sizes
@@ -198,12 +198,23 @@
         for copy in copies:
             copy.wait_recv()
 
+    def drain(count):
+        for _ in range(count):
+            moves.pop(0).wait_send()
+
     flip = 1 - 2 * z // parts
+    chip_order = [i + (1 - lax.rem(chip, 2)) * (chips - 2 * i) for i in range(1, chips)]
     distances = [0] + [i + flip * (parts - 2 * i) for i in range(1, parts)]
+
+    def half(c):
+        return pl.ds(pl.multiple_of(c * LANES, LANES), LANES)
+
+    def units_of(d):
+        return pl.ds(pl.multiple_of(lax.rem(z - d + parts, parts) * unit, unit), unit)
 
     def send_chips(d):
         block = stack_all.at[core, d, chip]
-        return [send(block, block, chips_sems, (d, k), place(2 * k, 0)) for k in range(1, chips)]
+        return [send(block, block, chips_sems, (d, k), place(2 * k, 0)) for k in chip_order]
 
     def send_plane_wide(d):
         block = stack_all.at[core, d, chip]
@@ -217,7 +228,6 @@
         send(stack_all.at[core, 0, chip], stack_all.at[core, d, chip], block_sems, (d,), place(0, d))
         for d in distances[1:]
     ]
-    chips_moves = [send_chips(0)]
     for copy in started[1:4]:
         copy.wait()
     row, col = iota((2 * width, hid), 0), iota((2 * width, hid), 1)
@@ -229,9 +239,11 @@
     first_all[own_units, :] = shard.astype(bf16)
     valid_all[s] = jnp.broadcast_to(valid_own[...].astype(f32), valid_all.shape[1:])
 
+    own_half = first_all.at[own_units, half(core)]
     first_moves = [
-        send(first_all.at[own_units], first_all.at[own_units], first_sems, (d,), place(0, d)) for d in reversed(distances[1:])
+        send(own_half, own_half, first_sems, (d,), place(0, d)) for d in reversed(distances[1:])
     ][::-1]
+    chips_moves = [send_chips(0)]
     valid_moves = [
         send(valid_all.at[s], valid_all.at[s], valid_sems, (k,), place(k, 0)) for k in range(1, seeds_axis)
     ]
@@ -284,7 +296,7 @@
             joined_one[0:width, lanes] = own_rows[:, lanes]
 
     def layer_one(i):
-        units = pl.ds(pl.multiple_of(lax.rem(z - distances[i] + parts, parts) * unit, unit), unit)
+        units = units_of(distances[i])
 
         def tile_units(tile, tiles):
             lanes = pl.ds(pl.multiple_of(tile * LANES, LANES), LANES * tiles)
@@ -312,14 +324,19 @@
     layer_one(0)
     for d, copy in zip(distances[1:], block_moves):
         arrive([copy])
-        chips_moves.append((send_plane_wide if copy is block_moves[-1] else send_chips)(d))
+        chips_moves.append(send_chips(d))
     pair_moves = []
     arrive(chips_moves[0])
     pair_moves.append(send_pair(distances[0]))
+    cross_moves = []
+    for d, copy in zip(distances[1:], first_moves):
+        arrive([copy])
+        got = first_all.at[units_of(d), half(core)]
+        cross_moves.append(send(got, got, cross_sems, (d,), (sibling, z)))
     for i in range(1, parts):
-        arrive(first_moves[i - 1 : i])
+        arrive(cross_moves[i - 1 : i])
         layer_one(i)
-    for i in range(1, parts - 1):
+    for i in range(1, parts):
         arrive(chips_moves[i])
         pair_moves.append(send_pair(distances[i]))
     squares = jnp.sum(square_rows[0:parts, :], axis=0, keepdims=True)
@@ -357,7 +374,7 @@
                     low_stack[l, :, c, h, :, lanes] = value.astype(bf16).reshape(chips, short, LANES)
         return low_stack[l].reshape(2 * hid, hid)
 
-    arrive(pair_moves + chips_moves[-1])
+    arrive(pair_moves)
     weight_two = gathered(0)
     preact = dot_tn(weight_two, joined_two[...])
     output, active_two, slope_two, scale_two = activate(preact)
@@ -391,7 +408,7 @@
         plane_send[l] = (core_send[l, core].astype(f32) + core_recv[l].astype(f32)).astype(bf16)
         return [
             send(plane_send.at[l, lax.rem(chip + k, chips)], plane_recv.at[l, k], plane_sems, (l, k), place(2 * k, 0))
-            for k in range(1, chips)
+            for k in chip_order
         ]
 
     def send_turn(l):
@@ -459,12 +476,10 @@
     total += waiting()
     first_send[...] = (grad_one[...] + total).astype(bf16)
 
-    def half(c):
-        return pl.ds(pl.multiple_of(c * LANES, LANES), LANES)
-
     def part(d):
         return pl.ds(pl.multiple_of(lax.rem(z + d, parts) * unit, unit), unit)
 
+    sent = len(moves)
     half_moves = [send(first_send.at[:, half(1 - core)], half_recv, half_sems, (0,), (sibling, z))]
     for l in (1, 0):
         arrive(core_moves[l])
@@ -475,6 +490,7 @@
     part_moves = [
         send(half_send.at[part(d)], part_recv.at[d], part_sems, (d,), place(0, d)) for d in distances[1:]
     ]
+    drain(sent)
     arrive(plane_moves[1])
     turn_moves[1] = send_turn(1)
     arrive(part_moves)
@@ -559,6 +575,7 @@
             dma((17,)),
             dma((2, parts)),
             dma((2, parts)),
+            dma((2, parts)),
             dma((2, parts, chips)),
             dma((2, seeds_axis)),
             dma((2, parts)),

time: 30.6 us -> 30.6 us (level)
  no operation moved by 1% of the time
where the time goes in v8:
time: 30.6 us; the launch traced here: 30.4 us
  Pallas kernels  29.7 us (97%)
  between operations  0.65 us (2%)
    pallas_call x1, Pallas kernels, step(): pl.pallas_call(functools.partial(step_kernel, sizes), out_shape=(shape((c...  27.7 us
    pallas_call x1, Pallas kernels, update(): pl.pallas_call(functools.partial(update_kernel, width, classes), out_shap...  2.05 us

profile of v8, /device:TPU:0, one launch (start us, length us, event | category | flops | bytes accessed | tf_op | source)
XLA Modules:
  0.0 30.4 jit_solution(13967267722625047823)
XLA Ops:
  0.6 27.7 %shard_map.230 = (bf16[4,64,256]{2,1,0:T(8,128)(2,1)}, bf16[2,4,32,128]{3,2,1,0:T(8,128)(2,1)}, f32[8,128]{1,0:T(8,128)}) custom-call(bf16[100,32768]{1,0:T(8,128)(2,1)} %bitcast.20, s32[10,8192]{1,0:T(8,128)} %bitcast.21, s32[10,1024]{1,0:T(8,128)} %bitcast.26, s32[25,128]{1,0:T(8,128)} %bitcast.31, s32[1,128]{1,0:T(1,128)} %bitcast.32, s32[1,128]{1,0:T(1,128)} %bitcast.33, ...), custom_call_target="tpu_custom_call" | custom-call | tf_op jit(solution)/shard_map/pallas_call | solution.py:531
  28.3 2.0 %shard_map.231 = (f32[1,1]{1,0:T(1,128)}, f32[1,1]{1,0:T(1,128)}, f32[64,200]{1,0:T(8,128)}, f32[64,200]{1,0:T(8,128)}, f32[64,200]{1,0:T(8,128)}, /*index=5*/f3...) custom-call(bf16[4,64,256]{2,1,0:T(8,128)(2,1)} %get-tuple-element.2, ...), custom_call_target="tpu_custom_call" | custom-call | tf_op jit(solution)/shard_map/pallas_call | solution.py:646
